TPU v7x, 32 devices: a whole 2x2x4 slice. The times are simulated.
32 devices in a mesh: design: 2 (over y), gx: 4 (over x, core), gy: 4 (over z).
Axes of the slice: x: 2, y: 2, z: 4, core: 2. Of those that a mesh axis runs over, the one named last changes fastest.
Arguments:
- adj_e: float32 [6, 2, 512, 1024], P('design', None, 'gx', 'gy'), parts along dimension 0, may hold values from -6 to 6
- adj_h: float32 [6, 2, 512, 1024], P('design', None, 'gx', 'gy'), parts along dimension 0, may hold values from -6 to 6
- fwd_e: float32 [4, 3, 2, 512, 1024], P('design', None, None, 'gx', 'gy'), parts along dimension 0, may hold values from -6 to 6
- labels: int32 [1024, 1024], P(('design', 'gx'), 'gy'), parts along dimension 0, may hold values from 0 to 7
- eps_table: float32 [8], replicated, may hold values from 1 to 12
- density: float32 [1024, 1024], P(('design', 'gx'), 'gy'), parts along dimension 0, may hold values from 0 to 3
Outputs:
- elec_out: float32 [6, 2, 512, 1024], P('design', None, 'gx', 'gy'), parts along dimension 0
- magn_out: float32 [6, 2, 512, 1024], P('design', None, 'gx', 'gy'), parts along dimension 0
- design_grad: float32 [1024, 1024], P(('design', 'gx'), 'gy'), parts along dimension 0
There are 2 independent parts, one for each index of `design`. A program takes and returns all parts, laid end to end along the dimension named above; an argument that names none is the same for every part. Nothing has to cross between parts.
All inputs are finite; a program needn't handle non-finite values.
Results may differ from a plain program's by a relative error of at most 0.0001.
Values sent between devices are 32-bit elements; how exact they have to be, the bound alone decides.
No kernel may reach another device: no remote copies, remote signals or barrier semaphores. Data moves between devices by JAX's collectives and lax.ppermute only.
A program may use at most 64 MiB of HBM per device.

v0:
```python
import jax
import jax.numpy as jnp
from jax import lax
from jax.sharding import PartitionSpec as P

STEPS = 2
NMAT = 8
FILT = 16


courant = 0.5
spread_ratio = 0.6


def from_behind(value, axis, steps):
    count = lax.axis_size(axis)
    pairs = [(source, (source + steps) % count) for source in range(count)]
    return lax.ppermute(value, axis, pairs)


def with_halo(x, sides, width):
    for axis, dim in sides:
        size, length = (lax.axis_size(axis), x.shape[dim])
        up = [(i, (i + 1) % size) for i in range(size)]
        down = [(j, i) for i, j in up]
        last = lax.slice_in_dim(x, length - width, length, axis=dim)
        leading = lax.slice_in_dim(x, 0, width, axis=dim)
        before = lax.ppermute(last, axis, up)
        after = lax.ppermute(leading, axis, down)
        x = jnp.concatenate([before, x, after], axis=dim)
    return x


def band_values(shifted, radius):
    offsets = jnp.arange(-radius, radius + 1).astype(jnp.float32)
    spread = spread_ratio * radius
    raw_taps = jnp.exp(-offsets * offsets / (2.0 * spread * spread))
    scale = jnp.sqrt(jnp.sum(raw_taps * raw_taps))
    inside = (shifted >= 0) & (shifted <= 2 * radius)
    distance = (shifted - radius).astype(jnp.float32)
    values = jnp.exp(-distance * distance / (2.0 * spread * spread)) / scale
    return jnp.where(inside, values, jnp.float32(0.0))


def row_band_matrix(count, radius):
    shifted = jnp.arange(count + 2 * radius)[None, :] - jnp.arange(count)[:, None]
    return band_values(shifted, radius)


def col_band_matrix(count, radius):
    shifted = jnp.arange(count + 2 * radius)[:, None] - jnp.arange(count)[None, :]
    return band_values(shifted, radius)


def depth_low(field):
    depth = lax.broadcasted_iota(jnp.int32, field.shape, 0)
    return jnp.where(depth == 0, jnp.float32(0.0), jnp.roll(field, 1, axis=0))


def depth_high(field):
    depth = lax.broadcasted_iota(jnp.int32, field.shape, 0)
    return jnp.where(depth == field.shape[0] - 1, jnp.float32(0.0), jnp.roll(field, -1, axis=0))


def join_low(plane, field, axis):
    place = lax.broadcasted_iota(jnp.int32, field.shape, axis)
    return jnp.where(place == 0, jnp.expand_dims(plane, axis), jnp.roll(field, 1, axis=axis))


def join_high(field, plane, axis):
    place = lax.broadcasted_iota(jnp.int32, field.shape, axis)
    last = field.shape[axis] - 1
    return jnp.where(place == last, jnp.expand_dims(plane, axis), jnp.roll(field, -1, axis=axis))


def electric_update(electric, magnetic, ratio):
    plane_x = from_behind(jnp.stack([magnetic[1][:, -1, :], magnetic[2][:, -1, :]]), "gx", 1)
    plane_y = from_behind(jnp.stack([magnetic[0][:, :, -1], magnetic[2][:, :, -1]]), "gy", 1)
    second_xlow = join_low(plane_x[0], magnetic[1], 1)
    third_xlow = join_low(plane_x[1], magnetic[2], 1)
    first_ylow = join_low(plane_y[0], magnetic[0], 2)
    third_ylow = join_low(plane_y[1], magnetic[2], 2)
    rotor = [
        magnetic[2] - third_ylow - (magnetic[1] - depth_low(magnetic[1])),
        magnetic[0] - depth_low(magnetic[0]) - (magnetic[2] - third_xlow),
        magnetic[1] - second_xlow - (magnetic[0] - first_ylow),
    ]
    return [electric[component] - ratio[None] * rotor[component] for component in range(3)]


def magnetic_update(electric, magnetic):
    plane_x = from_behind(jnp.stack([electric[1][:, 0, :], electric[2][:, 0, :]]), "gx", -1)
    plane_y = from_behind(jnp.stack([electric[0][:, :, 0], electric[2][:, :, 0]]), "gy", -1)
    second_xhigh = join_high(electric[1], plane_x[0], 1)
    third_xhigh = join_high(electric[2], plane_x[1], 1)
    first_yhigh = join_high(electric[0], plane_y[0], 2)
    third_yhigh = join_high(electric[2], plane_y[1], 2)
    rotor = [
        third_yhigh - electric[2] - (depth_high(electric[1]) - electric[1]),
        depth_high(electric[0]) - electric[0] - (third_xhigh - electric[2]),
        second_xhigh - electric[1] - (first_yhigh - electric[0]),
    ]
    return [magnetic[component] + courant * rotor[component] for component in range(3)]


def body(adj_e, adj_h, fwd_e, labels, eps_table, density):
    choose = labels[None, :, :] == jnp.arange(NMAT, dtype=jnp.int32)[:, None, None]
    permittivity = (
        jnp.sum(jnp.where(choose, eps_table[:, None, None], jnp.float32(0.0)), axis=0) + density
    )
    ratio = courant / permittivity
    electric = [adj_e[0], adj_e[1], adj_e[2]]
    magnetic = [adj_h[0], adj_h[1], adj_h[2]]
    gradient = jnp.zeros(labels.shape, jnp.float32)
    for instant in range(STEPS):
        electric = electric_update(electric, magnetic, ratio)
        product = (
            electric[0] * fwd_e[instant, 0]
            + electric[1] * fwd_e[instant, 1]
            + electric[2] * fwd_e[instant, 2]
        )
        gradient = gradient + jnp.sum(product, axis=0)
        magnetic = magnetic_update(electric, magnetic)
    rows_count = gradient.shape[0]
    cols_count = gradient.shape[1]
    row_band = row_band_matrix(rows_count, FILT)
    col_band = col_band_matrix(cols_count, FILT)
    highest = lax.Precision.HIGHEST
    padded = with_halo(gradient, (("gx", 0), ("gy", 1)), FILT)
    along_rows = jnp.dot(row_band, padded, precision=highest, preferred_element_type=jnp.float32)
    filtered = jnp.dot(along_rows, col_band, precision=highest, preferred_element_type=jnp.float32)
    return (jnp.stack(electric), jnp.stack(magnetic), filtered)


def solution(mesh):
    return jax.shard_map(
        body,
        mesh=mesh,
        in_specs=(
            P("design", None, "gx", "gy"),
            P("design", None, "gx", "gy"),
            P("design", None, None, "gx", "gy"),
            P(("design", "gx"), "gy"),
            P(),
            P(("design", "gx"), "gy"),
        ),
        out_specs=(
            P("design", None, "gx", "gy"),
            P("design", None, "gx", "gy"),
            P(("design", "gx"), "gy"),
        ),
        check_vma=False,
    )
```

profile of v0, /device:TPU:0, one launch (start us, length us, event | category | flops | bytes accessed | tf_op | source)
XLA Modules:
  0.0 71.7 jit_solution(11476894158138143163)
XLA Ops:
  0.6 1.2 %slice_bitcast_fusion.6 = (f32[2,128,256]{2,1,0:T(8,128)S(1)}, f32[2,128,256]{2,1,0:T(8,128)S(1)}, f32[2,128,256]{2,1,0:T(8,128)S(1)}) fusion(f32[3,2,128,256]{3,2,1,0:T(8,128)} %param.7), kind=kLoop, calls=%fused_computation.189 | loop fusion | bytes 1572864 | tf_op jit(solution)/shard_map/squeeze | solution.py:113
  3.5 0.8 %slice_bitcast_fusion.65 = (f32[1,2,128,1]{3,2,1,0:T(8,128)}, f32[2,128]{1,0:T(2,128)S(1)}, f32[2,128,1]{2,1,0:T(8,128)}) fusion(f32[2,128,256]{2,1,0:T(8,128)S(1)} %get-tuple-element.56), kind=kLoop, calls=%fused_computation.319 | loop fusion | bytes 4096 | tf_op jit(solution)/shard_map/jit(_roll_static)/concatenate | solution.py:67
  4.3 0.8 %slice_bitcast_fusion.66 = (f32[1,2,128,1]{3,2,1,0:T(8,128)}, f32[2,128]{1,0:T(2,128)S(1)}, f32[2,128,1]{2,1,0:T(8,128)S(1)}) fusion(f32[2,128,256]{2,1,0:T(8,128)S(1)} %get-tuple-element.58), kind=kLoop, calls=%fused_computation.321 | loop fusion | bytes 4096 | tf_op jit(solution)/shard_map/jit(_roll_static)/concatenate | solution.py:67
  5.7 2.6 %collective-permute-start = (f32[2,2,128]{2,1,0:T(2,128)}, f32[2,2,128]{2,1,0:T(2,128)}, u32[]{:S(2)}, u32[]{:S(2)}) collective-permute-start(f32[2,2,128]{2,1,0:T(2,128)} %pad_maximum_fusion.9), channel_id=1, source_target_pairs={{0,1},{1,2},{2,3},{3,0},{4,5},{5,6},{6,7},{7,4},{8,9},{9,10},{10,1... | collective-permute-start | bytes 6152 | tf_op jit(solution)/shard_map/ppermute | solution.py:18
  9.9 0.7 %slice_bitcast_fusion.62 = (f32[1,2,127,256]{3,2,1,0:T(8,128)}, f32[2,127,256]{2,1,0:T(8,128)S(1)}) fusion(f32[2,128,256]{2,1,0:T(8,128)S(1)} %get-tuple-element.57), kind=kLoop, calls=%fused_computation.316 | loop fusion | bytes 780288 | tf_op jit(solution)/shard_map/jit(_roll_static)/concatenate | solution.py:67
  10.7 0.7 %slice_bitcast_fusion.61 = (f32[1,2,128,255]{3,2,1,0:T(8,128)}, f32[2,128,255]{2,1,0:T(8,128)S(1)}) fusion(f32[2,128,256]{2,1,0:T(8,128)S(1)} %get-tuple-element.58), kind=kLoop, calls=%fused_computation.315 | loop fusion | bytes 783360 | tf_op jit(solution)/shard_map/jit(_roll_static)/concatenate | solution.py:67
  12.2 0.9 %fusion.182 = (f32[1,1,128,256]{3,2,1,0:T(8,128)}, f32[1,128,256]{2,1,0:T(8,128)S(1)}, f32[1,128,256]{2,1,0:T(8,128)}, f32[1,128,256]{2,1,0:T(8,128)S(1)}, f32[1...) fusion(f32[3,2,128,256]{3,2,1,0:T(8,128)S(1)} %copy-done), kind=kLoop, calls=%fused_computation.323 | loop fusion | bytes 1572864 | tf_op jit(solution)/shard_map/jit(_roll_static)/slice | solution.py:57
  15.9 1.1 %fusion.48 = f32[2,128,256]{2,1,0:T(8,128)S(1)} fusion(f32[2,128,255]{2,1,0:T(8,128)S(1)} %get-tuple-element.82, f32[2,128,1]{2,1,0:T(8,128)S(1)} %copy-done.15, f32[1,128,256]{2,1,0:T(8,128)} %get-tuple-element.50, f32[1,128,256]{2,1,0:T(8,128)S(1)} %get-tuple-element.49, f32[3,2,128,256]{3,2,1,0:T(8,128)S(1)} %copy-done.1, ...), kind=kLoop, calls=%fused_computation.65 | loop fusion | flops 589824 | bytes 1705218 | tf_op jit(solution)/shard_map/sub | solution.py:88
  21.4 2.1 %collective-permute-start.3 = (f32[2,2,128]{2,1,0:T(2,128)S(1)}, f32[2,2,128]{2,1,0:T(2,128)S(1)}, u32[]{:S(2)}, u32[]{:S(2)}) collective-permute-start(f32[2,2,128]{2,1,0:T(2,128)S(1)} %pad_maximum_fusion.10), channel_id=1, source_target_pairs={{0,3},{1,0},{2,1},{3,2},{4,7},{5,4},{6,5},{7,6},{8,11},{9,8},{10,9... | collective-permute-start | bytes 6152 | tf_op jit(solution)/shard_map/ppermute | solution.py:18
  23.5 1.5 %collective-permute-start.2 = (f32[2,2,256]{2,1,0:T(2,128)S(1)}, f32[2,2,256]{2,1,0:T(2,128)S(1)}, u32[]{:S(2)}, u32[]{:S(2)}) collective-permute-start(f32[2,2,256]{2,1,0:T(2,128)S(1)} %pad_maximum_fusion.6), channel_id=1, source_target_pairs={{0,12},{4,0},{8,4},{12,8},{1,13},{5,1},{9,5},{13,9},{2,14},{6,2},{... | collective-permute-start | bytes 12296 | tf_op jit(solution)/shard_map/ppermute | solution.py:18
  27.1 0.8 %slice_bitcast_fusion.40 = (f32[1,1,128,256]{3,2,1,0:T(8,128)}, f32[1,1,128,256]{3,2,1,0:T(8,128)}, f32[1,128,256]{2,1,0:T(8,128)S(1)}, f32[1,128,256]{2,1,0:T(8,128)S(1)}) fusion(f32[2,128,256]{2,1,0:T(8,128)S(1)} %get-tuple-element.46), kind=kLoop, calls=%fused_computation.290 | loop fusion | bytes 786432 | tf_op jit(solution)/shard_map/jit(_roll_static)/concatenate | solution.py:57
  27.9 0.8 %slice_bitcast_fusion.55 = (f32[1,2,128,1]{3,2,1,0:T(8,128)}, f32[2,128]{1,0:T(2,128)S(1)}, f32[2,128,1]{2,1,0:T(8,128)S(1)}) fusion(f32[2,128,256]{2,1,0:T(8,128)S(1)} %get-tuple-element.47), kind=kLoop, calls=%fused_computation.306 | loop fusion | bytes 4096 | tf_op jit(solution)/shard_map/jit(_roll_static)/concatenate | solution.py:67
  31.7 0.8 %slice_bitcast_fusion.54 = (f32[1,2,128,1]{3,2,1,0:T(8,128)}, f32[2,128]{1,0:T(2,128)S(1)}, f32[2,128,1]{2,1,0:T(8,128)S(1)}) fusion(f32[2,128,256]{2,1,0:T(8,128)S(1)} %fusion.59), kind=kLoop, calls=%fused_computation.304 | loop fusion | bytes 4096 | tf_op jit(solution)/shard_map/jit(_roll_static)/concatenate | solution.py:67
  33.9 1.1 %collective-permute-start.4 = (f32[2,2,128]{2,1,0:T(2,128)S(1)}, f32[2,2,128]{2,1,0:T(2,128)S(1)}, u32[]{:S(2)}, u32[]{:S(2)}) collective-permute-start(f32[2,2,128]{2,1,0:T(2,128)S(1)} %pad_maximum_fusion.11), channel_id=1, source_target_pairs={{0,1},{1,2},{2,3},{3,0},{4,5},{5,6},{6,7},{7,4},{8,9},{9,10},{10,1... | collective-permute-start | bytes 6152 | tf_op jit(solution)/shard_map/ppermute | solution.py:18
  35.6 3.8 %collective-permute-done.4 = f32[2,2,128]{2,1,0:T(2,128)S(1)} collective-permute-done((f32[2,2,128]{2,1,0:T(2,128)S(1)}, f32[2,2,128]{2,1,0:T(2,128)S(1)}, u32[]{:S(2)}, u32[]{:S(2)}) %collective-permute-start.4) | collective-permute-done | bytes 2080 | tf_op jit(solution)/shard_map/ppermute | solution.py:18
  39.4 1.3 %fusion.127 = (f32[128,256]{1,0:T(8,128)}, f32[128,256]{1,0:T(8,128)}, f32[2,128,256]{2,1,0:T(8,128)S(1)}, f32[2,128,256]{2,1,0:T(8,128)S(1)}, f32[2,128,256]{2,1,0:T(8,128)S(1)}) fusion(f32[2,3,2,128,256]{4,3,2,1,0:T(8,128)S(1)} %copy-done.2, f32[2,128,256]{2,1,0:T(8,128)S(1)} %fusion.34, f32[2,128,256]{2,1,0:T(8,128)S(1)} %fusion.29, ...), kind=kLoop, calls=%fused_computation.177 | loop fusion | flops 2490368 | bytes 5904770 | tf_op jit(solution)/shard_map/reduce_sum | solution.py:122
  41.3 1.2 %slice_reduce_fusion = (f32[2,128]{1,0:T(2,128)}, f32[1,2,128,1]{3,2,1,0:T(8,128)}) fusion(f32[2,128,256]{2,1,0:T(8,128)S(1)} %get-tuple-element.32), kind=kLoop, calls=%fused_computation.213 | loop fusion | bytes 3072 | tf_op jit(solution)/shard_map/slice | solution.py:93
  42.5 1.2 %slice_bitcast_fusion.12 = (f32[1,2,128,1]{3,2,1,0:T(8,128)}, f32[2,128]{1,0:T(2,128)}) fusion(f32[2,128,256]{2,1,0:T(8,128)S(1)} %get-tuple-element.33), kind=kLoop, calls=%fused_computation.214 | loop fusion | bytes 3072 | tf_op jit(solution)/shard_map/jit(_roll_static)/concatenate | solution.py:73
  43.8 0.9 %slice_bitcast_fusion = f32[1,2,128,255]{3,2,1,0:T(8,128)} fusion(f32[2,128,256]{2,1,0:T(8,128)S(1)} %get-tuple-element.33), kind=kLoop, calls=%fused_computation.24 | loop fusion | bytes 522240 | tf_op jit(solution)/shard_map/jit(_roll_static)/concatenate | solution.py:73
  48.1 0.8 %slice_bitcast_fusion.3 = f32[1,2,128,255]{3,2,1,0:T(8,128)} fusion(f32[2,128,256]{2,1,0:T(8,128)S(1)} %get-tuple-element.32), kind=kLoop, calls=%fused_computation.27 | loop fusion | bytes 522240 | tf_op jit(solution)/shard_map/jit(_roll_static)/concatenate | solution.py:73
  49.0 1.7 %copy.1107 = f32[128,256]{0,1:T(8,128)} copy(f32[128,256]{1,0:T(8,128)} %get-tuple-element.30) | data formatting | bytes 262144
  53.1 1.7 %copy.1106 = f32[128,256]{0,1:T(8,128)} copy(f32[128,256]{1,0:T(8,128)} %get-tuple-element.31) | data formatting | bytes 262144
  55.5 1.0 %collective-permute-start.6 = (f32[2,2,128]{2,1,0:T(2,128)S(1)}, f32[2,2,128]{2,1,0:T(2,128)S(1)}, u32[]{:S(2)}, u32[]{:S(2)}) collective-permute-start(f32[2,2,128]{2,1,0:T(2,128)S(1)} %pad_maximum_fusion.12), channel_id=1, source_target_pairs={{0,3},{1,0},{2,1},{3,2},{4,7},{5,4},{6,5},{7,6},{8,11},{9,8},{10,9... | collective-permute-start | bytes 6152 | tf_op jit(solution)/shard_map/ppermute | solution.py:18
  56.5 1.0 %add.81 = f32[128,256]{0,1:T(8,128)S(1)} add(f32[128,256]{0,1:T(8,128)} %copy.1106, f32[128,256]{0,1:T(8,128)} %copy.1107) | non-fusion elementwise | flops 32768 | bytes 393216 | tf_op jit(solution)/shard_map/add | solution.py:122
  57.8 1.5 %collective-permute-start.9 = (f32[16,256]{0,1:T(8,128)S(1)}, f32[16,256]{0,1:T(8,128)S(1)}, u32[]{:S(2)}, u32[]{:S(2)}) collective-permute-start(f32[16,256]{0,1:T(8,128)S(1)} %get-tuple-element.144), channel_id=1, source_target_pairs={{4,0},{8,4},{12,8},{0,12},{5,1},{9,5},{13,9},{1,13},{6,2},{10,6},{... | collective-permute-start | bytes 49160 | tf_op jit(solution)/shard_map/ppermute | solution.py:29
  59.5 2.6 %fusion.109 = (f32[1,2,128,256]{3,2,1,0:T(8,128)S(1)}, f32[1,2,128,256]{3,2,1,0:T(8,128)S(1)}, f32[1,2,128,256]{3,2,1,0:T(8,128)S(1)}, f32[1,2,128,256]{3,2,1,0:...) fusion(f32[1,2,128,256]{3,2,1,0:T(8,128)S(1)} %get-tuple-element.43, ...), kind=kLoop, calls=%fused_computation.151 | loop fusion | flops 3538944 | bytes 6435588 | tf_op jit(solution)/shard_map/add | solution.py:103
  63.5 0.9 %pad_maximum_fusion = f32[3,2,128,256]{3,2,1,0:T(8,128)} fusion(f32[1,2,128,256]{3,2,1,0:T(8,128)S(1)} %get-tuple-element.38, f32[1,2,128,256]{3,2,1,0:T(8,128)S(1)} %get-tuple-element.36, f32[1,2,128,256]{3,2,1,0:T(8,128)S(1)} %get-tuple-element.42), kind=kLoop, calls=%fused_computation.2 | loop fusion | flops 393216 | bytes 1572864 | tf_op jit(solution)/shard_map/stack | solution.py:132
  64.5 1.1 %collective-permute-start.10 = (f32[160,16]{0,1:T(8,128)S(1)}, f32[160,16]{0,1:T(8,128)S(1)}, u32[]{:S(2)}, u32[]{:S(2)}) collective-permute-start(f32[160,16]{0,1:T(8,128)S(1)} %get-tuple-element.59), channel_id=1, source_target_pairs={{0,1},{1,2},{2,3},{3,0},{4,5},{5,6},{6,7},{7,4},{8,9},{9,10},{10,1... | collective-permute-start | bytes 30728 | tf_op jit(solution)/shard_map/ppermute | solution.py:28
  65.6 2.8 %collective-permute-start.11 = (f32[160,16]{0,1:T(8,128)S(1)}, f32[160,16]{0,1:T(8,128)S(1)}, u32[]{:S(2)}, u32[]{:S(2)}) collective-permute-start(f32[160,16]{0,1:T(8,128)S(1)} %get-tuple-element.60), channel_id=1, source_target_pairs={{1,0},{2,1},{3,2},{0,3},{5,4},{6,5},{7,6},{4,7},{9,8},{10,9},{11,1... | collective-permute-start | bytes 30728 | tf_op jit(solution)/shard_map/ppermute | solution.py:29
  68.4 0.9 %pad_maximum_fusion.1 = f32[3,2,128,256]{3,2,1,0:T(8,128)} fusion(f32[1,2,128,256]{3,2,1,0:T(8,128)S(1)} %fusion.124, f32[1,2,128,256]{3,2,1,0:T(8,128)S(1)} %get-tuple-element.41, f32[1,2,128,256]{3,2,1,0:T(8,128)S(1)} %get-tuple-element.35), kind=kLoop, calls=%fused_computation.3 | loop fusion | flops 393216 | bytes 1572864 | tf_op jit(solution)/shard_map/stack | solution.py:132
  69.3 0.8 %collective-permute-done.10 = f32[160,16]{0,1:T(8,128)S(1)} collective-permute-done((f32[160,16]{0,1:T(8,128)S(1)}, f32[160,16]{0,1:T(8,128)S(1)}, u32[]{:S(2)}, u32[]{:S(2)}) %collective-permute-start.10) | collective-permute-done | bytes 10272 | tf_op jit(solution)/shard_map/ppermute | solution.py:28
  70.6 1.2 %fusion.16 = f32[128,256]{1,0:T(8,128)} fusion(f32[128,288]{0,1:T(8,128)S(1)} %fusion.4, f32[]{:T(128)S(6)} %sqrt.4), kind=kOutput, calls=%fused_computation.22 | convolution fusion | flops 114057216 | bytes 278532 | tf_op jit(solution)/shard_map/dot_general | solution.py:131
  (167 shorter events, 27.6 us)
Async XLA Ops:
  3.0 15.6 %collective-permute-start.1 = (f32[2,2,256]{2,1,0:T(2,128)}, f32[2,2,256]{2,1,0:T(2,128)}, u32[]{:S(2)}, u32[]{:S(2)}) collective-permute-start(f32[2,2,256]{2,1,0:T(2,128)} %pad_maximum_fusion.5), channel_id=1, source_target_pairs={{0,4},{4,8},{8,12},{12,0},{1,5},{5,9},{9,13},{13,1},{2,6},{6,10},{... | collective-permute-start | bytes 12296 | tf_op jit(solution)/shard_map/ppermute | solution.py:18
  5.7 9.6 %collective-permute-start = (f32[2,2,128]{2,1,0:T(2,128)}, f32[2,2,128]{2,1,0:T(2,128)}, u32[]{:S(2)}, u32[]{:S(2)}) collective-permute-start(f32[2,2,128]{2,1,0:T(2,128)} %pad_maximum_fusion.9), channel_id=1, source_target_pairs={{0,1},{1,2},{2,3},{3,0},{4,5},{5,6},{6,7},{7,4},{8,9},{9,10},{10,1... | collective-permute-start | bytes 6152 | tf_op jit(solution)/shard_map/ppermute | solution.py:18
  12.2 3.8 %copy-start.1 = (f32[3,2,128,256]{3,2,1,0:T(8,128)S(1)}, f32[3,2,128,256]{3,2,1,0:T(8,128)}, u32[]{:S(2)}) copy-start(f32[3,2,128,256]{3,2,1,0:T(8,128)} %param.6) | copy-start | bytes 2359300
  12.2 3.7 %copy-start.15 = (f32[2,128,1]{2,1,0:T(8,128)S(1)}, f32[2,128,1]{2,1,0:T(8,128)}, u32[]{:S(2)}) copy-start(f32[2,128,1]{2,1,0:T(8,128)} %get-tuple-element.80) | copy-start | bytes 3076
  20.4 4.6 %copy-start.4 = (f32[1,2,127,256]{3,2,1,0:T(8,128)S(1)}, f32[1,2,127,256]{3,2,1,0:T(8,128)}, u32[]{:S(2)}) copy-start(f32[1,2,127,256]{3,2,1,0:T(8,128)} %get-tuple-element.132) | copy-start | bytes 780292
  20.4 4.6 %copy-start.5 = (f32[1,2,128,255]{3,2,1,0:T(8,128)S(1)}, f32[1,2,128,255]{3,2,1,0:T(8,128)}, u32[]{:S(2)}) copy-start(f32[1,2,128,255]{3,2,1,0:T(8,128)} %get-tuple-element.137) | copy-start | bytes 783364
  20.4 4.6 %copy-start.6 = (f32[1,2,127,256]{3,2,1,0:T(8,128)S(1)}, f32[1,2,127,256]{3,2,1,0:T(8,128)}, u32[]{:S(2)}) copy-start(f32[1,2,127,256]{3,2,1,0:T(8,128)} %get-tuple-element.141) | copy-start | bytes 780292
  20.4 4.6 %copy-start.11 = (f32[1,2,128,1]{3,2,1,0:T(8,128)S(1)}, f32[1,2,128,1]{3,2,1,0:T(8,128)}, u32[]{:S(2)}) copy-start(f32[1,2,128,1]{3,2,1,0:T(8,128)} %get-tuple-element.134) | copy-start | bytes 3076
  20.4 4.6 %copy-start.12 = (f32[1,1,128,256]{3,2,1,0:T(8,128)S(1)}, f32[1,1,128,256]{3,2,1,0:T(8,128)}, u32[]{:S(2)}) copy-start(f32[1,1,128,256]{3,2,1,0:T(8,128)} %get-tuple-element.54) | copy-start | bytes 393220
  20.4 4.6 %copy-start.13 = (f32[1,1,128,256]{3,2,1,0:T(8,128)S(1)}, f32[1,1,128,256]{3,2,1,0:T(8,128)}, u32[]{:S(2)}) copy-start(f32[1,1,128,256]{3,2,1,0:T(8,128)} %get-tuple-element.55) | copy-start | bytes 393220
  20.4 4.6 %copy-start.28 = (pred[256]{0:T(512)(128)(4,1)S(1)}, pred[256]{0:T(512)(128)(4,1)}, u32[]{:S(2)}) copy-start(pred[256]{0:T(512)(128)(4,1)} %iota_compare_fusion.1) | copy-start | bytes 772
  20.5 4.6 %copy-start.35 = (f32[1,2,1,256]{3,2,1,0:T(1,128)S(1)}, f32[1,2,1,256]{3,2,1,0:T(1,128)}, u32[]{:S(2)}) copy-start(f32[1,2,1,256]{3,2,1,0:T(1,128)} %get-tuple-element.139) | copy-start | bytes 6148
  20.5 4.6 %copy-start.36 = (f32[1,2,1,256]{3,2,1,0:T(1,128)S(1)}, f32[1,2,1,256]{3,2,1,0:T(1,128)}, u32[]{:S(2)}) copy-start(f32[1,2,1,256]{3,2,1,0:T(1,128)} %get-tuple-element.162) | copy-start | bytes 6148
  20.5 4.6 %copy-start.39 = (pred[2]{0:T(512)(128)(4,1)S(1)}, pred[2]{0:T(512)(128)(4,1)}, u32[]{:S(2)}) copy-start(pred[2]{0:T(512)(128)(4,1)} %iota_compare_fusion.3) | copy-start | bytes 10
  21.4 3.6 %collective-permute-start.3 = (f32[2,2,128]{2,1,0:T(2,128)S(1)}, f32[2,2,128]{2,1,0:T(2,128)S(1)}, u32[]{:S(2)}, u32[]{:S(2)}) collective-permute-start(f32[2,2,128]{2,1,0:T(2,128)S(1)} %pad_maximum_fusion.10), channel_id=1, source_target_pairs={{0,3},{1,0},{2,1},{3,2},{4,7},{5,4},{6,5},{7,6},{8,11},{9,8},{10,9... | collective-permute-start | bytes 6152 | tf_op jit(solution)/shard_map/ppermute | solution.py:18
  23.5 2.8 %collective-permute-start.2 = (f32[2,2,256]{2,1,0:T(2,128)S(1)}, f32[2,2,256]{2,1,0:T(2,128)S(1)}, u32[]{:S(2)}, u32[]{:S(2)}) collective-permute-start(f32[2,2,256]{2,1,0:T(2,128)S(1)} %pad_maximum_fusion.6), channel_id=1, source_target_pairs={{0,12},{4,0},{8,4},{12,8},{1,13},{5,1},{9,5},{13,9},{2,14},{6,2},{... | collective-permute-start | bytes 12296 | tf_op jit(solution)/shard_map/ppermute | solution.py:18
  25.0 5.9 %copy-start.34 = (f32[2,128]{1,0:T(2,128)}, f32[2,128]{1,0:T(2,128)S(1)}, u32[]{:S(2)}) copy-start(f32[2,128]{1,0:T(2,128)S(1)} %get-tuple-element.157) | copy-start | bytes 3076
  26.3 4.6 %copy-start.23 = (f32[2,256]{1,0:T(2,128)}, f32[2,256]{1,0:T(2,128)S(1)}, u32[]{:S(2)}) copy-start(f32[2,256]{1,0:T(2,128)S(1)} %get-tuple-element.150) | copy-start | bytes 6148
  30.9 8.5 %copy-start.2 = (f32[2,3,2,128,256]{4,3,2,1,0:T(8,128)S(1)}, f32[2,3,2,128,256]{4,3,2,1,0:T(8,128)}, u32[]{:S(2)}) copy-start(f32[2,3,2,128,256]{4,3,2,1,0:T(8,128)} %param.8) | copy-start | bytes 4718596
  33.9 5.4 %collective-permute-start.4 = (f32[2,2,128]{2,1,0:T(2,128)S(1)}, f32[2,2,128]{2,1,0:T(2,128)S(1)}, u32[]{:S(2)}, u32[]{:S(2)}) collective-permute-start(f32[2,2,128]{2,1,0:T(2,128)S(1)} %pad_maximum_fusion.11), channel_id=1, source_target_pairs={{0,1},{1,2},{2,3},{3,0},{4,5},{5,6},{6,7},{7,4},{8,9},{9,10},{10,1... | collective-permute-start | bytes 6152 | tf_op jit(solution)/shard_map/ppermute | solution.py:18
  35.0 4.3 %collective-permute-start.5 = (f32[2,2,256]{2,1,0:T(2,128)S(1)}, f32[2,2,256]{2,1,0:T(2,128)S(1)}, u32[]{:S(2)}, u32[]{:S(2)}) collective-permute-start(f32[2,2,256]{2,1,0:T(2,128)S(1)} %pad_maximum_fusion.7), channel_id=1, source_target_pairs={{0,4},{4,8},{8,12},{12,0},{1,5},{5,9},{9,13},{13,1},{2,6},{6,10},{... | collective-permute-start | bytes 12296 | tf_op jit(solution)/shard_map/ppermute | solution.py:18
  52.6 9.6 %collective-permute-start.7 = (f32[2,2,256]{2,1,0:T(2,128)}, f32[2,2,256]{2,1,0:T(2,128)}, u32[]{:S(2)}, u32[]{:S(2)}) collective-permute-start(f32[2,2,256]{2,1,0:T(2,128)} %pad_maximum_fusion.8), channel_id=1, source_target_pairs={{0,12},{4,0},{8,4},{12,8},{1,13},{5,1},{9,5},{13,9},{2,14},{6,2},{... | collective-permute-start | bytes 12296 | tf_op jit(solution)/shard_map/ppermute | solution.py:18
  55.5 3.9 %collective-permute-start.6 = (f32[2,2,128]{2,1,0:T(2,128)S(1)}, f32[2,2,128]{2,1,0:T(2,128)S(1)}, u32[]{:S(2)}, u32[]{:S(2)}) collective-permute-start(f32[2,2,128]{2,1,0:T(2,128)S(1)} %pad_maximum_fusion.12), channel_id=1, source_target_pairs={{0,3},{1,0},{2,1},{3,2},{4,7},{5,4},{6,5},{7,6},{8,11},{9,8},{10,9... | collective-permute-start | bytes 6152 | tf_op jit(solution)/shard_map/ppermute | solution.py:18
  57.5 6.9 %collective-permute-start.8 = (f32[16,256]{0,1:T(8,128)S(1)}, f32[16,256]{0,1:T(8,128)S(1)}, u32[]{:S(2)}, u32[]{:S(2)}) collective-permute-start(f32[16,256]{0,1:T(8,128)S(1)} %get-tuple-element.143), channel_id=1, source_target_pairs={{0,4},{4,8},{8,12},{12,0},{1,5},{5,9},{9,13},{13,1},{2,6},{6,10},{... | collective-permute-start | bytes 49160 | tf_op jit(solution)/shard_map/ppermute | solution.py:28
  57.8 6.6 %collective-permute-start.9 = (f32[16,256]{0,1:T(8,128)S(1)}, f32[16,256]{0,1:T(8,128)S(1)}, u32[]{:S(2)}, u32[]{:S(2)}) collective-permute-start(f32[16,256]{0,1:T(8,128)S(1)} %get-tuple-element.144), channel_id=1, source_target_pairs={{4,0},{8,4},{12,8},{0,12},{5,1},{9,5},{13,9},{1,13},{6,2},{10,6},{... | collective-permute-start | bytes 49160 | tf_op jit(solution)/shard_map/ppermute | solution.py:29
  59.4 3.5 %copy-start.3 = (f32[1,2,128,255]{3,2,1,0:T(8,128)S(1)}, f32[1,2,128,255]{3,2,1,0:T(8,128)}, u32[]{:S(2)}) copy-start(f32[1,2,128,255]{3,2,1,0:T(8,128)} %get-tuple-element.68) | copy-start | bytes 783364
  59.4 3.5 %copy-start.7 = (f32[1,2,127,256]{3,2,1,0:T(8,128)S(1)}, f32[1,2,127,256]{3,2,1,0:T(8,128)}, u32[]{:S(2)}) copy-start(f32[1,2,127,256]{3,2,1,0:T(8,128)} %slice_bitcast_fusion.2) | copy-start | bytes 780292
  59.4 3.5 %copy-start.10 = (f32[1,2,128,1]{3,2,1,0:T(8,128)S(1)}, f32[1,2,128,1]{3,2,1,0:T(8,128)}, u32[]{:S(2)}) copy-start(f32[1,2,128,1]{3,2,1,0:T(8,128)} %get-tuple-element.65) | copy-start | bytes 3076
  59.4 3.5 %copy-start.16 = (f32[1,1,128,256]{3,2,1,0:T(8,128)S(1)}, f32[1,1,128,256]{3,2,1,0:T(8,128)}, u32[]{:S(2)}) copy-start(f32[1,1,128,256]{3,2,1,0:T(8,128)} %get-tuple-element.70) | copy-start | bytes 393220
  59.4 3.5 %copy-start.17 = (f32[1,1,128,256]{3,2,1,0:T(8,128)S(1)}, f32[1,1,128,256]{3,2,1,0:T(8,128)}, u32[]{:S(2)}) copy-start(f32[1,1,128,256]{3,2,1,0:T(8,128)} %get-tuple-element.71) | copy-start | bytes 393220
  64.5 5.6 %collective-permute-start.10 = (f32[160,16]{0,1:T(8,128)S(1)}, f32[160,16]{0,1:T(8,128)S(1)}, u32[]{:S(2)}, u32[]{:S(2)}) collective-permute-start(f32[160,16]{0,1:T(8,128)S(1)} %get-tuple-element.59), channel_id=1, source_target_pairs={{0,1},{1,2},{2,3},{3,0},{4,5},{5,6},{6,7},{7,4},{8,9},{9,10},{10,1... | collective-permute-start | bytes 30728 | tf_op jit(solution)/shard_map/ppermute | solution.py:28
  65.6 4.5 %collective-permute-start.11 = (f32[160,16]{0,1:T(8,128)S(1)}, f32[160,16]{0,1:T(8,128)S(1)}, u32[]{:S(2)}, u32[]{:S(2)}) collective-permute-start(f32[160,16]{0,1:T(8,128)S(1)} %get-tuple-element.60), channel_id=1, source_target_pairs={{1,0},{2,1},{3,2},{0,3},{5,4},{6,5},{7,6},{4,7},{9,8},{10,9},{11,1... | collective-permute-start | bytes 30728 | tf_op jit(solution)/shard_map/ppermute | solution.py:29
  (22 other events, 46.6 us)
where the time goes:
time: 72.1 us; the launch traced here: 71.7 us
  local copies, waits for them, and re-layouts  32.1 us (45%)
  starting transfers between devices  15.5 us (21%)
  other arithmetic  15.2 us (21%)
  waiting for transfers between devices  5.34 us (7%)
  between operations  2 us (3%)
  matrix products  1.61 us (2%)
    concatenate x15, local copies, waits for them, and re-layouts, join_low(): jnp.roll(field, 1, axis=axis)  10.1 us
    ppermute x8, starting transfers between devices, from_behind(): return lax.ppermute(value, axis, pairs)  9.77 us
    concatenate x12, local copies, waits for them, and re-layouts, join_high(): jnp.roll(field, -1, axis=axis)  7.05 us
    unnamed x94, local copies, waits for them, and re-layouts  4.88 us
    ppermute x8, waiting for transfers between devices, from_behind(): return lax.ppermute(value, axis, pairs)  4.56 us
    ppermute x2, starting transfers between devices, with_halo(): after = lax.ppermute(leading, axis, down)  4.3 us
    add x6, other arithmetic, magnetic_update(): magnetic[component] + courant * rotor[component]  3.95 us
    concatenate x3, local copies, waits for them, and re-layouts, depth_high(): jnp.roll(field, -1, axis=0)  2.18 us
  transfers between devices with their start and end apart: 12, of which 4 were waited for; matrix products, arithmetic and copies ran while one was open for 30% of the time, Pallas kernels for 0%

commit v1 on v0

v1 whole, which is shorter than its diff:
```python
import math

import jax
import jax.numpy as jnp
from jax import lax
from jax.experimental import pallas as pl
from jax.experimental.pallas import tpu as pltpu
from jax.sharding import PartitionSpec as P

STEPS = 2
NMAT = 8
FILT = 16

courant = 0.5
spread_ratio = 0.6

F32 = jnp.float32
HIGHEST = lax.Precision.HIGHEST

LO_G, LO_E1T, LO_E1Z, LO_E2T, LO_E2Z = 0, 16, 18, 20, 22
LO_F0T, LO_F0Z, LO_F1T, LO_F1N, LO_F1Z = 24, 26, 28, 30, 32
LO_W1T, LO_W1Z, LO_R0, LO_R1, LO_ROWS = 34, 36, 38, 39, 40
HI_G, HI_H0T, HI_H0Z, HI_H1T, HI_H1Z = 0, 16, 18, 20, 22
HI_WT, HI_WN, HI_WZ, HI_R, HI_ROWS = 24, 26, 28, 30, 32
LANE_HI = 64
EXT = 24


def tap(distance):
    spread = spread_ratio * FILT
    norm = math.sqrt(sum(math.exp(-d * d / (spread * spread)) for d in range(-FILT, FILT + 1)))
    far = distance.astype(F32)
    value = jnp.exp(-far * far / (2.0 * spread * spread)) / norm
    return jnp.where(jnp.abs(distance) <= FILT, value, F32(0.0))


def iota(shape, dim):
    return lax.broadcasted_iota(jnp.int32, shape, dim)


def local_solve(e0, h0, fwd, ratio):
    n, m = ratio.shape
    row, col = iota((n, m), 0), iota((n, m), 1)
    nz = len(e0[0])

    def lx(f):
        return jnp.where(row == 0, 0.0, pltpu.roll(f, 1, 0))

    def ux(f):
        return jnp.where(row == n - 1, 0.0, pltpu.roll(f, n - 1, 0))

    def ly(f):
        return jnp.where(col == 0, 0.0, pltpu.roll(f, 1, 1))

    def uy(f):
        return jnp.where(col == m - 1, 0.0, pltpu.roll(f, m - 1, 1))

    def electric(e, h):
        out = [[None] * nz for _ in range(3)]
        for z in range(nz):
            hx, hy, hz = h[0][z], h[1][z], h[2][z]
            dzx = hx - h[0][z - 1] if z > 0 else hx
            dzy = hy - h[1][z - 1] if z > 0 else hy
            out[0][z] = e[0][z] - ratio * ((hz - ly(hz)) - dzy)
            out[1][z] = e[1][z] - ratio * (dzx - (hz - lx(hz)))
            out[2][z] = e[2][z] - ratio * ((hy - lx(hy)) - (hx - ly(hx)))
        return out

    def magnetic(e, h):
        out = [[None] * nz for _ in range(3)]
        for z in range(nz):
            ex, ey, ez = e[0][z], e[1][z], e[2][z]
            dzx = e[0][z + 1] - ex if z < nz - 1 else -ex
            dzy = e[1][z + 1] - ey if z < nz - 1 else -ey
            out[0][z] = h[0][z] + courant * ((uy(ez) - ez) - dzy)
            out[1][z] = h[1][z] + courant * (dzx - (ux(ez) - ez))
            out[2][z] = h[2][z] + courant * ((ux(ey) - ey) - (uy(ex) - ex))
        return out

    def product(e, f):
        total = None
        for c in range(3):
            for z in range(nz):
                term = e[c][z] * f[c][z]
                total = term if total is None else total + term
        return total

    e1 = electric(e0, h0)
    grad = product(e1, fwd[0])
    h1 = magnetic(e1, h0)
    e2 = electric(e1, h1)
    grad = grad + product(e2, fwd[1])
    h2 = magnetic(e2, h1)
    return e1, h1, e2, h2, grad


def seam(sgn, a, b, up, down):
    odd = iota(a["h0t"].shape, 0) % 2 == 1
    half = sgn * courant

    def uz(f):
        return jnp.where(odd, 0.0, pltpu.roll(f, 7, 0))

    def lz(f):
        return jnp.where(odd, pltpu.roll(f, 1, 0), 0.0)

    rb, rb1, ra = sgn * b["r0"], sgn * b["r1"], sgn * a["r"]
    d = {}
    e1t = rb * a["h0z"]
    e1z = -rb * a["h0t"]
    e1t_b = b["e1t"] + e1t
    e1z_b = b["e1z"] + e1z
    ah1t = half * e1z_b
    ah1z = -half * e1t_b
    h1t_a = a["h1t"] + ah1t
    h1z_a = a["h1z"] + ah1z
    bh1t = -half * e1z
    bh1n = half * ((uz(e1t) - e1t) - (up(e1z) - e1z))
    bh1z = half * e1t
    e2t = e1t - rb * ((bh1z - h1z_a) - (bh1n - lz(bh1n)))
    e2n = -rb * ((bh1t - lz(bh1t)) - (bh1z - down(bh1z)))
    e2z = e1z - rb * ((bh1n - down(bh1n)) - (bh1t - h1t_a))
    f2t = rb1 * bh1z
    f2z = -rb1 * bh1t
    at = ah1z
    an = (ah1t - lz(ah1t)) - (ah1z - down(ah1z))
    az = -ah1t
    g2t, g2n, g2z = -ra * at, -ra * an, -ra * az
    gb0 = b["f0t"] * e1t + b["f0z"] * e1z + b["f1t"] * e2t + b["f1n"] * e2n + b["f1z"] * e2z
    gb1 = sgn * (b["w1t"] * bh1z - b["w1z"] * bh1t)
    ga = -sgn * (a["wt"] * at + a["wn"] * an + a["wz"] * az)
    e2t_b = b["e2t"] + e2t
    e2z_b = b["e2z"] + e2z
    d["b_e1z"], d["b_h1n"], d["b_h1z"], d["a_h1z"] = e1z, bh1n, bh1z, ah1z
    none = jnp.zeros_like(e1t)
    d["e"] = {"t": (none, g2t, e2t, f2t), "n": (none, g2n, e2n, none), "z": (none, g2z, e2z, f2z)}
    d["h"] = {
        "t": (
            half * g2z,
            ah1t + half * ((e2z_b - g2z) - (uz(g2n) - g2n)),
            bh1t + half * ((f2z - e2z) - (uz(e2n) - e2n)),
            -half * f2z,
        ),
        "n": (
            none,
            half * ((uz(g2t) - g2t) - (up(g2z) - g2z)),
            bh1n + half * ((uz(e2t) - e2t) - (up(e2z) - e2z)),
            half * ((uz(f2t) - f2t) - (up(f2z) - f2z)),
        ),
        "z": (
            -half * g2t,
            ah1z + half * ((up(g2n) - g2n) - (e2t_b - g2t)),
            bh1z + half * ((up(e2n) - e2n) - (f2t - e2t)),
            half * f2t,
        ),
    }
    d["gb0"], d["gb1"], d["ga"] = (g + pltpu.roll(g, 7, 0) for g in (gb0, gb1, ga))
    return d


def two(first, second, at, count=2):
    if count == 1:
        one, other = first[at : at + 1], second[at : at + 1]
        parts = [one, one, other, other]
    else:
        parts = [first[at : at + 2], second[at : at + 2]]
    parts.append(jnp.zeros((4, first.shape[1]), F32))
    return jnp.concatenate(parts, axis=0)


def seam_inputs(left_hi, my_hi, my_lo, right_lo):
    a = {
        "h0t": two(left_hi, my_hi, HI_H0T),
        "h0z": two(left_hi, my_hi, HI_H0Z),
        "h1t": two(left_hi, my_hi, HI_H1T),
        "h1z": two(left_hi, my_hi, HI_H1Z),
        "wt": two(left_hi, my_hi, HI_WT),
        "wn": two(left_hi, my_hi, HI_WN),
        "wz": two(left_hi, my_hi, HI_WZ),
        "r": two(left_hi, my_hi, HI_R, 1),
    }
    b = {
        "e1t": two(my_lo, right_lo, LO_E1T),
        "e1z": two(my_lo, right_lo, LO_E1Z),
        "e2t": two(my_lo, right_lo, LO_E2T),
        "e2z": two(my_lo, right_lo, LO_E2Z),
        "f0t": two(my_lo, right_lo, LO_F0T),
        "f0z": two(my_lo, right_lo, LO_F0Z),
        "f1t": two(my_lo, right_lo, LO_F1T),
        "f1n": two(my_lo, right_lo, LO_F1N),
        "f1z": two(my_lo, right_lo, LO_F1Z),
        "w1t": two(my_lo, right_lo, LO_W1T),
        "w1z": two(my_lo, right_lo, LO_W1Z),
        "r0": two(my_lo, right_lo, LO_R0, 1),
        "r1": two(my_lo, right_lo, LO_R1, 1),
    }
    return a, b


def even(axis):
    return lax.axis_index(axis) % 2 == 0


def solve_kernel(e_ref, h_ref, f_ref, lab_ref, den_ref, eps_ref,
                 a_ref, b_ref, lo_ref, hi_ref, pack_ref, grad_ref, e2_ref, h2_ref):
    n, m = lab_ref.shape
    nz = e_ref.shape[1]
    labels = lab_ref[...]
    eps = jnp.full((n, m), eps_ref[0], F32)
    for k in range(1, NMAT):
        eps = jnp.where(labels == k, eps_ref[k], eps)
    ratio = courant / (eps + den_ref[...])
    e0 = [[e_ref[c, z] for z in range(nz)] for c in range(3)]
    h0 = [[h_ref[c, z] for z in range(nz)] for c in range(3)]
    fwd = [[[f_ref[s, c, z] for z in range(nz)] for c in range(3)] for s in range(STEPS)]
    e1, h1, e2, h2, grad = local_solve(e0, h0, fwd, ratio)
    for c in range(3):
        for z in range(nz):
            e2_ref[c, z] = e2[c][z]
            h2_ref[c, z] = h2[c][z]
    grad_ref[...] = grad

    def lists(t, nrm):
        zs = range(nz)
        lo = (
            [(e1[c][z], 0) for c in (t, 2) for z in zs]
            + [(e2[c][z], 0) for c in (t, 2) for z in zs]
            + [(fwd[0][c][z], 0) for c in (t, 2) for z in zs]
            + [(fwd[1][c][z], 0) for c in (t, nrm, 2) for z in zs]
            + [((ratio, fwd[1][c][z]), 1) for c in (t, 2) for z in zs]
            + [(ratio, 0), (ratio, 1)]
        )
        hi = (
            [(h0[c][z], -1) for c in (t, 2) for z in zs]
            + [(h1[c][z], -1) for c in (t, 2) for z in zs]
            + [((ratio, fwd[1][c][z]), -1) for c in (t, nrm, 2) for z in zs]
            + [(ratio, -1)]
        )
        return lo, hi

    def line(item, at):
        if isinstance(item, tuple):
            return line(item[0], at) * line(item[1], at)
        at = at % n
        return item[at : at + 1]

    lo, hi = lists(1, 0)
    lo_ref[0:FILT] = grad[0:FILT]
    for k, (item, at) in enumerate(lo):
        lo_ref[FILT + k : FILT + k + 1] = line(item, at)
    hi_ref[0:FILT] = grad[n - FILT : n]
    for k, (item, at) in enumerate(hi):
        hi_ref[FILT + k : FILT + k + 1] = line(item, at)
    hi_ref[HI_ROWS - 1 : HI_ROWS] = jnp.zeros((1, m), F32)

    lane = iota((n, 128), 1)
    lo, hi = lists(0, 1)
    first, last = grad[:, 0:128], grad[:, m - 128 : m]
    pack = jnp.where(lane < FILT, first, 0.0)
    moved = pltpu.roll(last, LANE_HI + FILT, 1)
    pack = jnp.where((lane >= LANE_HI) & (lane < LANE_HI + FILT), moved, pack)

    def tile(item, at):
        if isinstance(item, tuple):
            return tile(item[0], at) * tile(item[1], at)
        return item[:, m - 128 : m] if at < 0 else item[:, 0:128]

    for group, start in ((lo, FILT), (hi, LANE_HI + FILT)):
        for k, (item, at) in enumerate(group):
            pack = jnp.where(lane == start + k, pltpu.roll(tile(item, at), (start + k - at) % 128, 1), pack)
    pack_ref[...] = pack

    def corner(rows):
        low = jnp.concatenate([rows[0:8], rows[8:16]], axis=1)
        high = jnp.concatenate([rows[16:24], jnp.zeros((8, m - 128), F32)], axis=1)
        return jnp.concatenate([low, high], axis=0)

    lo_all = jnp.concatenate([lo_ref[...], corner(pack[0:EXT])], axis=0)
    hi_all = jnp.concatenate([hi_ref[...], jnp.zeros((LO_ROWS - HI_ROWS, m), F32), corner(pack[n - EXT : n])], axis=0)
    first_even = even("gx")
    a_ref[...] = jnp.where(first_even, hi_all, lo_all)
    b_ref[...] = jnp.where(first_even, lo_all, hi_all)


def x_kernel(ra_ref, rb_ref, lo_ref, hi_ref, pack_ref, grad_ref,
             a_ref, b_ref, ylo_ref, yhi_ref, ext_ref, dr_ref):
    n, m = grad_ref.shape
    first_even = even("gx")
    right = jnp.where(first_even, ra_ref[...], rb_ref[...])
    left = jnp.where(first_even, rb_ref[...], ra_ref[...])
    a, b = seam_inputs(left, hi_ref[...], lo_ref[...], right)
    col = iota((8, m), 1)
    d = seam(
        -1.0, a, b,
        lambda f: jnp.where(col == m - 1, 0.0, pltpu.roll(f, m - 1, 1)),
        lambda f: jnp.where(col == 0, 0.0, pltpu.roll(f, 1, 1)),
    )
    for f, field in enumerate(("e", "h")):
        for c, name in enumerate(("n", "t", "z")):
            before, end, begin, after = d[field][name]
            for z in range(2):
                p = 4 * (6 * f + 2 * c + z)
                dr_ref[p : p + 1] = before[2 + z : 3 + z]
                dr_ref[p + 1 : p + 2] = end[2 + z : 3 + z]
                dr_ref[p + 2 : p + 3] = begin[z : z + 1]
                dr_ref[p + 3 : p + 4] = after[z : z + 1]
    gb0, gb1, ga = d["gb0"], d["gb1"], d["ga"]
    top = iota((8, m), 0)
    ext_ref[0:n] = grad_ref[...]
    ext_ref[0:8] = grad_ref[0:8] + jnp.where(top == 0, gb0[0:1], jnp.where(top == 1, gb1[0:1], 0.0))
    ext_ref[n - 8 : n] = grad_ref[n - 8 : n] + jnp.where(top == 7, ga[2:3], 0.0)
    ext_ref[n : n + 8] = right[0:8] + jnp.where(top == 0, gb0[2:3], jnp.where(top == 1, gb1[2:3], 0.0))
    ext_ref[n + 8 : n + 16] = right[8:16]
    ext_ref[n + 16 : 2 * n - 16] = jnp.zeros((n - 32, m), F32)
    ext_ref[2 * n - 16 : 2 * n - 8] = left[0:8]
    ext_ref[2 * n - 8 : 2 * n] = left[8:16] + jnp.where(top == 7, ga[0:1], 0.0)

    lane = iota((1, 128), 1)

    def strips(g):
        out = jnp.where(lane < FILT, g[:, 0:128], 0.0)
        moved = pltpu.roll(g[:, m - 128 : m], LANE_HI + FILT, 1)
        return jnp.where((lane >= LANE_HI) & (lane < LANE_HI + FILT), moved, out)

    def put(row_vec, at, value, seam_row, c):
        for z in range(2):
            one = value[seam_row + z : seam_row + z + 1, c : c + 1]
            row_vec = jnp.where(lane == at + z, one, row_vec)
        return row_vec

    hi = LANE_HI
    row0 = strips(gb0[0:1])
    row0 = put(row0, LO_E1Z, d["b_e1z"], 0, 0)
    row0 = put(row0, LO_E2T, d["e"]["n"][2], 0, 0)
    row0 = put(row0, LO_E2Z, d["e"]["z"][2], 0, 0)
    row0 = put(row0, hi + HI_H1T, d["b_h1n"], 0, m - 1)
    row0 = put(row0, hi + HI_H1Z, d["b_h1z"], 0, m - 1)
    row1 = strips(gb1[0:1])
    row1 = put(row1, LO_E2Z, d["e"]["z"][3], 0, 0)
    end = strips(ga[2:3])
    end = put(end, LO_E2T, d["e"]["n"][1], 2, 0)
    end = put(end, LO_E2Z, d["e"]["z"][1], 2, 0)
    end = put(end, hi + HI_H1Z, d["a_h1z"], 2, m - 1)
    out0 = strips(gb0[2:3])
    out0 = put(out0, LO_E1Z, d["b_e1z"], 2, 0)
    out0 = put(out0, hi + HI_H1T, d["b_h1n"], 2, m - 1)
    out0 = put(out0, hi + HI_H1Z, d["b_h1z"], 2, m - 1)
    out1 = strips(gb1[2:3])
    before = strips(ga[0:1])
    before = put(before, hi + HI_H1Z, d["a_h1z"], 0, m - 1)

    sub = iota((8, 128), 0)

    def corner(message):
        return [message[40:48, 0:128], message[40:48, 128:256], message[48:56, 0:128]]

    above, below = corner(right), corner(left)
    above[0] = above[0] + jnp.where(sub == 0, out0, jnp.where(sub == 1, out1, 0.0))
    below[2] = below[2] + jnp.where(sub == 7, before, 0.0)
    head = pack_ref[0:8] + jnp.where(sub == 0, row0, jnp.where(sub == 1, row1, 0.0))
    tail = pack_ref[n - 8 : n] + jnp.where(sub == 7, end, 0.0)
    inner = jnp.concatenate([head, pack_ref[8 : n - 8], tail], axis=0)
    outer = jnp.concatenate(above + [jnp.zeros((n - 2 * EXT, 128), F32)] + below, axis=0)
    packed = jnp.concatenate([inner.T, outer.T], axis=1)
    lo, hi_part = packed[0:LO_ROWS], packed[LANE_HI : LANE_HI + LO_ROWS]
    ylo_ref[...] = lo
    yhi_ref[...] = hi_part
    y_even = even("gy")
    a_ref[...] = jnp.where(y_even, hi_part, lo)
    b_ref[...] = jnp.where(y_even, lo, hi_part)


def inner_kernel(ext_ref, out_ref):
    rows, m = ext_ref.shape
    n = out_ref.shape[0]
    d = iota((n, rows), 1) - iota((n, rows), 0)
    d = jnp.where(d > rows // 2, d - rows, jnp.where(d < -(rows // 2), d + rows, d))
    along = jnp.dot(tap(d), ext_ref[...], precision=HIGHEST, preferred_element_type=F32)
    e = iota((m, m), 0) - iota((m, m), 1)
    out_ref[...] = jnp.dot(along, tap(e), precision=HIGHEST, preferred_element_type=F32)


def y_kernel(ra_ref, rb_ref, lo_ref, hi_ref, dr_ref, e2_ref, h2_ref, inner_ref,
             e_ref, h_ref, out_ref, gt_ref, dc_ref):
    n, m = inner_ref.shape
    y_even = even("gy")
    right = jnp.where(y_even, ra_ref[...], rb_ref[...])
    left = jnp.where(y_even, rb_ref[...], ra_ref[...])
    rows = right.shape[1]
    a, b = seam_inputs(left, hi_ref[...], lo_ref[...], right)
    d = seam(1.0, a, b, lambda f: pltpu.roll(f, rows - 1, 1), lambda f: pltpu.roll(f, 1, 1))

    gb0, gb1, ga = d["gb0"], d["gb1"], d["ga"]
    top = iota((8, rows), 0)
    gt_ref[0:8] = right[0:8] + jnp.where(top == 0, gb0[2:3], jnp.where(top == 1, gb1[2:3], 0.0))
    gt_ref[8:16] = right[8:16]
    gt_ref[16:24] = left[0:8]
    gt_ref[24:32] = left[8:16] + jnp.where(top == 7, ga[0:1], 0.0)
    gt_ref[32:40] = jnp.where(top == 0, gb0[0:1], jnp.where(top == 1, gb1[0:1], jnp.where(top == 2, ga[2:3], 0.0)))

    for f, field in enumerate(("e", "h")):
        for c, name in enumerate(("t", "n", "z")):
            before, end, begin, after = d[field][name]
            for z in range(2):
                p = 4 * (6 * f + 2 * c + z)
                dc_ref[p : p + 1] = before[2 + z : 3 + z, 0:n]
                dc_ref[p + 1 : p + 2] = end[2 + z : 3 + z, 0:n]
                dc_ref[p + 2 : p + 3] = begin[z : z + 1, 0:n]
                dc_ref[p + 3 : p + 4] = after[z : z + 1, 0:n]
    dc_ref[48:128] = jnp.zeros((80, n), F32)
    columns = dc_ref[...].T
    lane = iota((n, 128), 1)
    sub = iota((8, m), 0)
    for f, (src, dst) in enumerate(((e2_ref, e_ref), (h2_ref, h_ref))):
        for c in range(3):
            for z in range(2):
                p = 4 * (6 * f + 2 * c + z)
                moved = pltpu.roll(columns, (126 - p) % 128, 1)
                low = src[c, z, :, 0:128] + jnp.where(lane < 2, moved, 0.0)
                high = src[c, z, :, m - 128 : m] + jnp.where(lane >= 126, moved, 0.0)
                dst[c, z, :, 0:128] = low
                dst[c, z, :, m - 128 : m] = high
                dst[c, z, 0:8] += jnp.where(sub == 0, dr_ref[p + 2 : p + 3], jnp.where(sub == 1, dr_ref[p + 3 : p + 4], 0.0))
                dst[c, z, n - 8 : n] += jnp.where(sub == 6, dr_ref[p : p + 1], jnp.where(sub == 7, dr_ref[p + 1 : p + 2], 0.0))

    d = iota((rows, n), 0) - iota((rows, n), 1)
    d = jnp.where(d > rows // 2, d - rows, jnp.where(d < -(rows // 2), d + rows, d))
    along = jnp.dot(gt_ref[...], tap(d), precision=HIGHEST, preferred_element_type=F32)
    k = iota((40, m), 0)
    place = jnp.where(k < 16, m + k, jnp.where(k < 32, k - 32, jnp.where(k < 34, k - 32, m - 1)))
    spread = jnp.where(k < 35, tap(place - iota((40, m), 1)), 0.0)
    extra = lax.dot_general(along, spread, (((0,), (0,)), ((), ())), precision=HIGHEST, preferred_element_type=F32)
    out_ref[...] = inner_ref[...] + extra


def swap_pairs(count, which):
    if which == 0:
        return [(i, i ^ 1) for i in range(count)]
    return [(i, (i - 1) % count if i % 2 == 0 else (i + 1) % count) for i in range(count)]


def call(kernel, shapes, ins, scratch=()):
    vmem = pl.BlockSpec(memory_space=pltpu.VMEM)
    return pl.pallas_call(
        kernel,
        out_shape=[jax.ShapeDtypeStruct(s, F32) for s in shapes],
        in_specs=[pl.BlockSpec(memory_space=pltpu.SMEM) if x.shape == (NMAT,) else vmem for x in ins],
        out_specs=[vmem] * len(shapes),
        scratch_shapes=[pltpu.VMEM(s, F32) for s in scratch],
        compiler_params=pltpu.CompilerParams(vmem_limit_bytes=40 * 1024 * 1024),
    )(*ins)


def body(adj_e, adj_h, fwd_e, labels, eps_table, density):
    n, m = labels.shape
    block = adj_e.shape
    message = (LO_ROWS + 16, m)
    xa, xb, lo, hi, pack, grad, e2, h2 = call(
        solve_kernel,
        [message, message, (LO_ROWS, m), (HI_ROWS, m), (n, 128), (n, m), block, block],
        [adj_e, adj_h, fwd_e, labels, density, eps_table],
    )
    gx, gy = lax.axis_size("gx"), lax.axis_size("gy")
    got_a = lax.ppermute(xa, "gx", swap_pairs(gx, 0))
    got_b = lax.ppermute(xb, "gx", swap_pairs(gx, 1))
    column = (LO_ROWS, 2 * n)
    ya, yb, ylo, yhi, ext, dr = call(
        x_kernel,
        [column, column, column, column, (2 * n, m), (48, m)],
        [got_a, got_b, lo, hi, pack, grad],
    )
    got_a = lax.ppermute(ya, "gy", swap_pairs(gy, 0))
    got_b = lax.ppermute(yb, "gy", swap_pairs(gy, 1))
    (inner,) = call(inner_kernel, [(n, m)], [ext])
    return tuple(
        call(
            y_kernel,
            [block, block, (n, m)],
            [got_a, got_b, ylo, yhi, dr, e2, h2, inner],
            [(40, 2 * n), (128, n)],
        )
    )


def solution(mesh):
    return jax.shard_map(
        body,
        mesh=mesh,
        in_specs=(
            P("design", None, "gx", "gy"),
            P("design", None, "gx", "gy"),
            P("design", None, None, "gx", "gy"),
            P(("design", "gx"), "gy"),
            P(),
            P(("design", "gx"), "gy"),
        ),
        out_specs=(
            P("design", None, "gx", "gy"),
            P("design", None, "gx", "gy"),
            P(("design", "gx"), "gy"),
        ),
        check_vma=False,
    )
```

time: 72.1 us -> 24.2 us (0.34)
  local copies, waits for them, and re-layouts: 32.1 us -> 6.13 us
  other arithmetic: 15.2 us -> 0 us
  starting transfers between devices: 15.5 us -> 7.11 us
  Pallas kernels: 0 us -> 5.23 us
  matrix products: 1.61 us -> 0 us
  between operations: 2 us -> 0.68 us
    concatenate x32 -> x0, local copies, waits for them, and re-layouts: 20.8 us -> none  [the longest x15 10.1 us: join_low(): jnp.roll(field, 1, axis=axis)]
    ppermute x12 -> x4, starting transfers between devices: 15.5 us -> 7.11 us  [the longest x1 2.61 us: body(): got_b = lax.ppermute(xb, 'gx', swap_pairs(gx, 1))]
    pallas_call x0 -> x4, Pallas kernels: none -> 5.23 us  [call(): pl.pallas_call(kernel, out_shape=[jax.ShapeDtypeStruct(s, F32) for s in s...]
    add x7 -> x0, other arithmetic: 4.93 us -> none  [the longest x6 3.95 us: magnetic_update(): magnetic[component] + courant * rotor[component]]
    another operation x10 -> x0, other arithmetic: 4.35 us -> none  [the longest x2 1.88 us: body(): return (jnp.stack(electric), jnp.stack(magnetic), filtered)]
    slice x7 -> x0, local copies, waits for them, and re-layouts: 3.1 us -> none  [the longest x2 1.33 us: magnetic_update(): electric[2][:, :, 0]]
    eq x6 -> x0, other arithmetic: 2.21 us -> none  [the longest x2 1.09 us: join_high(): place == last]
    reduce_sum x3 -> x0, other arithmetic: 2.18 us -> none  [the longest x1 1.35 us: body(): gradient = gradient + jnp.sum(product, axis=0)]
  transfers between devices with their start and end apart: 12 -> 4, of which waited for: 4 -> 2; matrix products, arithmetic and copies ran while one was open for 30% -> 0% of each run, Pallas kernels for 0% -> 3%
where the time goes in v1:
time: 24.2 us; the launch traced here: 24 us
  starting transfers between devices  7.11 us (29%)
  local copies, waits for them, and re-layouts  6.13 us (25%)
  Pallas kernels  5.23 us (22%)
  waiting for transfers between devices  4.79 us (20%)
  between operations  0.68 us (3%)
    unnamed x12, local copies, waits for them, and re-layouts  6.13 us
    pallas_call x4, Pallas kernels, call(): pl.pallas_call(kernel, out_shape=[jax.ShapeDtypeStruct(s, F32) for s in s...  5.23 us
    ppermute x1, starting transfers between devices, body(): got_b = lax.ppermute(xb, 'gx', swap_pairs(gx, 1))  2.61 us
    ppermute x1, waiting for transfers between devices, body(): got_b = lax.ppermute(yb, 'gy', swap_pairs(gy, 1))  2.6 us
    ppermute x1, starting transfers between devices, body(): got_b = lax.ppermute(yb, 'gy', swap_pairs(gy, 1))  2.47 us
    ppermute x1, waiting for transfers between devices, body(): got_b = lax.ppermute(xb, 'gx', swap_pairs(gx, 1))  2.19 us
    ppermute x1, starting transfers between devices, body(): got_a = lax.ppermute(ya, 'gy', swap_pairs(gy, 0))  1.51 us
    ppermute x1, starting transfers between devices, body(): got_a = lax.ppermute(xa, 'gx', swap_pairs(gx, 0))  0.52 us
  transfers between devices with their start and end apart: 4, of which 2 were waited for; matrix products, arithmetic and copies ran while one was open for 0% of the time, Pallas kernels for 3%

profile of v1, /device:TPU:0, one launch (start us, length us, event | category | flops | bytes accessed | tf_op | source)
XLA Modules:
  0.0 24.0 jit_solution(358592168918654539)
XLA Ops:
  0.6 0.0 copy-start
  0.6 1.4 %copy-done = f32[2,3,2,128,256]{4,3,2,1,0:T(8,128)S(1)} copy-done((f32[2,3,2,128,256]{4,3,2,1,0:T(8,128)S(1)}, f32[2,3,2,128,256]{4,3,2,1,0:T(8,128)}, u32[]{:S(2)}) %copy-start) | copy-done | bytes 1572888
  2.0 0.0 copy-start.1
  2.0 1.1 %copy-done.1 = f32[3,2,128,256]{3,2,1,0:T(8,128)S(1)} copy-done((f32[3,2,128,256]{3,2,1,0:T(8,128)S(1)}, f32[3,2,128,256]{3,2,1,0:T(8,128)}, u32[]{:S(2)}) %copy-start.1) | copy-done | bytes 786456
  3.2 0.0 copy-start.2
  3.2 1.1 %copy-done.2 = f32[3,2,128,256]{3,2,1,0:T(8,128)S(1)} copy-done((f32[3,2,128,256]{3,2,1,0:T(8,128)S(1)}, f32[3,2,128,256]{3,2,1,0:T(8,128)}, u32[]{:S(2)}) %copy-start.2) | copy-done | bytes 786456
  4.3 0.0 copy-start.3
  4.3 0.9 %copy-done.3 = s32[128,256]{1,0:T(8,128)S(1)} copy-done((s32[128,256]{1,0:T(8,128)S(1)}, s32[128,256]{1,0:T(8,128)}, u32[]{:S(2)}) %copy-start.3) | copy-done | bytes 131096
  5.2 0.0 copy-start.4
  5.2 0.9 %copy-done.4 = f32[128,256]{1,0:T(8,128)S(1)} copy-done((f32[128,256]{1,0:T(8,128)S(1)}, f32[128,256]{1,0:T(8,128)}, u32[]{:S(2)}) %copy-start.4) | copy-done | bytes 131096
  6.1 0.0 copy-start.5
  6.1 0.7 %copy-done.5 = f32[8]{0:T(128)S(1)} copy-done((f32[8]{0:T(128)S(1)}, f32[8]{0:T(128)}, u32[]{:S(2)}) %copy-start.5) | copy-done | bytes 56
  6.8 2.4 %shard_map.85 = (f32[56,256]{1,0:T(8,128)S(1)}, f32[56,256]{1,0:T(8,128)S(1)}, f32[40,256]{1,0:T(8,128)S(1)}, f32[32,256]{1,0:T(8,128)S(1)}, f32[128,128]{1,0:T(...) custom-call(f32[3,2,128,256]{3,2,1,0:T(8,128)S(1)} %copy-done.1, ...), custom_call_target="tpu_custom_call" | custom-call | tf_op jit(solution)/shard_map/pallas_call | solution.py:444
  9.2 0.5 %collective-permute-start = (f32[56,256]{1,0:T(8,128)S(1)}, f32[56,256]{1,0:T(8,128)S(1)}, u32[]{:S(2)}, u32[]{:S(2)}) collective-permute-start(f32[56,256]{1,0:T(8,128)S(1)} %get-tuple-element.17), channel_id=1, source_target_pairs={{0,4},{4,0},{8,12},{12,8},{1,5},{5,1},{9,13},{13,9},{2,6},{6,2},{1... | collective-permute-start | bytes 172040 | tf_op jit(solution)/shard_map/ppermute | solution.py:464
  9.7 2.6 %collective-permute-start.1 = (f32[56,256]{1,0:T(8,128)S(1)}, f32[56,256]{1,0:T(8,128)S(1)}, u32[]{:S(2)}, u32[]{:S(2)}) collective-permute-start(f32[56,256]{1,0:T(8,128)S(1)} %get-tuple-element.18), channel_id=1, source_target_pairs={{0,12},{4,8},{8,4},{12,0},{1,13},{5,9},{9,5},{13,1},{2,14},{6,10},... | collective-permute-start | bytes 172040 | tf_op jit(solution)/shard_map/ppermute | solution.py:465
  12.3 0.0 collective-permute-done.ra_ref
  12.3 2.2 %collective-permute-done.1.rb_ref = f32[56,256]{1,0:T(8,128)S(1)} collective-permute-done((f32[56,256]{1,0:T(8,128)S(1)}, f32[56,256]{1,0:T(8,128)S(1)}, u32[]{:S(2)}, u32[]{:S(2)}) %collective-permute-start.1) | collective-permute-done | bytes 57376 | tf_op jit(solution)/shard_map/ppermute | solution.py:465
  14.5 0.4 %shard_map.86 = (f32[40,256]{1,0:T(8,128)S(1)}, f32[40,256]{1,0:T(8,128)S(1)}, f32[40,256]{1,0:T(8,128)S(1)}, f32[40,256]{1,0:T(8,128)S(1)}, f32[256,256]{1,0:T(8,128)S(1)}, /*index=5*/f32[48,256]{1,0:T(8,128)S(1)}) custom-call(f32[56,256]{1,0:T(8,128)S(1)} %collective-permute-done.ra_ref, f32[56,256]{1,0:T(8,128)S(1)} %collective-permute-done.1.rb_ref, ...), custom_call_target="tpu_custom_call" | custom-call | tf_op jit(solution)/shard_map/pallas_call | solution.py:444
  14.9 1.5 %collective-permute-start.2 = (f32[40,256]{1,0:T(8,128)S(1)}, f32[40,256]{1,0:T(8,128)S(1)}, u32[]{:S(2)}, u32[]{:S(2)}) collective-permute-start(f32[40,256]{1,0:T(8,128)S(1)} %get-tuple-element.23), channel_id=1, source_target_pairs={{0,1},{1,0},{2,3},{3,2},{4,5},{5,4},{6,7},{7,6},{8,9},{9,8},{10,11... | collective-permute-start | bytes 122888 | tf_op jit(solution)/shard_map/ppermute | solution.py:472
  16.4 2.5 %collective-permute-start.3 = (f32[40,256]{1,0:T(8,128)S(1)}, f32[40,256]{1,0:T(8,128)S(1)}, u32[]{:S(2)}, u32[]{:S(2)}) collective-permute-start(f32[40,256]{1,0:T(8,128)S(1)} %get-tuple-element.24), channel_id=1, source_target_pairs={{0,3},{1,2},{2,1},{3,0},{4,7},{5,6},{6,5},{7,4},{8,11},{9,10},{10,... | collective-permute-start | bytes 122888 | tf_op jit(solution)/shard_map/ppermute | solution.py:473
  18.9 0.7 %shard_map.87.inner_ref = f32[128,256]{1,0:T(8,128)S(1)} custom-call(f32[256,256]{1,0:T(8,128)S(1)} %get-tuple-element.30.ext_ref), custom_call_target="tpu_custom_call" | custom-call | tf_op jit(solution)/shard_map/pallas_call | solution.py:444
  19.6 0.0 collective-permute-done.2.ra_ref
  19.6 2.6 %collective-permute-done.3.rb_ref = f32[40,256]{1,0:T(8,128)S(1)} collective-permute-done((f32[40,256]{1,0:T(8,128)S(1)}, f32[40,256]{1,0:T(8,128)S(1)}, u32[]{:S(2)}, u32[]{:S(2)}) %collective-permute-start.3) | collective-permute-done | bytes 40992 | tf_op jit(solution)/shard_map/ppermute | solution.py:473
  22.2 1.8 %shard_map.88 = (f32[3,2,128,256]{3,2,1,0:T(8,128)}, f32[3,2,128,256]{3,2,1,0:T(8,128)}, f32[128,256]{1,0:T(8,128)}) custom-call(f32[40,256]{1,0:T(8,128)S(1)} %collective-permute-done.2.ra_ref, f32[40,256]{1,0:T(8,128)S(1)} %collective-permute-done.3.rb_ref, f32[40,256]{1,0:T(8,128)S(1)} %get-tuple-element.25.lo_ref, ...), custom_call_target="tpu_custom_call" | custom-call | tf_op jit(solution)/shard_map/pallas_call | solution.py:444
Async XLA Ops:
  0.6 1.4 %copy-start = (f32[2,3,2,128,256]{4,3,2,1,0:T(8,128)S(1)}, f32[2,3,2,128,256]{4,3,2,1,0:T(8,128)}, u32[]{:S(2)}) copy-start(f32[2,3,2,128,256]{4,3,2,1,0:T(8,128)} %f_ref.1) | copy-start | bytes 4718596
  2.0 1.1 %copy-start.1 = (f32[3,2,128,256]{3,2,1,0:T(8,128)S(1)}, f32[3,2,128,256]{3,2,1,0:T(8,128)}, u32[]{:S(2)}) copy-start(f32[3,2,128,256]{3,2,1,0:T(8,128)} %e_ref.1) | copy-start | bytes 2359300
  3.2 1.1 %copy-start.2 = (f32[3,2,128,256]{3,2,1,0:T(8,128)S(1)}, f32[3,2,128,256]{3,2,1,0:T(8,128)}, u32[]{:S(2)}) copy-start(f32[3,2,128,256]{3,2,1,0:T(8,128)} %h_ref.1) | copy-start | bytes 2359300
  4.3 0.9 %copy-start.3 = (s32[128,256]{1,0:T(8,128)S(1)}, s32[128,256]{1,0:T(8,128)}, u32[]{:S(2)}) copy-start(s32[128,256]{1,0:T(8,128)} %lab_ref.1) | copy-start | bytes 393220
  5.2 0.9 %copy-start.4 = (f32[128,256]{1,0:T(8,128)S(1)}, f32[128,256]{1,0:T(8,128)}, u32[]{:S(2)}) copy-start(f32[128,256]{1,0:T(8,128)} %den_ref.1) | copy-start | bytes 393220
  6.1 0.7 %copy-start.5 = (f32[8]{0:T(128)S(1)}, f32[8]{0:T(128)}, u32[]{:S(2)}) copy-start(f32[8]{0:T(128)} %eps_ref.1) | copy-start | bytes 100
  9.2 3.1 %collective-permute-start = (f32[56,256]{1,0:T(8,128)S(1)}, f32[56,256]{1,0:T(8,128)S(1)}, u32[]{:S(2)}, u32[]{:S(2)}) collective-permute-start(f32[56,256]{1,0:T(8,128)S(1)} %get-tuple-element.17), channel_id=1, source_target_pairs={{0,4},{4,0},{8,12},{12,8},{1,5},{5,1},{9,13},{13,9},{2,6},{6,2},{1... | collective-permute-start | bytes 172040 | tf_op jit(solution)/shard_map/ppermute | solution.py:464
  9.7 4.8 %collective-permute-start.1 = (f32[56,256]{1,0:T(8,128)S(1)}, f32[56,256]{1,0:T(8,128)S(1)}, u32[]{:S(2)}, u32[]{:S(2)}) collective-permute-start(f32[56,256]{1,0:T(8,128)S(1)} %get-tuple-element.18), channel_id=1, source_target_pairs={{0,12},{4,8},{8,4},{12,0},{1,13},{5,9},{9,5},{13,1},{2,14},{6,10},... | collective-permute-start | bytes 172040 | tf_op jit(solution)/shard_map/ppermute | solution.py:465
  14.9 4.7 %collective-permute-start.2 = (f32[40,256]{1,0:T(8,128)S(1)}, f32[40,256]{1,0:T(8,128)S(1)}, u32[]{:S(2)}, u32[]{:S(2)}) collective-permute-start(f32[40,256]{1,0:T(8,128)S(1)} %get-tuple-element.23), channel_id=1, source_target_pairs={{0,1},{1,0},{2,3},{3,2},{4,5},{5,4},{6,7},{7,6},{8,9},{9,8},{10,11... | collective-permute-start | bytes 122888 | tf_op jit(solution)/shard_map/ppermute | solution.py:472
  16.4 5.8 %collective-permute-start.3 = (f32[40,256]{1,0:T(8,128)S(1)}, f32[40,256]{1,0:T(8,128)S(1)}, u32[]{:S(2)}, u32[]{:S(2)}) collective-permute-start(f32[40,256]{1,0:T(8,128)S(1)} %get-tuple-element.24), channel_id=1, source_target_pairs={{0,3},{1,2},{2,1},{3,0},{4,7},{5,6},{6,5},{7,4},{8,11},{9,10},{10,... | collective-permute-start | bytes 122888 | tf_op jit(solution)/shard_map/ppermute | solution.py:473

commit v2 on v1

--- a/solution.py
+++ b/solution.py
@@ -38,10 +38,8 @@
     return lax.broadcasted_iota(jnp.int32, shape, dim)
 
 
-def local_solve(e0, h0, fwd, ratio):
-    n, m = ratio.shape
+def updates(n, m, nz):
     row, col = iota((n, m), 0), iota((n, m), 1)
-    nz = len(e0[0])
 
     def lx(f):
         return jnp.where(row == 0, 0.0, pltpu.roll(f, 1, 0))
@@ -55,7 +53,7 @@
     def uy(f):
         return jnp.where(col == m - 1, 0.0, pltpu.roll(f, m - 1, 1))
 
-    def electric(e, h):
+    def electric(e, h, ratio):
         out = [[None] * nz for _ in range(3)]
         for z in range(nz):
             hx, hy, hz = h[0][z], h[1][z], h[2][z]
@@ -77,21 +75,28 @@
             out[2][z] = h[2][z] + courant * ((ux(ey) - ey) - (uy(ex) - ex))
         return out
 
-    def product(e, f):
-        total = None
-        for c in range(3):
-            for z in range(nz):
-                term = e[c][z] * f[c][z]
-                total = term if total is None else total + term
-        return total
-
-    e1 = electric(e0, h0)
+    return electric, magnetic
+
+
+def product(e, f):
+    total = None
+    for c in range(3):
+        for z in range(len(e[c])):
+            term = e[c][z] * f[c][z]
+            total = term if total is None else total + term
+    return total
+
+
+def local_solve(e0, h0, saved, ratio):
+    electric, magnetic = updates(*ratio.shape, len(e0[0]))
+    e1 = electric(e0, h0, ratio)
+    h1 = magnetic(e1, h0)
+    fwd = [saved(0)]
     grad = product(e1, fwd[0])
-    h1 = magnetic(e1, h0)
-    e2 = electric(e1, h1)
+    e2 = electric(e1, h1, ratio)
+    fwd.append(saved(1))
     grad = grad + product(e2, fwd[1])
-    h2 = magnetic(e2, h1)
-    return e1, h1, e2, h2, grad
+    return e1, h1, e2, grad, fwd
 
 
 def seam(sgn, a, b, up, down):
@@ -201,60 +206,39 @@
     return lax.axis_index(axis) % 2 == 0
 
 
-def solve_kernel(e_ref, h_ref, f_ref, lab_ref, den_ref, eps_ref,
-                 a_ref, b_ref, lo_ref, hi_ref, pack_ref, grad_ref, e2_ref, h2_ref):
-    n, m = lab_ref.shape
-    nz = e_ref.shape[1]
-    labels = lab_ref[...]
-    eps = jnp.full((n, m), eps_ref[0], F32)
+def ratio_of(labels, density, eps_ref):
+    eps = jnp.full(labels.shape, eps_ref[0], F32)
     for k in range(1, NMAT):
         eps = jnp.where(labels == k, eps_ref[k], eps)
-    ratio = courant / (eps + den_ref[...])
-    e0 = [[e_ref[c, z] for z in range(nz)] for c in range(3)]
-    h0 = [[h_ref[c, z] for z in range(nz)] for c in range(3)]
-    fwd = [[[f_ref[s, c, z] for z in range(nz)] for c in range(3)] for s in range(STEPS)]
-    e1, h1, e2, h2, grad = local_solve(e0, h0, fwd, ratio)
-    for c in range(3):
-        for z in range(nz):
-            e2_ref[c, z] = e2[c][z]
-            h2_ref[c, z] = h2[c][z]
-    grad_ref[...] = grad
-
-    def lists(t, nrm):
-        zs = range(nz)
-        lo = (
-            [(e1[c][z], 0) for c in (t, 2) for z in zs]
-            + [(e2[c][z], 0) for c in (t, 2) for z in zs]
-            + [(fwd[0][c][z], 0) for c in (t, 2) for z in zs]
-            + [(fwd[1][c][z], 0) for c in (t, nrm, 2) for z in zs]
-            + [((ratio, fwd[1][c][z]), 1) for c in (t, 2) for z in zs]
-            + [(ratio, 0), (ratio, 1)]
-        )
-        hi = (
-            [(h0[c][z], -1) for c in (t, 2) for z in zs]
-            + [(h1[c][z], -1) for c in (t, 2) for z in zs]
-            + [((ratio, fwd[1][c][z]), -1) for c in (t, nrm, 2) for z in zs]
-            + [(ratio, -1)]
-        )
-        return lo, hi
-
-    def line(item, at):
-        if isinstance(item, tuple):
-            return line(item[0], at) * line(item[1], at)
-        at = at % n
-        return item[at : at + 1]
-
-    lo, hi = lists(1, 0)
-    lo_ref[0:FILT] = grad[0:FILT]
-    for k, (item, at) in enumerate(lo):
-        lo_ref[FILT + k : FILT + k + 1] = line(item, at)
-    hi_ref[0:FILT] = grad[n - FILT : n]
-    for k, (item, at) in enumerate(hi):
-        hi_ref[FILT + k : FILT + k + 1] = line(item, at)
-    hi_ref[HI_ROWS - 1 : HI_ROWS] = jnp.zeros((1, m), F32)
-
+    return courant / (eps + density)
+
+
+def planes(ref, *lead):
+    return [[ref[(*lead, c, z)] for z in range(ref.shape[-3])] for c in range(3)]
+
+
+def edge_lists(t, nrm, e1, h0, h1, e2, fwd, ratio):
+    zs = range(len(e1[0]))
+    lo = (
+        [(e1[c][z], 0) for c in (t, 2) for z in zs]
+        + [(e2[c][z], 0) for c in (t, 2) for z in zs]
+        + [(fwd[0][c][z], 0) for c in (t, 2) for z in zs]
+        + [(fwd[1][c][z], 0) for c in (t, nrm, 2) for z in zs]
+        + [((ratio, fwd[1][c][z]), 1) for c in (t, 2) for z in zs]
+        + [(ratio, 0), (ratio, 1)]
+    )
+    hi = (
+        [(h0[c][z], -1) for c in (t, 2) for z in zs]
+        + [(h1[c][z], -1) for c in (t, 2) for z in zs]
+        + [((ratio, fwd[1][c][z]), -1) for c in (t, nrm, 2) for z in zs]
+        + [(ratio, -1)]
+    )
+    return lo, hi
+
+
+def pack_columns(grad, lo, hi):
+    n, m = grad.shape
     lane = iota((n, 128), 1)
-    lo, hi = lists(0, 1)
     first, last = grad[:, 0:128], grad[:, m - 128 : m]
     pack = jnp.where(lane < FILT, first, 0.0)
     moved = pltpu.roll(last, LANE_HI + FILT, 1)
@@ -268,18 +252,83 @@
     for group, start in ((lo, FILT), (hi, LANE_HI + FILT)):
         for k, (item, at) in enumerate(group):
             pack = jnp.where(lane == start + k, pltpu.roll(tile(item, at), (start + k - at) % 128, 1), pack)
-    pack_ref[...] = pack
-
-    def corner(rows):
-        low = jnp.concatenate([rows[0:8], rows[8:16]], axis=1)
-        high = jnp.concatenate([rows[16:24], jnp.zeros((8, m - 128), F32)], axis=1)
+    return pack
+
+
+def edge_kernel(e_hbm, h_hbm, f_hbm, lab_hbm, den_hbm, eps_hbm,
+                a_ref, b_ref, lo_ref, hi_ref,
+                e_ref, h_ref, f_ref, lab_ref, den_ref, tab_ref, sems):
+    n, m = lab_hbm.shape
+    copies = []
+
+    def fetch(src, dst, lead):
+        for at, start in ((0, 0), (EXT, n - EXT)):
+            index = (*lead, pl.ds(start, EXT))
+            copy = pltpu.make_async_copy(src.at[index], dst.at[(*lead, pl.ds(at, EXT))], sems.at[len(copies) - 1])
+            copy.start()
+            copies.append(copy)
+
+    every = slice(None)
+    table = pltpu.make_async_copy(eps_hbm, tab_ref, sems.at[12])
+    table.start()
+    copies.append(table)
+    fetch(lab_hbm, lab_ref, ())
+    fetch(den_hbm, den_ref, ())
+    fetch(h_hbm, h_ref, (every, every))
+    fetch(e_hbm, e_ref, (every, every))
+    for step in range(STEPS):
+        fetch(f_hbm, f_ref, (step, every, every))
+    for copy in copies[:9]:
+        copy.wait()
+    ratio = ratio_of(lab_ref[...], den_ref[...], tab_ref)
+    h0 = planes(h_ref)
+
+    def saved(step):
+        for copy in copies[9 + 2 * step : 11 + 2 * step]:
+            copy.wait()
+        return planes(f_ref, step)
+
+    e1, h1, e2, grad, fwd = local_solve(planes(e_ref), h0, saved, ratio)
+    rows = 2 * EXT
+
+    def line(item, at):
+        if isinstance(item, tuple):
+            return line(item[0], at) * line(item[1], at)
+        at = at % rows
+        return item[at : at + 1]
+
+    lo, hi = edge_lists(1, 0, e1, h0, h1, e2, fwd, ratio)
+    lo_ref[0:FILT] = grad[0:FILT]
+    for k, (item, at) in enumerate(lo):
+        lo_ref[FILT + k : FILT + k + 1] = line(item, at)
+    hi_ref[0:FILT] = grad[rows - FILT : rows]
+    for k, (item, at) in enumerate(hi):
+        hi_ref[FILT + k : FILT + k + 1] = line(item, at)
+    hi_ref[HI_ROWS - 1 : HI_ROWS] = jnp.zeros((1, m), F32)
+    pack = pack_columns(grad, *edge_lists(0, 1, e1, h0, h1, e2, fwd, ratio))
+
+    def corner(part):
+        low = jnp.concatenate([part[0:8], part[8:16]], axis=1)
+        high = jnp.concatenate([part[16:24], jnp.zeros((8, m - 128), F32)], axis=1)
         return jnp.concatenate([low, high], axis=0)
 
     lo_all = jnp.concatenate([lo_ref[...], corner(pack[0:EXT])], axis=0)
-    hi_all = jnp.concatenate([hi_ref[...], jnp.zeros((LO_ROWS - HI_ROWS, m), F32), corner(pack[n - EXT : n])], axis=0)
+    hi_all = jnp.concatenate([hi_ref[...], jnp.zeros((LO_ROWS - HI_ROWS, m), F32), corner(pack[EXT:rows])], axis=0)
     first_even = even("gx")
     a_ref[...] = jnp.where(first_even, hi_all, lo_all)
     b_ref[...] = jnp.where(first_even, lo_all, hi_all)
+
+
+def solve_kernel(e_ref, h_ref, f_ref, lab_ref, den_ref, eps_ref, pack_ref, grad_ref, e2_ref, h1_ref):
+    ratio = ratio_of(lab_ref[...], den_ref[...], eps_ref)
+    h0 = planes(h_ref)
+    e1, h1, e2, grad, fwd = local_solve(planes(e_ref), h0, lambda step: planes(f_ref, step), ratio)
+    for c in range(3):
+        for z in range(e_ref.shape[1]):
+            e2_ref[c, z] = e2[c][z]
+            h1_ref[c, z] = h1[c][z]
+    grad_ref[...] = grad
+    pack_ref[...] = pack_columns(grad, *edge_lists(0, 1, e1, h0, h1, e2, fwd, ratio))
 
 
 def x_kernel(ra_ref, rb_ref, lo_ref, hi_ref, pack_ref, grad_ref,
@@ -370,7 +419,13 @@
     b_ref[...] = jnp.where(y_even, lo, hi_part)
 
 
-def inner_kernel(ext_ref, out_ref):
+def inner_kernel(ext_ref, e2_ref, h1_ref, out_ref, h2_ref):
+    nz = e2_ref.shape[1]
+    _, magnetic = updates(*out_ref.shape, nz)
+    h2 = magnetic(planes(e2_ref), planes(h1_ref))
+    for c in range(3):
+        for z in range(nz):
+            h2_ref[c, z] = h2[c][z]
     rows, m = ext_ref.shape
     n = out_ref.shape[0]
     d = iota((n, rows), 1) - iota((n, rows), 0)
@@ -439,39 +494,52 @@
     return [(i, (i - 1) % count if i % 2 == 0 else (i + 1) % count) for i in range(count)]
 
 
-def call(kernel, shapes, ins, scratch=()):
+def call(kernel, shapes, ins, scratch=(), far=(), sems=0):
     vmem = pl.BlockSpec(memory_space=pltpu.VMEM)
+    hbm = pl.BlockSpec(memory_space=pltpu.HBM)
+    smem = pl.BlockSpec(memory_space=pltpu.SMEM)
+    ins = [pltpu.with_memory_space_constraint(x, pltpu.HBM) if k in far else x for k, x in enumerate(ins)]
+    scratches = [s if hasattr(s, "dtype") else pltpu.VMEM(s, F32) for s in scratch]
+    if sems:
+        scratches.append(pltpu.SemaphoreType.DMA((sems,)))
     return pl.pallas_call(
         kernel,
         out_shape=[jax.ShapeDtypeStruct(s, F32) for s in shapes],
-        in_specs=[pl.BlockSpec(memory_space=pltpu.SMEM) if x.shape == (NMAT,) else vmem for x in ins],
+        in_specs=[hbm if k in far else smem if x.shape == (NMAT,) else vmem for k, x in enumerate(ins)],
         out_specs=[vmem] * len(shapes),
-        scratch_shapes=[pltpu.VMEM(s, F32) for s in scratch],
-        compiler_params=pltpu.CompilerParams(vmem_limit_bytes=40 * 1024 * 1024),
+        scratch_shapes=scratches,
+        compiler_params=pltpu.CompilerParams(vmem_limit_bytes=24 * 1024 * 1024),
     )(*ins)
 
 
 def body(adj_e, adj_h, fwd_e, labels, eps_table, density):
     n, m = labels.shape
     block = adj_e.shape
+    nz = block[1]
+    ins = [adj_e, adj_h, fwd_e, labels, density, eps_table]
     message = (LO_ROWS + 16, m)
-    xa, xb, lo, hi, pack, grad, e2, h2 = call(
-        solve_kernel,
-        [message, message, (LO_ROWS, m), (HI_ROWS, m), (n, 128), (n, m), block, block],
-        [adj_e, adj_h, fwd_e, labels, density, eps_table],
+    strip = (2 * EXT, m)
+    xa, xb, lo, hi = call(
+        edge_kernel,
+        [message, message, (LO_ROWS, m), (HI_ROWS, m)],
+        ins,
+        [(3, nz, *strip), (3, nz, *strip), (STEPS, 3, nz, *strip), pltpu.VMEM(strip, jnp.int32), strip, pltpu.SMEM((NMAT,), F32)],
+        range(6),
+        13,
     )
     gx, gy = lax.axis_size("gx"), lax.axis_size("gy")
     got_a = lax.ppermute(xa, "gx", swap_pairs(gx, 0))
     got_b = lax.ppermute(xb, "gx", swap_pairs(gx, 1))
+    pack, grad, e2, h1 = call(solve_kernel, [(n, 128), (n, m), block, block], ins)
     column = (LO_ROWS, 2 * n)
     ya, yb, ylo, yhi, ext, dr = call(
         x_kernel,
         [column, column, column, column, (2 * n, m), (48, m)],
         [got_a, got_b, lo, hi, pack, grad],
     )
+    got_b = lax.ppermute(yb, "gy", swap_pairs(gy, 1))
     got_a = lax.ppermute(ya, "gy", swap_pairs(gy, 0))
-    got_b = lax.ppermute(yb, "gy", swap_pairs(gy, 1))
-    (inner,) = call(inner_kernel, [(n, m)], [ext])
+    inner, h2 = call(inner_kernel, [(n, m), block], [ext, e2, h1])
     return tuple(
         call(
             y_kernel,

time: 24.2 us -> 18.1 us (0.75)
  local copies, waits for them, and re-layouts: 6.13 us -> 0.03 us
  waiting for transfers between devices: 4.79 us -> 2.54 us
  Pallas kernels: 5.23 us -> 7.38 us
    unnamed x12, local copies, waits for them, and re-layouts: 6.13 us -> 0.03 us
    ppermute x1, waiting for transfers between devices: 2.19 us -> 0.01 us  [body(): got_b = lax.ppermute(xb, 'gx', swap_pairs(gx, 1))]
    pallas_call x4 -> x5, Pallas kernels: 5.23 us -> 7.38 us  [call(): pl.pallas_call(kernel, out_shape=[jax.ShapeDtypeStruct(s, F32) for s in s...]
  transfers between devices with their start and end apart: 4 -> 4, of which waited for: 2 -> 1; matrix products, arithmetic and copies ran while one was open for 0% -> 0% of each run, Pallas kernels for 3% -> 17%
where the time goes in v2:
time: 18.1 us; the launch traced here: 17.9 us
  Pallas kernels  7.38 us (41%)
  starting transfers between devices  7.25 us (40%)
  waiting for transfers between devices  2.54 us (14%)
  between operations  0.75 us (4%)
    pallas_call x5, Pallas kernels, call(): pl.pallas_call(kernel, out_shape=[jax.ShapeDtypeStruct(s, F32) for s in s...  7.38 us
    ppermute x1, starting transfers between devices, body(): got_b = lax.ppermute(xb, 'gx', swap_pairs(gx, 1))  2.61 us
    ppermute x1, waiting for transfers between devices, body(): got_b = lax.ppermute(yb, 'gy', swap_pairs(gy, 1))  2.53 us
    ppermute x1, starting transfers between devices, body(): got_b = lax.ppermute(yb, 'gy', swap_pairs(gy, 1))  2.47 us
    ppermute x1, starting transfers between devices, body(): got_a = lax.ppermute(ya, 'gy', swap_pairs(gy, 0))  1.64 us
    ppermute x1, starting transfers between devices, body(): got_a = lax.ppermute(xa, 'gx', swap_pairs(gx, 0))  0.52 us
  transfers between devices with their start and end apart: 4, of which 1 were waited for; matrix products, arithmetic and copies ran while one was open for 0% of the time, Pallas kernels for 17%

profile of v2, /device:TPU:0, one launch (start us, length us, event | category | flops | bytes accessed | tf_op | source)
XLA Modules:
  0.0 17.9 jit_solution(6284661144703619728)
XLA Ops:
  0.6 0.0 copy-start.4
  0.6 0.0 copy-start.5
  0.7 0.0 copy-start.3
  0.7 0.0 copy-start
  0.7 0.0 copy-start.2
  0.7 0.0 copy-start.1
  0.7 2.2 %shard_map.85 = (f32[56,256]{1,0:T(8,128)S(1)}, f32[56,256]{1,0:T(8,128)S(1)}, f32[40,256]{1,0:T(8,128)S(1)}, f32[32,256]{1,0:T(8,128)S(1)}) custom-call(f32[3,2,128,256]{3,2,1,0:T(8,128)} %e_ref.1, f32[3,2,128,256]{3,2,1,0:T(8,128)} %h_ref.1, f32[2,3,2,128,256]{4,3,2,1,0:T(8,128)} %f_ref.1, s32[128,256]{1,0:T(8,128)} %lab_ref.1, f32[128,256]{1,0:T(8,128)} %den_ref.1, ...), custom_call_target="tpu_custom_call" | custom-call | tf_op jit(solution)/shard_map/pallas_call | solution.py:505
  2.9 0.5 %collective-permute-start = (f32[56,256]{1,0:T(8,128)S(1)}, f32[56,256]{1,0:T(8,128)S(1)}, u32[]{:S(2)}, u32[]{:S(2)}) collective-permute-start(f32[56,256]{1,0:T(8,128)S(1)} %get-tuple-element.19), channel_id=1, source_target_pairs={{0,4},{4,0},{8,12},{12,8},{1,5},{5,1},{9,13},{13,9},{2,6},{6,2},{1... | collective-permute-start | bytes 172040 | tf_op jit(solution)/shard_map/ppermute | solution.py:531
  3.4 2.6 %collective-permute-start.1 = (f32[56,256]{1,0:T(8,128)S(1)}, f32[56,256]{1,0:T(8,128)S(1)}, u32[]{:S(2)}, u32[]{:S(2)}) collective-permute-start(f32[56,256]{1,0:T(8,128)S(1)} %get-tuple-element.20), channel_id=1, source_target_pairs={{0,12},{4,8},{8,4},{12,0},{1,13},{5,9},{9,5},{13,1},{2,14},{6,10},... | collective-permute-start | bytes 172040 | tf_op jit(solution)/shard_map/ppermute | solution.py:532
  6.0 0.0 copy-done.4
  6.0 0.0 copy-done.5
  6.0 0.0 copy-done.3
  6.0 0.0 copy-done
  6.0 0.0 copy-done.2
  6.0 0.0 copy-done.1
  6.0 2.3 %shard_map.86 = (f32[128,128]{1,0:T(8,128)S(1)}, f32[128,256]{1,0:T(8,128)S(1)}, f32[3,2,128,256]{3,2,1,0:T(8,128)S(1)}, f32[3,2,128,256]{3,2,1,0:T(8,128)S(1)}) custom-call(f32[3,2,128,256]{3,2,1,0:T(8,128)S(1)} %copy-done.1, f32[3,2,128,256]{3,2,1,0:T(8,128)S(1)} %copy-done.2, f32[2,3,2,128,256]{4,3,2,1,0:T(8,128)S(1)} %copy-done, ...), custom_call_target="tpu_custom_call" | custom-call | tf_op jit(solution)/shard_map/pallas_call | solution.py:505
  8.3 0.0 collective-permute-done.ra_ref
  8.4 0.0 collective-permute-done.1.rb_ref
  8.4 0.4 %shard_map.87 = (f32[40,256]{1,0:T(8,128)S(1)}, f32[40,256]{1,0:T(8,128)S(1)}, f32[40,256]{1,0:T(8,128)S(1)}, f32[40,256]{1,0:T(8,128)S(1)}, f32[256,256]{1,0:T(8,128)S(1)}, /*index=5*/f32[48,256]{1,0:T(8,128)S(1)}) custom-call(f32[56,256]{1,0:T(8,128)S(1)} %collective-permute-done.ra_ref, f32[56,256]{1,0:T(8,128)S(1)} %collective-permute-done.1.rb_ref, ...), custom_call_target="tpu_custom_call" | custom-call | tf_op jit(solution)/shard_map/pallas_call | solution.py:505
  8.7 1.6 %collective-permute-start.2 = (f32[40,256]{1,0:T(8,128)S(1)}, f32[40,256]{1,0:T(8,128)S(1)}, u32[]{:S(2)}, u32[]{:S(2)}) collective-permute-start(f32[40,256]{1,0:T(8,128)S(1)} %get-tuple-element.25), channel_id=1, source_target_pairs={{0,1},{1,0},{2,3},{3,2},{4,5},{5,4},{6,7},{7,6},{8,9},{9,8},{10,11... | collective-permute-start | bytes 122888 | tf_op jit(solution)/shard_map/ppermute | solution.py:541
  10.4 2.5 %collective-permute-start.3 = (f32[40,256]{1,0:T(8,128)S(1)}, f32[40,256]{1,0:T(8,128)S(1)}, u32[]{:S(2)}, u32[]{:S(2)}) collective-permute-start(f32[40,256]{1,0:T(8,128)S(1)} %get-tuple-element.26), channel_id=1, source_target_pairs={{0,3},{1,2},{2,1},{3,0},{4,7},{5,6},{6,5},{7,4},{8,11},{9,10},{10,... | collective-permute-start | bytes 122888 | tf_op jit(solution)/shard_map/ppermute | solution.py:540
  12.9 0.8 %shard_map.88 = (f32[128,256]{1,0:T(8,128)S(1)}, f32[3,2,128,256]{3,2,1,0:T(8,128)S(1)}) custom-call(f32[256,256]{1,0:T(8,128)S(1)} %get-tuple-element.31.ext_ref, f32[3,2,128,256]{3,2,1,0:T(8,128)S(1)} %get-tuple-element.30.e2_ref, f32[3,2,128,256]{3,2,1,0:T(8,128)S(1)} %get-tuple-element.32.h1_ref), custom_call_target="tpu_custom_call" | custom-call | tf_op jit(solution)/shard_map/pallas_call | solution.py:505
  13.6 0.0 collective-permute-done.2.ra_ref
  13.6 2.5 %collective-permute-done.3.rb_ref = f32[40,256]{1,0:T(8,128)S(1)} collective-permute-done((f32[40,256]{1,0:T(8,128)S(1)}, f32[40,256]{1,0:T(8,128)S(1)}, u32[]{:S(2)}, u32[]{:S(2)}) %collective-permute-start.3) | collective-permute-done | bytes 40992 | tf_op jit(solution)/shard_map/ppermute | solution.py:540
  16.2 1.8 %shard_map.89 = (f32[3,2,128,256]{3,2,1,0:T(8,128)}, f32[3,2,128,256]{3,2,1,0:T(8,128)}, f32[128,256]{1,0:T(8,128)}) custom-call(f32[40,256]{1,0:T(8,128)S(1)} %collective-permute-done.2.ra_ref, f32[40,256]{1,0:T(8,128)S(1)} %collective-permute-done.3.rb_ref, f32[40,256]{1,0:T(8,128)S(1)} %get-tuple-element.27.lo_ref, ...), custom_call_target="tpu_custom_call" | custom-call | tf_op jit(solution)/shard_map/pallas_call | solution.py:505
Async XLA Ops:
  0.6 5.4 %copy-start.4 = (f32[128,256]{1,0:T(8,128)S(1)}, f32[128,256]{1,0:T(8,128)}, u32[]{:S(2)}) copy-start(f32[128,256]{1,0:T(8,128)} %den_ref.1) | copy-start | bytes 393220
  0.6 5.4 %copy-start.5 = (f32[8]{0:T(128)S(1)}, f32[8]{0:T(128)}, u32[]{:S(2)}) copy-start(f32[8]{0:T(128)} %eps_ref.1) | copy-start | bytes 100
  0.7 5.4 %copy-start.3 = (s32[128,256]{1,0:T(8,128)S(1)}, s32[128,256]{1,0:T(8,128)}, u32[]{:S(2)}) copy-start(s32[128,256]{1,0:T(8,128)} %lab_ref.1) | copy-start | bytes 393220
  0.7 5.4 %copy-start = (f32[2,3,2,128,256]{4,3,2,1,0:T(8,128)S(1)}, f32[2,3,2,128,256]{4,3,2,1,0:T(8,128)}, u32[]{:S(2)}) copy-start(f32[2,3,2,128,256]{4,3,2,1,0:T(8,128)} %f_ref.1) | copy-start | bytes 4718596
  0.7 5.4 %copy-start.2 = (f32[3,2,128,256]{3,2,1,0:T(8,128)S(1)}, f32[3,2,128,256]{3,2,1,0:T(8,128)}, u32[]{:S(2)}) copy-start(f32[3,2,128,256]{3,2,1,0:T(8,128)} %h_ref.1) | copy-start | bytes 2359300
  0.7 5.4 %copy-start.1 = (f32[3,2,128,256]{3,2,1,0:T(8,128)S(1)}, f32[3,2,128,256]{3,2,1,0:T(8,128)}, u32[]{:S(2)}) copy-start(f32[3,2,128,256]{3,2,1,0:T(8,128)} %e_ref.1) | copy-start | bytes 2359300
  2.9 5.5 %collective-permute-start = (f32[56,256]{1,0:T(8,128)S(1)}, f32[56,256]{1,0:T(8,128)S(1)}, u32[]{:S(2)}, u32[]{:S(2)}) collective-permute-start(f32[56,256]{1,0:T(8,128)S(1)} %get-tuple-element.19), channel_id=1, source_target_pairs={{0,4},{4,0},{8,12},{12,8},{1,5},{5,1},{9,13},{13,9},{2,6},{6,2},{1... | collective-permute-start | bytes 172040 | tf_op jit(solution)/shard_map/ppermute | solution.py:531
  3.4 5.0 %collective-permute-start.1 = (f32[56,256]{1,0:T(8,128)S(1)}, f32[56,256]{1,0:T(8,128)S(1)}, u32[]{:S(2)}, u32[]{:S(2)}) collective-permute-start(f32[56,256]{1,0:T(8,128)S(1)} %get-tuple-element.20), channel_id=1, source_target_pairs={{0,12},{4,8},{8,4},{12,0},{1,13},{5,9},{9,5},{13,1},{2,14},{6,10},... | collective-permute-start | bytes 172040 | tf_op jit(solution)/shard_map/ppermute | solution.py:532
  8.7 4.9 %collective-permute-start.2 = (f32[40,256]{1,0:T(8,128)S(1)}, f32[40,256]{1,0:T(8,128)S(1)}, u32[]{:S(2)}, u32[]{:S(2)}) collective-permute-start(f32[40,256]{1,0:T(8,128)S(1)} %get-tuple-element.25), channel_id=1, source_target_pairs={{0,1},{1,0},{2,3},{3,2},{4,5},{5,4},{6,7},{7,6},{8,9},{9,8},{10,11... | collective-permute-start | bytes 122888 | tf_op jit(solution)/shard_map/ppermute | solution.py:541
  10.4 5.8 %collective-permute-start.3 = (f32[40,256]{1,0:T(8,128)S(1)}, f32[40,256]{1,0:T(8,128)S(1)}, u32[]{:S(2)}, u32[]{:S(2)}) collective-permute-start(f32[40,256]{1,0:T(8,128)S(1)} %get-tuple-element.26), channel_id=1, source_target_pairs={{0,3},{1,2},{2,1},{3,0},{4,7},{5,6},{6,5},{7,4},{8,11},{9,10},{10,... | collective-permute-start | bytes 122888 | tf_op jit(solution)/shard_map/ppermute | solution.py:540

commit v3 on v2

--- a/solution.py
+++ b/solution.py
@@ -332,7 +332,7 @@
 
 
 def x_kernel(ra_ref, rb_ref, lo_ref, hi_ref, pack_ref, grad_ref,
-             a_ref, b_ref, ylo_ref, yhi_ref, ext_ref, dr_ref):
+             yhi_ref, ylo_ref, ext_ref, dr_ref):
     n, m = grad_ref.shape
     first_even = even("gx")
     right = jnp.where(first_even, ra_ref[...], rb_ref[...])
@@ -414,9 +414,6 @@
     lo, hi_part = packed[0:LO_ROWS], packed[LANE_HI : LANE_HI + LO_ROWS]
     ylo_ref[...] = lo
     yhi_ref[...] = hi_part
-    y_even = even("gy")
-    a_ref[...] = jnp.where(y_even, hi_part, lo)
-    b_ref[...] = jnp.where(y_even, lo, hi_part)
 
 
 def inner_kernel(ext_ref, e2_ref, h1_ref, out_ref, h2_ref):
@@ -435,12 +432,10 @@
     out_ref[...] = jnp.dot(along, tap(e), precision=HIGHEST, preferred_element_type=F32)
 
 
-def y_kernel(ra_ref, rb_ref, lo_ref, hi_ref, dr_ref, e2_ref, h2_ref, inner_ref,
+def y_kernel(left_ref, right_ref, lo_ref, hi_ref, dr_ref, e2_ref, h2_ref, inner_ref,
              e_ref, h_ref, out_ref, gt_ref, dc_ref):
     n, m = inner_ref.shape
-    y_even = even("gy")
-    right = jnp.where(y_even, ra_ref[...], rb_ref[...])
-    left = jnp.where(y_even, rb_ref[...], ra_ref[...])
+    right, left = right_ref[...], left_ref[...]
     rows = right.shape[1]
     a, b = seam_inputs(left, hi_ref[...], lo_ref[...], right)
     d = seam(1.0, a, b, lambda f: pltpu.roll(f, rows - 1, 1), lambda f: pltpu.roll(f, 1, 1))
@@ -532,19 +527,19 @@
     got_b = lax.ppermute(xb, "gx", swap_pairs(gx, 1))
     pack, grad, e2, h1 = call(solve_kernel, [(n, 128), (n, m), block, block], ins)
     column = (LO_ROWS, 2 * n)
-    ya, yb, ylo, yhi, ext, dr = call(
+    yhi, ylo, ext, dr = call(
         x_kernel,
-        [column, column, column, column, (2 * n, m), (48, m)],
+        [column, column, (2 * n, m), (48, m)],
         [got_a, got_b, lo, hi, pack, grad],
     )
-    got_b = lax.ppermute(yb, "gy", swap_pairs(gy, 1))
-    got_a = lax.ppermute(ya, "gy", swap_pairs(gy, 0))
+    left = lax.ppermute(yhi, "gy", [(i, (i + 1) % gy) for i in range(gy)])
+    right = lax.ppermute(ylo, "gy", [(i, (i - 1) % gy) for i in range(gy)])
     inner, h2 = call(inner_kernel, [(n, m), block], [ext, e2, h1])
     return tuple(
         call(
             y_kernel,
             [block, block, (n, m)],
-            [got_a, got_b, ylo, yhi, dr, e2, h2, inner],
+            [left, right, ylo, yhi, dr, e2, h2, inner],
             [(40, 2 * n), (128, n)],
         )
     )

time: 18.1 us -> 16.7 us (0.923)
  waiting for transfers between devices: 2.54 us -> 1.42 us
  starting transfers between devices: 7.25 us -> 7.01 us
    ppermute x2, waiting for transfers between devices: 2.54 us -> 1.41 us  [the longest x1 1.35 us: body(): left = lax.ppermute(yhi, 'gy', [(i, (i + 1) % gy) for i in range(gy)])]
    ppermute x2, starting transfers between devices: 4.12 us -> 3.88 us  [the longest x1 2.25 us: body(): right = lax.ppermute(ylo, 'gy', [(i, (i - 1) % gy) for i in range(gy)])]
  transfers between devices with their start and end apart: 4 -> 4, of which waited for: 1 -> 2; matrix products, arithmetic and copies ran while one was open for 0% -> 0% of each run, Pallas kernels for 17% -> 19%
where the time goes in v3:
time: 16.7 us; the launch traced here: 16.6 us
  Pallas kernels  7.37 us (44%)
  starting transfers between devices  7.01 us (42%)
  waiting for transfers between devices  1.42 us (9%)
  between operations  0.74 us (4%)
    pallas_call x5, Pallas kernels, call(): pl.pallas_call(kernel, out_shape=[jax.ShapeDtypeStruct(s, F32) for s in s...  7.37 us
    ppermute x1, starting transfers between devices, body(): got_b = lax.ppermute(xb, 'gx', swap_pairs(gx, 1))  2.61 us
    ppermute x1, starting transfers between devices, body(): right = lax.ppermute(ylo, 'gy', [(i, (i - 1) % gy) for i in range(gy)])  2.25 us
    ppermute x1, starting transfers between devices, body(): left = lax.ppermute(yhi, 'gy', [(i, (i + 1) % gy) for i in range(gy)])  1.63 us
    ppermute x1, waiting for transfers between devices, body(): left = lax.ppermute(yhi, 'gy', [(i, (i + 1) % gy) for i in range(gy)])  1.35 us
    ppermute x1, starting transfers between devices, body(): got_a = lax.ppermute(xa, 'gx', swap_pairs(gx, 0))  0.52 us
  transfers between devices with their start and end apart: 4, of which 2 were waited for; matrix products, arithmetic and copies ran while one was open for 0% of the time, Pallas kernels for 19%

profile of v3, /device:TPU:0, one launch (start us, length us, event | category | flops | bytes accessed | tf_op | source)
XLA Modules:
  0.0 16.6 jit_solution(794962618365175804)
XLA Ops:
  0.6 0.0 copy-start.4
  0.6 0.0 copy-start.5
  0.7 0.0 copy-start.3
  0.7 0.0 copy-start
  0.7 0.0 copy-start.2
  0.7 0.0 copy-start.1
  0.7 2.2 %shard_map.85 = (f32[56,256]{1,0:T(8,128)S(1)}, f32[56,256]{1,0:T(8,128)S(1)}, f32[40,256]{1,0:T(8,128)S(1)}, f32[32,256]{1,0:T(8,128)S(1)}) custom-call(f32[3,2,128,256]{3,2,1,0:T(8,128)} %e_ref.1, f32[3,2,128,256]{3,2,1,0:T(8,128)} %h_ref.1, f32[2,3,2,128,256]{4,3,2,1,0:T(8,128)} %f_ref.1, s32[128,256]{1,0:T(8,128)} %lab_ref.1, f32[128,256]{1,0:T(8,128)} %den_ref.1, ...), custom_call_target="tpu_custom_call" | custom-call | tf_op jit(solution)/shard_map/pallas_call | solution.py:500
  2.9 0.5 %collective-permute-start = (f32[56,256]{1,0:T(8,128)S(1)}, f32[56,256]{1,0:T(8,128)S(1)}, u32[]{:S(2)}, u32[]{:S(2)}) collective-permute-start(f32[56,256]{1,0:T(8,128)S(1)} %get-tuple-element.17), channel_id=1, source_target_pairs={{0,4},{4,0},{8,12},{12,8},{1,5},{5,1},{9,13},{13,9},{2,6},{6,2},{1... | collective-permute-start | bytes 172040 | tf_op jit(solution)/shard_map/ppermute | solution.py:526
  3.4 2.6 %collective-permute-start.1 = (f32[56,256]{1,0:T(8,128)S(1)}, f32[56,256]{1,0:T(8,128)S(1)}, u32[]{:S(2)}, u32[]{:S(2)}) collective-permute-start(f32[56,256]{1,0:T(8,128)S(1)} %get-tuple-element.18), channel_id=1, source_target_pairs={{0,12},{4,8},{8,4},{12,0},{1,13},{5,9},{9,5},{13,1},{2,14},{6,10},... | collective-permute-start | bytes 172040 | tf_op jit(solution)/shard_map/ppermute | solution.py:527
  6.0 0.0 copy-done.4
  6.0 0.0 copy-done.5
  6.0 0.0 copy-done.3
  6.0 0.0 copy-done
  6.0 0.0 copy-done.2
  6.0 0.0 copy-done.1
  6.0 2.3 %shard_map.86 = (f32[128,128]{1,0:T(8,128)S(1)}, f32[128,256]{1,0:T(8,128)S(1)}, f32[3,2,128,256]{3,2,1,0:T(8,128)S(1)}, f32[3,2,128,256]{3,2,1,0:T(8,128)S(1)}) custom-call(f32[3,2,128,256]{3,2,1,0:T(8,128)S(1)} %copy-done.1, f32[3,2,128,256]{3,2,1,0:T(8,128)S(1)} %copy-done.2, f32[2,3,2,128,256]{4,3,2,1,0:T(8,128)S(1)} %copy-done, ...), custom_call_target="tpu_custom_call" | custom-call | tf_op jit(solution)/shard_map/pallas_call | solution.py:500
  8.3 0.0 collective-permute-done.ra_ref
  8.4 0.0 collective-permute-done.1.rb_ref
  8.4 0.4 %shard_map.87 = (f32[40,256]{1,0:T(8,128)S(1)}, f32[40,256]{1,0:T(8,128)S(1)}, f32[256,256]{1,0:T(8,128)S(1)}, f32[48,256]{1,0:T(8,128)S(1)}) custom-call(f32[56,256]{1,0:T(8,128)S(1)} %collective-permute-done.ra_ref, f32[56,256]{1,0:T(8,128)S(1)} %collective-permute-done.1.rb_ref, f32[40,256]{1,0:T(8,128)S(1)} %get-tuple-element.19.lo_ref, ...), custom_call_target="tpu_custom_call" | custom-call | tf_op jit(solution)/shard_map/pallas_call | solution.py:500
  8.7 1.6 %collective-permute-start.2 = (f32[40,256]{1,0:T(8,128)S(1)}, f32[40,256]{1,0:T(8,128)S(1)}, u32[]{:S(2)}, u32[]{:S(2)}) collective-permute-start(f32[40,256]{1,0:T(8,128)S(1)} %get-tuple-element.23.hi_ref), channel_id=1, source_target_pairs={{0,1},{1,2},{2,3},{3,0},{4,5},{5,6},{6,7},{7,4},{8,9},{9,10},{10,1... | collective-permute-start | bytes 122888 | tf_op jit(solution)/shard_map/ppermute | solution.py:535
  10.4 2.2 %collective-permute-start.3 = (f32[40,256]{1,0:T(8,128)S(1)}, f32[40,256]{1,0:T(8,128)S(1)}, u32[]{:S(2)}, u32[]{:S(2)}) collective-permute-start(f32[40,256]{1,0:T(8,128)S(1)} %get-tuple-element.24.lo_ref), channel_id=1, source_target_pairs={{0,3},{1,0},{2,1},{3,2},{4,7},{5,4},{6,5},{7,6},{8,11},{9,8},{10,9... | collective-permute-start | bytes 122888 | tf_op jit(solution)/shard_map/ppermute | solution.py:536
  12.6 0.8 %shard_map.88 = (f32[128,256]{1,0:T(8,128)S(1)}, f32[3,2,128,256]{3,2,1,0:T(8,128)S(1)}) custom-call(f32[256,256]{1,0:T(8,128)S(1)} %get-tuple-element.27.ext_ref, f32[3,2,128,256]{3,2,1,0:T(8,128)S(1)} %get-tuple-element.26.e2_ref, f32[3,2,128,256]{3,2,1,0:T(8,128)S(1)} %get-tuple-element.28.h1_ref), custom_call_target="tpu_custom_call" | custom-call | tf_op jit(solution)/shard_map/pallas_call | solution.py:500
  13.4 1.3 %collective-permute-done.2.left_ref = f32[40,256]{1,0:T(8,128)S(1)} collective-permute-done((f32[40,256]{1,0:T(8,128)S(1)}, f32[40,256]{1,0:T(8,128)S(1)}, u32[]{:S(2)}, u32[]{:S(2)}) %collective-permute-start.2) | collective-permute-done | bytes 40992 | tf_op jit(solution)/shard_map/ppermute | solution.py:535
  14.7 0.1 collective-permute-done.3.right_ref
  14.8 1.8 %shard_map.89 = (f32[3,2,128,256]{3,2,1,0:T(8,128)}, f32[3,2,128,256]{3,2,1,0:T(8,128)}, f32[128,256]{1,0:T(8,128)}) custom-call(f32[40,256]{1,0:T(8,128)S(1)} %collective-permute-done.2.left_ref, f32[40,256]{1,0:T(8,128)S(1)} %collective-permute-done.3.right_ref, f32[40,256]{1,0:T(8,128)S(1)} %get-tuple-element.24.lo_ref, ...), custom_call_target="tpu_custom_call" | custom-call | tf_op jit(solution)/shard_map/pallas_call | solution.py:500
Async XLA Ops:
  0.6 5.4 %copy-start.4 = (f32[128,256]{1,0:T(8,128)S(1)}, f32[128,256]{1,0:T(8,128)}, u32[]{:S(2)}) copy-start(f32[128,256]{1,0:T(8,128)} %den_ref.1) | copy-start | bytes 393220
  0.6 5.4 %copy-start.5 = (f32[8]{0:T(128)S(1)}, f32[8]{0:T(128)}, u32[]{:S(2)}) copy-start(f32[8]{0:T(128)} %eps_ref.1) | copy-start | bytes 100
  0.7 5.4 %copy-start.3 = (s32[128,256]{1,0:T(8,128)S(1)}, s32[128,256]{1,0:T(8,128)}, u32[]{:S(2)}) copy-start(s32[128,256]{1,0:T(8,128)} %lab_ref.1) | copy-start | bytes 393220
  0.7 5.4 %copy-start = (f32[2,3,2,128,256]{4,3,2,1,0:T(8,128)S(1)}, f32[2,3,2,128,256]{4,3,2,1,0:T(8,128)}, u32[]{:S(2)}) copy-start(f32[2,3,2,128,256]{4,3,2,1,0:T(8,128)} %f_ref.1) | copy-start | bytes 4718596
  0.7 5.4 %copy-start.2 = (f32[3,2,128,256]{3,2,1,0:T(8,128)S(1)}, f32[3,2,128,256]{3,2,1,0:T(8,128)}, u32[]{:S(2)}) copy-start(f32[3,2,128,256]{3,2,1,0:T(8,128)} %h_ref.1) | copy-start | bytes 2359300
  0.7 5.4 %copy-start.1 = (f32[3,2,128,256]{3,2,1,0:T(8,128)S(1)}, f32[3,2,128,256]{3,2,1,0:T(8,128)}, u32[]{:S(2)}) copy-start(f32[3,2,128,256]{3,2,1,0:T(8,128)} %e_ref.1) | copy-start | bytes 2359300
  2.9 5.5 %collective-permute-start = (f32[56,256]{1,0:T(8,128)S(1)}, f32[56,256]{1,0:T(8,128)S(1)}, u32[]{:S(2)}, u32[]{:S(2)}) collective-permute-start(f32[56,256]{1,0:T(8,128)S(1)} %get-tuple-element.17), channel_id=1, source_target_pairs={{0,4},{4,0},{8,12},{12,8},{1,5},{5,1},{9,13},{13,9},{2,6},{6,2},{1... | collective-permute-start | bytes 172040 | tf_op jit(solution)/shard_map/ppermute | solution.py:526
  3.4 5.0 %collective-permute-start.1 = (f32[56,256]{1,0:T(8,128)S(1)}, f32[56,256]{1,0:T(8,128)S(1)}, u32[]{:S(2)}, u32[]{:S(2)}) collective-permute-start(f32[56,256]{1,0:T(8,128)S(1)} %get-tuple-element.18), channel_id=1, source_target_pairs={{0,12},{4,8},{8,4},{12,0},{1,13},{5,9},{9,5},{13,1},{2,14},{6,10},... | collective-permute-start | bytes 172040 | tf_op jit(solution)/shard_map/ppermute | solution.py:527
  8.7 6.0 %collective-permute-start.2 = (f32[40,256]{1,0:T(8,128)S(1)}, f32[40,256]{1,0:T(8,128)S(1)}, u32[]{:S(2)}, u32[]{:S(2)}) collective-permute-start(f32[40,256]{1,0:T(8,128)S(1)} %get-tuple-element.23.hi_ref), channel_id=1, source_target_pairs={{0,1},{1,2},{2,3},{3,0},{4,5},{5,6},{6,7},{7,4},{8,9},{9,10},{10,1... | collective-permute-start | bytes 122888 | tf_op jit(solution)/shard_map/ppermute | solution.py:535
  10.4 4.4 %collective-permute-start.3 = (f32[40,256]{1,0:T(8,128)S(1)}, f32[40,256]{1,0:T(8,128)S(1)}, u32[]{:S(2)}, u32[]{:S(2)}) collective-permute-start(f32[40,256]{1,0:T(8,128)S(1)} %get-tuple-element.24.lo_ref), channel_id=1, source_target_pairs={{0,3},{1,0},{2,1},{3,2},{4,7},{5,4},{6,5},{7,6},{8,11},{9,8},{10,9... | collective-permute-start | bytes 122888 | tf_op jit(solution)/shard_map/ppermute | solution.py:536

commit v4 on v3

--- a/solution.py
+++ b/solution.py
@@ -22,8 +22,24 @@
 LO_W1T, LO_W1Z, LO_R0, LO_R1, LO_ROWS = 34, 36, 38, 39, 40
 HI_G, HI_H0T, HI_H0Z, HI_H1T, HI_H1Z = 0, 16, 18, 20, 22
 HI_WT, HI_WN, HI_WZ, HI_R, HI_ROWS = 24, 26, 28, 30, 32
-LANE_HI = 64
-EXT = 24
+EXT, DONE = 24, 16
+
+PACK_F1, PACK_R, PACK_PAIR, PACK_F0, PACK_END = 16, 34, 37, 53, 57
+LO_LANES = (
+    list(range(FILT))
+    + [PACK_PAIR + 2 * j + 1 for j in range(8)]
+    + [PACK_F0 + j for j in range(4)]
+    + [PACK_F1 + 3 * k + 1 for k in range(6)]
+    + [PACK_F1 + 3 * k + 2 for k in (0, 1, 4, 5)]
+    + [PACK_R + 1, PACK_R + 2]
+)
+HI_LANES = (
+    list(range(128 - FILT, 128))
+    + [PACK_PAIR + 2 * j for j in range(8)]
+    + [PACK_F1 + 3 * k for k in range(6)]
+    + [PACK_R, PACK_END]
+)
+CORNER = PACK_END - PACK_F1
 
 
 def tap(distance):
@@ -236,27 +252,48 @@
     return lo, hi
 
 
-def pack_columns(grad, lo, hi):
-    n, m = grad.shape
-    lane = iota((n, 128), 1)
-    first, last = grad[:, 0:128], grad[:, m - 128 : m]
-    pack = jnp.where(lane < FILT, first, 0.0)
-    moved = pltpu.roll(last, LANE_HI + FILT, 1)
-    pack = jnp.where((lane >= LANE_HI) & (lane < LANE_HI + FILT), moved, pack)
-
-    def tile(item, at):
-        if isinstance(item, tuple):
-            return tile(item[0], at) * tile(item[1], at)
-        return item[:, m - 128 : m] if at < 0 else item[:, 0:128]
-
-    for group, start in ((lo, FILT), (hi, LANE_HI + FILT)):
-        for k, (item, at) in enumerate(group):
-            pack = jnp.where(lane == start + k, pltpu.roll(tile(item, at), (start + k - at) % 128, 1), pack)
+def fold(first, last):
+    m = first.shape[1]
+    lane = iota((first.shape[0], 128), 1)
+    return jnp.where(lane < 64, first[:, 0:128], last[:, m - 128 : m])
+
+
+def strips(grad):
+    lane = iota((grad.shape[0], 128), 1)
+    return jnp.where((lane < FILT) | (lane >= 128 - FILT), fold(grad, grad), 0.0)
+
+
+def place(pack, values, base, count=3):
+    lane = iota(pack.shape, 1)
+    return jnp.where((lane >= base) & (lane < base + count), pltpu.roll(values, base + 1, 1), pack)
+
+
+def pack_fields(pack, ratio, e1, h0, h1, e2):
+    pack = place(pack, fold(ratio, ratio), PACK_R)
+    for k, (first, last) in enumerate(((e1, h0), (e2, h1))):
+        for j, (c, z) in enumerate((c, z) for c in (0, 2) for z in range(2)):
+            pack = place(pack, fold(first[c][z], last[c][z]), PACK_PAIR + 8 * k + 2 * j, 2)
     return pack
 
 
+def pack_saved(pack, ratio, fwd):
+    lane = iota(pack.shape, 1)
+    for j, (c, z) in enumerate((c, z) for c in (0, 2) for z in range(2)):
+        pack = jnp.where(lane == PACK_F0 + j, pltpu.roll(fwd[0][c][z][:, 0:128], PACK_F0 + j, 1), pack)
+    scale = jnp.where(lane == 0, 1.0, fold(ratio, ratio))
+    for k, (c, z) in enumerate((c, z) for c in range(3) for z in range(2)):
+        pack = place(pack, fold(fwd[1][c][z], fwd[1][c][z]) * scale, PACK_F1 + 3 * k)
+    return pack
+
+
+def unpack_rows(packed, lanes, ref, at=0):
+    ref[0:FILT, at : at + 128] = packed[lanes[0] : lanes[0] + FILT]
+    for k in range(FILT, len(lanes)):
+        ref[k : k + 1, at : at + 128] = packed[lanes[k] : lanes[k] + 1]
+
+
 def edge_kernel(e_hbm, h_hbm, f_hbm, lab_hbm, den_hbm, eps_hbm,
-                a_ref, b_ref, lo_ref, hi_ref,
+                a_ref, b_ref, lo_ref, hi_ref, e2_ref, h1_ref, grad_ref, pack_ref,
                 e_ref, h_ref, f_ref, lab_ref, den_ref, tab_ref, sems):
     n, m = lab_hbm.shape
     copies = []
@@ -283,12 +320,20 @@
     ratio = ratio_of(lab_ref[...], den_ref[...], tab_ref)
     h0 = planes(h_ref)
 
-    def saved(step):
-        for copy in copies[9 + 2 * step : 11 + 2 * step]:
-            copy.wait()
-        return planes(f_ref, step)
-
-    e1, h1, e2, grad, fwd = local_solve(planes(e_ref), h0, saved, ratio)
+    electric, magnetic = updates(2 * EXT, m, e_hbm.shape[1])
+    e1 = electric(planes(e_ref), h0, ratio)
+    h1 = magnetic(e1, h0)
+    e2 = electric(e1, h1, ratio)
+    pack = pack_fields(jnp.zeros((2 * EXT, 128), F32), ratio, e1, h0, h1, e2)
+    for copy in copies[9:11]:
+        copy.wait()
+    fwd = [planes(f_ref, 0)]
+    grad = product(e1, fwd[0])
+    for copy in copies[11:13]:
+        copy.wait()
+    fwd.append(planes(f_ref, 1))
+    grad = grad + product(e2, fwd[1])
+    pack = pack_saved(pack, ratio, fwd)
     rows = 2 * EXT
 
     def line(item, at):
@@ -298,45 +343,74 @@
         return item[at : at + 1]
 
     lo, hi = edge_lists(1, 0, e1, h0, h1, e2, fwd, ratio)
-    lo_ref[0:FILT] = grad[0:FILT]
-    for k, (item, at) in enumerate(lo):
-        lo_ref[FILT + k : FILT + k + 1] = line(item, at)
-    hi_ref[0:FILT] = grad[rows - FILT : rows]
-    for k, (item, at) in enumerate(hi):
-        hi_ref[FILT + k : FILT + k + 1] = line(item, at)
+    for ref, group, strip in ((hi_ref, hi, grad[rows - FILT : rows]), (lo_ref, lo, grad[0:FILT])):
+        ref[0:FILT] = strip
+        for k, (item, at) in enumerate(group):
+            ref[FILT + k : FILT + k + 1] = line(item, at)
     hi_ref[HI_ROWS - 1 : HI_ROWS] = jnp.zeros((1, m), F32)
-    pack = pack_columns(grad, *edge_lists(0, 1, e1, h0, h1, e2, fwd, ratio))
+    lane = iota((8, 128), 1)
 
     def corner(part):
-        low = jnp.concatenate([part[0:8], part[8:16]], axis=1)
-        high = jnp.concatenate([part[16:24], jnp.zeros((8, m - 128), F32)], axis=1)
-        return jnp.concatenate([low, high], axis=0)
-
-    lo_all = jnp.concatenate([lo_ref[...], corner(pack[0:EXT])], axis=0)
-    hi_all = jnp.concatenate([hi_ref[...], jnp.zeros((LO_ROWS - HI_ROWS, m), F32), corner(pack[EXT:rows])], axis=0)
+        out = pltpu.roll(part[0:8], 128 - PACK_F1, 1)
+        for k in range(1, 3):
+            out = jnp.where(lane < CORNER * k, out, pltpu.roll(part[8 * k : 8 * k + 8], CORNER * k - PACK_F1, 1))
+        return out
+
     first_even = even("gx")
-    a_ref[...] = jnp.where(first_even, hi_all, lo_all)
-    b_ref[...] = jnp.where(first_even, lo_all, hi_all)
-
-
-def solve_kernel(e_ref, h_ref, f_ref, lab_ref, den_ref, eps_ref, pack_ref, grad_ref, e2_ref, h1_ref):
-    ratio = ratio_of(lab_ref[...], den_ref[...], eps_ref)
-    h0 = planes(h_ref)
-    e1, h1, e2, grad, fwd = local_solve(planes(e_ref), h0, lambda step: planes(f_ref, step), ratio)
+    lo_corner, hi_corner = corner(pack[0:EXT]), corner(pack[EXT:rows])
+    for half in range(2):
+        at, cols = half * LO_ROWS, slice(128 * half, 128 * half + 128)
+        low, high = lo_ref[:, cols], hi_ref[:, cols]
+        high = jnp.concatenate([high, jnp.zeros((LO_ROWS - HI_ROWS, 128), F32)], axis=0)
+        a_ref[at : at + LO_ROWS] = jnp.where(first_even, high, low)
+        b_ref[at : at + LO_ROWS] = jnp.where(first_even, low, high)
+    a_ref[2 * LO_ROWS :] = jnp.where(first_even, hi_corner, lo_corner)
+    b_ref[2 * LO_ROWS :] = jnp.where(first_even, lo_corner, hi_corner)
+    pack = jnp.where((iota(pack.shape, 1) < FILT) | (iota(pack.shape, 1) >= 128 - FILT), strips(grad), pack)
+    for to, at in ((0, 0), (DONE, rows - DONE)):
+        for c in range(3):
+            for z in range(e_hbm.shape[1]):
+                e2_ref[c, z, to : to + DONE] = e2[c][z][at : at + DONE]
+                h1_ref[c, z, to : to + DONE] = h1[c][z][at : at + DONE]
+        grad_ref[to : to + DONE] = grad[at : at + DONE]
+        pack_ref[to : to + DONE] = pack[at : at + DONE]
+
+
+def solve_kernel(e_ref, h_ref, f_ref, lab_ref, den_ref, eps_ref, e2_edge, h1_edge, grad_edge, pack_edge,
+                 lo_ref, hi_ref, grad_ref, e2_ref, h1_ref):
+    n, m = lab_ref.shape
+    nz = e_ref.shape[1]
+    rows = pl.ds(DONE - 8, n - 2 * DONE + 16)
+
+    def inner(ref, *lead):
+        return [[ref[(*lead, c, z, rows)] for z in range(nz)] for c in range(3)]
+
+    ratio = ratio_of(lab_ref[rows], den_ref[rows], eps_ref)
+    h0 = inner(h_ref)
+    e1, h1, e2, grad, fwd = local_solve(inner(e_ref), h0, lambda step: inner(f_ref, step), ratio)
+    last = n - DONE
     for c in range(3):
-        for z in range(e_ref.shape[1]):
-            e2_ref[c, z] = e2[c][z]
-            h1_ref[c, z] = h1[c][z]
-    grad_ref[...] = grad
-    pack_ref[...] = pack_columns(grad, *edge_lists(0, 1, e1, h0, h1, e2, fwd, ratio))
-
-
-def x_kernel(ra_ref, rb_ref, lo_ref, hi_ref, pack_ref, grad_ref,
+        for z in range(nz):
+            for ref, edge, value in ((e2_ref, e2_edge, e2), (h1_ref, h1_edge, h1)):
+                ref[c, z, 0:DONE] = edge[c, z, 0:DONE]
+                ref[c, z, DONE:last] = value[c][z][8 : last - DONE + 8]
+                ref[c, z, last:n] = edge[c, z, DONE : 2 * DONE]
+    grad_ref[0:DONE] = grad_edge[0:DONE]
+    grad_ref[DONE:last] = grad[8 : last - DONE + 8]
+    grad_ref[last:n] = grad_edge[DONE : 2 * DONE]
+    pack = pack_saved(pack_fields(strips(grad), ratio, e1, h0, h1, e2), ratio, fwd)
+    packed = jnp.concatenate([pack_edge[0:DONE], pack[8 : last - DONE + 8], pack_edge[DONE : 2 * DONE]], axis=0).T
+    unpack_rows(packed, LO_LANES, lo_ref)
+    unpack_rows(packed, HI_LANES, hi_ref)
+
+
+def x_kernel(ra_ref, rb_ref, lo_ref, hi_ref, plo_ref, phi_ref, grad_ref,
              yhi_ref, ylo_ref, ext_ref, dr_ref):
     n, m = grad_ref.shape
     first_even = even("gx")
-    right = jnp.where(first_even, ra_ref[...], rb_ref[...])
-    left = jnp.where(first_even, rb_ref[...], ra_ref[...])
+    got_right = jnp.where(first_even, ra_ref[...], rb_ref[...])
+    got_left = jnp.where(first_even, rb_ref[...], ra_ref[...])
+    right, left = (jnp.concatenate([got[0:LO_ROWS], got[LO_ROWS : 2 * LO_ROWS]], axis=1) for got in (got_right, got_left))
     a, b = seam_inputs(left, hi_ref[...], lo_ref[...], right)
     col = iota((8, m), 1)
     d = seam(
@@ -366,54 +440,57 @@
 
     lane = iota((1, 128), 1)
 
-    def strips(g):
-        out = jnp.where(lane < FILT, g[:, 0:128], 0.0)
-        moved = pltpu.roll(g[:, m - 128 : m], LANE_HI + FILT, 1)
-        return jnp.where((lane >= LANE_HI) & (lane < LANE_HI + FILT), moved, out)
-
-    def put(row_vec, at, value, seam_row, c):
+    def put(row_vec, lanes, at, value, seam_row, c):
         for z in range(2):
             one = value[seam_row + z : seam_row + z + 1, c : c + 1]
-            row_vec = jnp.where(lane == at + z, one, row_vec)
+            row_vec = jnp.where(lane == lanes[at + z], one, row_vec)
         return row_vec
 
-    hi = LANE_HI
-    row0 = strips(gb0[0:1])
-    row0 = put(row0, LO_E1Z, d["b_e1z"], 0, 0)
-    row0 = put(row0, LO_E2T, d["e"]["n"][2], 0, 0)
-    row0 = put(row0, LO_E2Z, d["e"]["z"][2], 0, 0)
-    row0 = put(row0, hi + HI_H1T, d["b_h1n"], 0, m - 1)
-    row0 = put(row0, hi + HI_H1Z, d["b_h1z"], 0, m - 1)
-    row1 = strips(gb1[0:1])
-    row1 = put(row1, LO_E2Z, d["e"]["z"][3], 0, 0)
-    end = strips(ga[2:3])
-    end = put(end, LO_E2T, d["e"]["n"][1], 2, 0)
-    end = put(end, LO_E2Z, d["e"]["z"][1], 2, 0)
-    end = put(end, hi + HI_H1Z, d["a_h1z"], 2, m - 1)
-    out0 = strips(gb0[2:3])
-    out0 = put(out0, LO_E1Z, d["b_e1z"], 2, 0)
-    out0 = put(out0, hi + HI_H1T, d["b_h1n"], 2, m - 1)
-    out0 = put(out0, hi + HI_H1Z, d["b_h1z"], 2, m - 1)
-    out1 = strips(gb1[2:3])
-    before = strips(ga[0:1])
-    before = put(before, hi + HI_H1Z, d["a_h1z"], 0, m - 1)
+    row0 = put(strips(gb0[0:1]), LO_LANES, LO_E1Z, d["b_e1z"], 0, 0)
+    row0 = put(row0, LO_LANES, LO_E2T, d["e"]["n"][2], 0, 0)
+    row0 = put(row0, LO_LANES, LO_E2Z, d["e"]["z"][2], 0, 0)
+    row0 = put(row0, HI_LANES, HI_H1T, d["b_h1n"], 0, m - 1)
+    row0 = put(row0, HI_LANES, HI_H1Z, d["b_h1z"], 0, m - 1)
+    row1 = put(strips(gb1[0:1]), LO_LANES, LO_E2Z, d["e"]["z"][3], 0, 0)
+    end = put(strips(ga[2:3]), LO_LANES, LO_E2T, d["e"]["n"][1], 2, 0)
+    end = put(end, LO_LANES, LO_E2Z, d["e"]["z"][1], 2, 0)
+    end = put(end, HI_LANES, HI_H1Z, d["a_h1z"], 2, m - 1)
+    none = jnp.zeros((1, 128), F32)
+    out0 = put(none, LO_LANES, LO_E1Z, d["b_e1z"], 2, 0)
+    out0 = put(out0, HI_LANES, HI_H1T, d["b_h1n"], 2, m - 1)
+    out0 = put(out0, HI_LANES, HI_H1Z, d["b_h1z"], 2, m - 1)
+    before = put(none, HI_LANES, HI_H1Z, d["a_h1z"], 0, m - 1)
 
     sub = iota((8, 128), 0)
-
-    def corner(message):
-        return [message[40:48, 0:128], message[40:48, 128:256], message[48:56, 0:128]]
-
-    above, below = corner(right), corner(left)
-    above[0] = above[0] + jnp.where(sub == 0, out0, jnp.where(sub == 1, out1, 0.0))
+    wide = iota((8, 128), 1)
+
+    def corner(message, first_row):
+        tile = message[2 * LO_ROWS : 2 * LO_ROWS + 8]
+        out = []
+        for k in range(3):
+            moved = pltpu.roll(tile, (PACK_F1 - CORNER * k) % 128, 1)
+            part = jnp.where((wide >= PACK_F1) & (wide < PACK_END), moved, 0.0)
+            at = first_row + 8 * k
+            if n <= at < n + FILT or at >= 2 * n - FILT:
+                part = part + strips(ext_ref[at : at + 8])
+            out.append(part)
+        return out
+
+    above, below = corner(got_right, n), corner(got_left, 2 * n - EXT)
+    above[0] = above[0] + jnp.where(sub == 0, out0, 0.0)
     below[2] = below[2] + jnp.where(sub == 7, before, 0.0)
-    head = pack_ref[0:8] + jnp.where(sub == 0, row0, jnp.where(sub == 1, row1, 0.0))
-    tail = pack_ref[n - 8 : n] + jnp.where(sub == 7, end, 0.0)
-    inner = jnp.concatenate([head, pack_ref[8 : n - 8], tail], axis=0)
-    outer = jnp.concatenate(above + [jnp.zeros((n - 2 * EXT, 128), F32)] + below, axis=0)
-    packed = jnp.concatenate([inner.T, outer.T], axis=1)
-    lo, hi_part = packed[0:LO_ROWS], packed[LANE_HI : LANE_HI + LO_ROWS]
-    ylo_ref[...] = lo
-    yhi_ref[...] = hi_part
+    own = jnp.where(sub == 0, end, jnp.where(sub == 1, row0, jnp.where(sub == 2, row1, 0.0)))
+    filler = jnp.zeros((8, 128), F32)
+    used = EXT // 8
+    tiles = above + [own] + [filler] * (n // 8 - 2 * used - 1) + below
+    packed = jnp.concatenate(tiles, axis=0).T
+    for ref, mine, lanes in ((ylo_ref, plo_ref, LO_LANES), (yhi_ref, phi_ref, HI_LANES)):
+        count = len(lanes)
+        unpack_rows(packed, lanes, ref, n)
+        at = iota((count, n), 1)
+        moved = pltpu.roll(ref[0:count, n : 2 * n], (n - EXT - 1) % n, 1)
+        ref[0:count, 0:n] = mine[...] + jnp.where((at < 2) | (at == n - 1), moved, 0.0)
+    yhi_ref[HI_ROWS:LO_ROWS] = jnp.zeros((LO_ROWS - HI_ROWS, 2 * n), F32)
 
 
 def inner_kernel(ext_ref, e2_ref, h1_ref, out_ref, h2_ref):
@@ -512,11 +589,12 @@
     block = adj_e.shape
     nz = block[1]
     ins = [adj_e, adj_h, fwd_e, labels, density, eps_table]
-    message = (LO_ROWS + 16, m)
+    message = (2 * LO_ROWS + 8, 128)
     strip = (2 * EXT, m)
-    xa, xb, lo, hi = call(
+    edges = (3, nz, 2 * DONE, m)
+    xa, xb, lo, hi, *solved = call(
         edge_kernel,
-        [message, message, (LO_ROWS, m), (HI_ROWS, m)],
+        [message, message, (LO_ROWS, m), (HI_ROWS, m), edges, edges, (2 * DONE, m), (2 * DONE, 128)],
         ins,
         [(3, nz, *strip), (3, nz, *strip), (STEPS, 3, nz, *strip), pltpu.VMEM(strip, jnp.int32), strip, pltpu.SMEM((NMAT,), F32)],
         range(6),
@@ -525,12 +603,14 @@
     gx, gy = lax.axis_size("gx"), lax.axis_size("gy")
     got_a = lax.ppermute(xa, "gx", swap_pairs(gx, 0))
     got_b = lax.ppermute(xb, "gx", swap_pairs(gx, 1))
-    pack, grad, e2, h1 = call(solve_kernel, [(n, 128), (n, m), block, block], ins)
+    plo, phi, grad, e2, h1 = call(
+        solve_kernel, [(LO_ROWS, n), (HI_ROWS, n), (n, m), block, block], ins + solved
+    )
     column = (LO_ROWS, 2 * n)
     yhi, ylo, ext, dr = call(
         x_kernel,
         [column, column, (2 * n, m), (48, m)],
-        [got_a, got_b, lo, hi, pack, grad],
+        [got_a, got_b, lo, hi, plo, phi, grad],
     )
     left = lax.ppermute(yhi, "gy", [(i, (i + 1) % gy) for i in range(gy)])
     right = lax.ppermute(ylo, "gy", [(i, (i - 1) % gy) for i in range(gy)])

time: 16.7 us -> 16.5 us (0.988)
  Pallas kernels: 7.37 us -> 6.69 us
  waiting for transfers between devices: 1.42 us -> 1.86 us
    pallas_call x5, Pallas kernels: 7.37 us -> 6.69 us  [call(): pl.pallas_call(kernel, out_shape=[jax.ShapeDtypeStruct(s, F32) for s in s...]
    ppermute x1, waiting for transfers between devices: 0.01 us -> 0.26 us  [body(): got_b = lax.ppermute(xb, 'gx', swap_pairs(gx, 1))]
    ppermute x1, waiting for transfers between devices: 0.07 us -> 0.27 us  [body(): right = lax.ppermute(ylo, 'gy', [(i, (i - 1) % gy) for i in range(gy)])]
  transfers between devices with their start and end apart: 4 -> 4, of which waited for: 2 -> 3; matrix products, arithmetic and copies ran while one was open for 0% -> 0% of each run, Pallas kernels for 19% -> 15%
where the time goes in v4:
time: 16.5 us; the launch traced here: 16.3 us
  starting transfers between devices  7.01 us (42%)
  Pallas kernels  6.69 us (41%)
  waiting for transfers between devices  1.86 us (11%)
  between operations  0.74 us (4%)
    pallas_call x5, Pallas kernels, call(): pl.pallas_call(kernel, out_shape=[jax.ShapeDtypeStruct(s, F32) for s in s...  6.69 us
    ppermute x1, starting transfers between devices, body(): got_b = lax.ppermute(xb, 'gx', swap_pairs(gx, 1))  2.61 us
    ppermute x1, starting transfers between devices, body(): right = lax.ppermute(ylo, 'gy', [(i, (i - 1) % gy) for i in range(gy)])  2.25 us
    ppermute x1, starting transfers between devices, body(): left = lax.ppermute(yhi, 'gy', [(i, (i + 1) % gy) for i in range(gy)])  1.63 us
    ppermute x1, waiting for transfers between devices, body(): left = lax.ppermute(yhi, 'gy', [(i, (i + 1) % gy) for i in range(gy)])  1.34 us
    ppermute x1, starting transfers between devices, body(): got_a = lax.ppermute(xa, 'gx', swap_pairs(gx, 0))  0.52 us
  transfers between devices with their start and end apart: 4, of which 3 were waited for; matrix products, arithmetic and copies ran while one was open for 0% of the time, Pallas kernels for 15%

profile of v4, /device:TPU:0, one launch (start us, length us, event | category | flops | bytes accessed | tf_op | source)
XLA Modules:
  0.0 16.3 jit_solution(13301419429598020502)
XLA Ops:
  0.6 0.0 copy-start.4
  0.6 0.0 copy-start.5
  0.7 0.0 copy-start.3
  0.7 0.0 copy-start
  0.7 0.0 copy-start.2
  0.7 0.0 copy-start.1
  0.7 2.1 %shard_map.85 = (f32[88,128]{1,0:T(8,128)S(1)}, f32[88,128]{1,0:T(8,128)S(1)}, f32[40,256]{1,0:T(8,128)S(1)}, f32[32,256]{1,0:T(8,128)S(1)}, f32[3,2,32,256]{3,2...) custom-call(f32[3,2,128,256]{3,2,1,0:T(8,128)} %e_ref.1, ...), custom_call_target="tpu_custom_call" | custom-call | tf_op jit(solution)/shard_map/pallas_call | solution.py:577
  2.8 0.5 %collective-permute-start = (f32[88,128]{1,0:T(8,128)S(1)}, f32[88,128]{1,0:T(8,128)S(1)}, u32[]{:S(2)}, u32[]{:S(2)}) collective-permute-start(f32[88,128]{1,0:T(8,128)S(1)} %get-tuple-element.22), channel_id=1, source_target_pairs={{0,4},{4,0},{8,12},{12,8},{1,5},{5,1},{9,13},{13,9},{2,6},{6,2},{1... | collective-permute-start | bytes 135176 | tf_op jit(solution)/shard_map/ppermute | solution.py:604
  3.3 2.6 %collective-permute-start.1 = (f32[88,128]{1,0:T(8,128)S(1)}, f32[88,128]{1,0:T(8,128)S(1)}, u32[]{:S(2)}, u32[]{:S(2)}) collective-permute-start(f32[88,128]{1,0:T(8,128)S(1)} %get-tuple-element.23), channel_id=1, source_target_pairs={{0,12},{4,8},{8,4},{12,0},{1,13},{5,9},{9,5},{13,1},{2,14},{6,10},... | collective-permute-start | bytes 135176 | tf_op jit(solution)/shard_map/ppermute | solution.py:605
  6.0 0.0 copy-done.4
  6.0 0.0 copy-done.5
  6.0 0.0 copy-done.3
  6.0 0.0 copy-done
  6.0 0.0 copy-done.2
  6.0 0.0 copy-done.1
  6.0 1.6 %shard_map.86 = (f32[40,128]{1,0:T(8,128)S(1)}, f32[32,128]{1,0:T(8,128)S(1)}, f32[128,256]{1,0:T(8,128)S(1)}, f32[3,2,128,256]{3,2,1,0:T(8,128)S(1)}, f32[3,2,128,256]{3,2,1,0:T(8,128)S(1)}) custom-call(f32[3,2,128,256]{3,2,1,0:T(8,128)S(1)} %copy-done.1, f32[3,2,128,256]{3,2,1,0:T(8,128)S(1)} %copy-done.2, f32[2,3,2,128,256]{4,3,2,1,0:T(8,128)S(1)} %copy-done, ...), custom_call_target="tpu_custom_call" | custom-call | tf_op jit(solution)/shard_map/pallas_call | solution.py:577
  7.6 0.0 collective-permute-done.ra_ref
  7.6 0.3 %collective-permute-done.1.rb_ref = f32[88,128]{1,0:T(8,128)S(1)} collective-permute-done((f32[88,128]{1,0:T(8,128)S(1)}, f32[88,128]{1,0:T(8,128)S(1)}, u32[]{:S(2)}, u32[]{:S(2)}) %collective-permute-start.1) | collective-permute-done | bytes 45088 | tf_op jit(solution)/shard_map/ppermute | solution.py:605
  7.9 0.4 %shard_map.87 = (f32[40,256]{1,0:T(8,128)S(1)}, f32[40,256]{1,0:T(8,128)S(1)}, f32[256,256]{1,0:T(8,128)S(1)}, f32[48,256]{1,0:T(8,128)S(1)}) custom-call(f32[88,128]{1,0:T(8,128)S(1)} %collective-permute-done.ra_ref, f32[88,128]{1,0:T(8,128)S(1)} %collective-permute-done.1.rb_ref, f32[40,256]{1,0:T(8,128)S(1)} %get-tuple-element.24.lo_ref, ...), custom_call_target="tpu_custom_call" | custom-call | tf_op jit(solution)/shard_map/pallas_call | solution.py:577
  8.3 1.6 %collective-permute-start.2 = (f32[40,256]{1,0:T(8,128)S(1)}, f32[40,256]{1,0:T(8,128)S(1)}, u32[]{:S(2)}, u32[]{:S(2)}) collective-permute-start(f32[40,256]{1,0:T(8,128)S(1)} %get-tuple-element.33.hi_ref), channel_id=1, source_target_pairs={{0,1},{1,2},{2,3},{3,0},{4,5},{5,6},{6,7},{7,4},{8,9},{9,10},{10,1... | collective-permute-start | bytes 122888 | tf_op jit(solution)/shard_map/ppermute | solution.py:615
  9.9 2.3 %collective-permute-start.3 = (f32[40,256]{1,0:T(8,128)S(1)}, f32[40,256]{1,0:T(8,128)S(1)}, u32[]{:S(2)}, u32[]{:S(2)}) collective-permute-start(f32[40,256]{1,0:T(8,128)S(1)} %get-tuple-element.34.lo_ref), channel_id=1, source_target_pairs={{0,3},{1,0},{2,1},{3,2},{4,7},{5,4},{6,5},{7,6},{8,11},{9,8},{10,9... | collective-permute-start | bytes 122888 | tf_op jit(solution)/shard_map/ppermute | solution.py:616
  12.2 0.8 %shard_map.88 = (f32[128,256]{1,0:T(8,128)S(1)}, f32[3,2,128,256]{3,2,1,0:T(8,128)S(1)}) custom-call(f32[256,256]{1,0:T(8,128)S(1)} %get-tuple-element.37.ext_ref, f32[3,2,128,256]{3,2,1,0:T(8,128)S(1)} %get-tuple-element.36.e2_ref, f32[3,2,128,256]{3,2,1,0:T(8,128)S(1)} %get-tuple-element.38.h1_ref), custom_call_target="tpu_custom_call" | custom-call | tf_op jit(solution)/shard_map/pallas_call | solution.py:577
  13.0 1.3 %collective-permute-done.2.left_ref = f32[40,256]{1,0:T(8,128)S(1)} collective-permute-done((f32[40,256]{1,0:T(8,128)S(1)}, f32[40,256]{1,0:T(8,128)S(1)}, u32[]{:S(2)}, u32[]{:S(2)}) %collective-permute-start.2) | collective-permute-done | bytes 40992 | tf_op jit(solution)/shard_map/ppermute | solution.py:615
  14.3 0.3 %collective-permute-done.3.right_ref = f32[40,256]{1,0:T(8,128)S(1)} collective-permute-done((f32[40,256]{1,0:T(8,128)S(1)}, f32[40,256]{1,0:T(8,128)S(1)}, u32[]{:S(2)}, u32[]{:S(2)}) %collective-permute-start.3) | collective-permute-done | bytes 40992 | tf_op jit(solution)/shard_map/ppermute | solution.py:616
  14.6 1.8 %shard_map.89 = (f32[3,2,128,256]{3,2,1,0:T(8,128)}, f32[3,2,128,256]{3,2,1,0:T(8,128)}, f32[128,256]{1,0:T(8,128)}) custom-call(f32[40,256]{1,0:T(8,128)S(1)} %collective-permute-done.2.left_ref, f32[40,256]{1,0:T(8,128)S(1)} %collective-permute-done.3.right_ref, f32[40,256]{1,0:T(8,128)S(1)} %get-tuple-element.34.lo_ref, ...), custom_call_target="tpu_custom_call" | custom-call | tf_op jit(solution)/shard_map/pallas_call | solution.py:577
Async XLA Ops:
  0.6 5.3 %copy-start.4 = (f32[128,256]{1,0:T(8,128)S(1)}, f32[128,256]{1,0:T(8,128)}, u32[]{:S(2)}) copy-start(f32[128,256]{1,0:T(8,128)} %den_ref.1) | copy-start | bytes 393220
  0.6 5.3 %copy-start.5 = (f32[8]{0:T(128)S(1)}, f32[8]{0:T(128)}, u32[]{:S(2)}) copy-start(f32[8]{0:T(128)} %eps_ref.1) | copy-start | bytes 100
  0.7 5.3 %copy-start.3 = (s32[128,256]{1,0:T(8,128)S(1)}, s32[128,256]{1,0:T(8,128)}, u32[]{:S(2)}) copy-start(s32[128,256]{1,0:T(8,128)} %lab_ref.1) | copy-start | bytes 393220
  0.7 5.3 %copy-start = (f32[2,3,2,128,256]{4,3,2,1,0:T(8,128)S(1)}, f32[2,3,2,128,256]{4,3,2,1,0:T(8,128)}, u32[]{:S(2)}) copy-start(f32[2,3,2,128,256]{4,3,2,1,0:T(8,128)} %f_ref.1) | copy-start | bytes 4718596
  0.7 5.3 %copy-start.2 = (f32[3,2,128,256]{3,2,1,0:T(8,128)S(1)}, f32[3,2,128,256]{3,2,1,0:T(8,128)}, u32[]{:S(2)}) copy-start(f32[3,2,128,256]{3,2,1,0:T(8,128)} %h_ref.1) | copy-start | bytes 2359300
  0.7 5.3 %copy-start.1 = (f32[3,2,128,256]{3,2,1,0:T(8,128)S(1)}, f32[3,2,128,256]{3,2,1,0:T(8,128)}, u32[]{:S(2)}) copy-start(f32[3,2,128,256]{3,2,1,0:T(8,128)} %e_ref.1) | copy-start | bytes 2359300
  2.8 4.8 %collective-permute-start = (f32[88,128]{1,0:T(8,128)S(1)}, f32[88,128]{1,0:T(8,128)S(1)}, u32[]{:S(2)}, u32[]{:S(2)}) collective-permute-start(f32[88,128]{1,0:T(8,128)S(1)} %get-tuple-element.22), channel_id=1, source_target_pairs={{0,4},{4,0},{8,12},{12,8},{1,5},{5,1},{9,13},{13,9},{2,6},{6,2},{1... | collective-permute-start | bytes 135176 | tf_op jit(solution)/shard_map/ppermute | solution.py:604
  3.3 4.5 %collective-permute-start.1 = (f32[88,128]{1,0:T(8,128)S(1)}, f32[88,128]{1,0:T(8,128)S(1)}, u32[]{:S(2)}, u32[]{:S(2)}) collective-permute-start(f32[88,128]{1,0:T(8,128)S(1)} %get-tuple-element.23), channel_id=1, source_target_pairs={{0,12},{4,8},{8,4},{12,0},{1,13},{5,9},{9,5},{13,1},{2,14},{6,10},... | collective-permute-start | bytes 135176 | tf_op jit(solution)/shard_map/ppermute | solution.py:605
  8.3 6.0 %collective-permute-start.2 = (f32[40,256]{1,0:T(8,128)S(1)}, f32[40,256]{1,0:T(8,128)S(1)}, u32[]{:S(2)}, u32[]{:S(2)}) collective-permute-start(f32[40,256]{1,0:T(8,128)S(1)} %get-tuple-element.33.hi_ref), channel_id=1, source_target_pairs={{0,1},{1,2},{2,3},{3,0},{4,5},{5,6},{6,7},{7,4},{8,9},{9,10},{10,1... | collective-permute-start | bytes 122888 | tf_op jit(solution)/shard_map/ppermute | solution.py:615
  9.9 4.6 %collective-permute-start.3 = (f32[40,256]{1,0:T(8,128)S(1)}, f32[40,256]{1,0:T(8,128)S(1)}, u32[]{:S(2)}, u32[]{:S(2)}) collective-permute-start(f32[40,256]{1,0:T(8,128)S(1)} %get-tuple-element.34.lo_ref), channel_id=1, source_target_pairs={{0,3},{1,0},{2,1},{3,2},{4,7},{5,4},{6,5},{7,6},{8,11},{9,8},{10,9... | collective-permute-start | bytes 122888 | tf_op jit(solution)/shard_map/ppermute | solution.py:616

commit v5 on v4

--- a/solution.py
+++ b/solution.py
@@ -22,7 +22,7 @@
 LO_W1T, LO_W1Z, LO_R0, LO_R1, LO_ROWS = 34, 36, 38, 39, 40
 HI_G, HI_H0T, HI_H0Z, HI_H1T, HI_H1Z = 0, 16, 18, 20, 22
 HI_WT, HI_WN, HI_WZ, HI_R, HI_ROWS = 24, 26, 28, 30, 32
-EXT, DONE = 24, 16
+EXT = 24
 
 PACK_F1, PACK_R, PACK_PAIR, PACK_F0, PACK_END = 16, 34, 37, 53, 57
 LO_LANES = (
@@ -69,15 +69,15 @@
     def uy(f):
         return jnp.where(col == m - 1, 0.0, pltpu.roll(f, m - 1, 1))
 
-    def electric(e, h, ratio):
+    def turn(h, ratio):
         out = [[None] * nz for _ in range(3)]
         for z in range(nz):
             hx, hy, hz = h[0][z], h[1][z], h[2][z]
             dzx = hx - h[0][z - 1] if z > 0 else hx
             dzy = hy - h[1][z - 1] if z > 0 else hy
-            out[0][z] = e[0][z] - ratio * ((hz - ly(hz)) - dzy)
-            out[1][z] = e[1][z] - ratio * (dzx - (hz - lx(hz)))
-            out[2][z] = e[2][z] - ratio * ((hy - lx(hy)) - (hx - ly(hx)))
+            out[0][z] = ratio * ((hz - ly(hz)) - dzy)
+            out[1][z] = ratio * (dzx - (hz - lx(hz)))
+            out[2][z] = ratio * ((hy - lx(hy)) - (hx - ly(hx)))
         return out
 
     def magnetic(e, h):
@@ -91,7 +91,11 @@
             out[2][z] = h[2][z] + courant * ((ux(ey) - ey) - (uy(ex) - ex))
         return out
 
-    return electric, magnetic
+    return turn, magnetic
+
+
+def less(e, change):
+    return [[a - b for a, b in zip(one, other, strict=True)] for one, other in zip(e, change, strict=True)]
 
 
 def product(e, f):
@@ -104,12 +108,12 @@
 
 
 def local_solve(e0, h0, saved, ratio):
-    electric, magnetic = updates(*ratio.shape, len(e0[0]))
-    e1 = electric(e0, h0, ratio)
+    turn, magnetic = updates(*ratio.shape, len(e0[0]))
+    e1 = less(e0, turn(h0, ratio))
     h1 = magnetic(e1, h0)
     fwd = [saved(0)]
     grad = product(e1, fwd[0])
-    e2 = electric(e1, h1, ratio)
+    e2 = less(e1, turn(h1, ratio))
     fwd.append(saved(1))
     grad = grad + product(e2, fwd[1])
     return e1, h1, e2, grad, fwd
@@ -222,10 +226,10 @@
     return lax.axis_index(axis) % 2 == 0
 
 
-def ratio_of(labels, density, eps_ref):
-    eps = jnp.full(labels.shape, eps_ref[0], F32)
+def ratio_of(labels, density, table):
+    eps = jnp.broadcast_to(table[0], labels.shape)
     for k in range(1, NMAT):
-        eps = jnp.where(labels == k, eps_ref[k], eps)
+        eps = jnp.where(labels == k, table[k], eps)
     return courant / (eps + density)
 
 
@@ -293,44 +297,47 @@
 
 
 def edge_kernel(e_hbm, h_hbm, f_hbm, lab_hbm, den_hbm, eps_hbm,
-                a_ref, b_ref, lo_ref, hi_ref, e2_ref, h1_ref, grad_ref, pack_ref,
+                a_ref, b_ref, lo_ref, hi_ref, table_ref,
                 e_ref, h_ref, f_ref, lab_ref, den_ref, tab_ref, sems):
     n, m = lab_hbm.shape
+    nz = e_hbm.shape[1]
     copies = []
 
-    def fetch(src, dst, lead):
-        for at, start in ((0, 0), (EXT, n - EXT)):
-            index = (*lead, pl.ds(start, EXT))
-            copy = pltpu.make_async_copy(src.at[index], dst.at[(*lead, pl.ds(at, EXT))], sems.at[len(copies) - 1])
+    def fetch(src, dst, *lead):
+        for to, at in ((0, 0), (EXT, n - EXT)):
+            copy = pltpu.make_async_copy(src.at[(*lead, pl.ds(at, EXT))], dst.at[(*lead, pl.ds(to, EXT))], sems.at[len(copies)])
             copy.start()
             copies.append(copy)
 
     every = slice(None)
-    table = pltpu.make_async_copy(eps_hbm, tab_ref, sems.at[12])
-    table.start()
-    copies.append(table)
-    fetch(lab_hbm, lab_ref, ())
-    fetch(den_hbm, den_ref, ())
-    fetch(h_hbm, h_ref, (every, every))
-    fetch(e_hbm, e_ref, (every, every))
+    fetch(h_hbm, h_ref, every, every)
+    fetch(lab_hbm, lab_ref)
+    fetch(den_hbm, den_ref)
+    copies.append(pltpu.make_async_copy(eps_hbm, tab_ref, sems.at[len(copies)]))
+    copies[-1].start()
+    fetch(e_hbm, e_ref, every, every)
     for step in range(STEPS):
-        fetch(f_hbm, f_ref, (step, every, every))
-    for copy in copies[:9]:
-        copy.wait()
+        fetch(f_hbm, f_ref, step, every, every)
+
+    def wait(first, last):
+        for copy in copies[first:last]:
+            copy.wait()
+
+    turn, magnetic = updates(2 * EXT, m, nz)
+    wait(2, 7)
     ratio = ratio_of(lab_ref[...], den_ref[...], tab_ref)
+    wait(0, 2)
     h0 = planes(h_ref)
-
-    electric, magnetic = updates(2 * EXT, m, e_hbm.shape[1])
-    e1 = electric(planes(e_ref), h0, ratio)
+    change = turn(h0, ratio)
+    wait(7, 9)
+    e1 = less(planes(e_ref), change)
     h1 = magnetic(e1, h0)
-    e2 = electric(e1, h1, ratio)
+    e2 = less(e1, turn(h1, ratio))
     pack = pack_fields(jnp.zeros((2 * EXT, 128), F32), ratio, e1, h0, h1, e2)
-    for copy in copies[9:11]:
-        copy.wait()
+    wait(9, 11)
     fwd = [planes(f_ref, 0)]
     grad = product(e1, fwd[0])
-    for copy in copies[11:13]:
-        copy.wait()
+    wait(11, 13)
     fwd.append(planes(f_ref, 1))
     grad = grad + product(e2, fwd[1])
     pack = pack_saved(pack, ratio, fwd)
@@ -366,40 +373,20 @@
         b_ref[at : at + LO_ROWS] = jnp.where(first_even, low, high)
     a_ref[2 * LO_ROWS :] = jnp.where(first_even, hi_corner, lo_corner)
     b_ref[2 * LO_ROWS :] = jnp.where(first_even, lo_corner, hi_corner)
-    pack = jnp.where((iota(pack.shape, 1) < FILT) | (iota(pack.shape, 1) >= 128 - FILT), strips(grad), pack)
-    for to, at in ((0, 0), (DONE, rows - DONE)):
-        for c in range(3):
-            for z in range(e_hbm.shape[1]):
-                e2_ref[c, z, to : to + DONE] = e2[c][z][at : at + DONE]
-                h1_ref[c, z, to : to + DONE] = h1[c][z][at : at + DONE]
-        grad_ref[to : to + DONE] = grad[at : at + DONE]
-        pack_ref[to : to + DONE] = pack[at : at + DONE]
-
-
-def solve_kernel(e_ref, h_ref, f_ref, lab_ref, den_ref, eps_ref, e2_edge, h1_edge, grad_edge, pack_edge,
-                 lo_ref, hi_ref, grad_ref, e2_ref, h1_ref):
-    n, m = lab_ref.shape
-    nz = e_ref.shape[1]
-    rows = pl.ds(DONE - 8, n - 2 * DONE + 16)
-
-    def inner(ref, *lead):
-        return [[ref[(*lead, c, z, rows)] for z in range(nz)] for c in range(3)]
-
-    ratio = ratio_of(lab_ref[rows], den_ref[rows], eps_ref)
-    h0 = inner(h_ref)
-    e1, h1, e2, grad, fwd = local_solve(inner(e_ref), h0, lambda step: inner(f_ref, step), ratio)
-    last = n - DONE
+    for k in range(NMAT):
+        table_ref[k : k + 1] = jnp.full((1, m), tab_ref[k], F32)
+
+
+def solve_kernel(e_ref, h_ref, f_ref, lab_ref, den_ref, table_ref, lo_ref, hi_ref, grad_ref, e2_ref, h1_ref):
+    ratio = ratio_of(lab_ref[...], den_ref[...], [table_ref[k : k + 1] for k in range(NMAT)])
+    h0 = planes(h_ref)
+    e1, h1, e2, grad, fwd = local_solve(planes(e_ref), h0, lambda step: planes(f_ref, step), ratio)
     for c in range(3):
-        for z in range(nz):
-            for ref, edge, value in ((e2_ref, e2_edge, e2), (h1_ref, h1_edge, h1)):
-                ref[c, z, 0:DONE] = edge[c, z, 0:DONE]
-                ref[c, z, DONE:last] = value[c][z][8 : last - DONE + 8]
-                ref[c, z, last:n] = edge[c, z, DONE : 2 * DONE]
-    grad_ref[0:DONE] = grad_edge[0:DONE]
-    grad_ref[DONE:last] = grad[8 : last - DONE + 8]
-    grad_ref[last:n] = grad_edge[DONE : 2 * DONE]
-    pack = pack_saved(pack_fields(strips(grad), ratio, e1, h0, h1, e2), ratio, fwd)
-    packed = jnp.concatenate([pack_edge[0:DONE], pack[8 : last - DONE + 8], pack_edge[DONE : 2 * DONE]], axis=0).T
+        for z in range(e_ref.shape[1]):
+            e2_ref[c, z] = e2[c][z]
+            h1_ref[c, z] = h1[c][z]
+    grad_ref[...] = grad
+    packed = pack_saved(pack_fields(strips(grad), ratio, e1, h0, h1, e2), ratio, fwd).T
     unpack_rows(packed, LO_LANES, lo_ref)
     unpack_rows(packed, HI_LANES, hi_ref)
 
@@ -493,37 +480,35 @@
     yhi_ref[HI_ROWS:LO_ROWS] = jnp.zeros((LO_ROWS - HI_ROWS, 2 * n), F32)
 
 
-def inner_kernel(ext_ref, e2_ref, h1_ref, out_ref, h2_ref):
+def cyclic(d, count):
+    return jnp.where(d > count // 2, d - count, jnp.where(d < -(count // 2), d + count, d))
+
+
+def inner_kernel(ext_ref, e2_ref, h1_ref, out_ref, h2_ref, band_ref, spread_ref):
+    rows, m = ext_ref.shape
+    n = out_ref.shape[0]
     nz = e2_ref.shape[1]
-    _, magnetic = updates(*out_ref.shape, nz)
+    _, magnetic = updates(n, m, nz)
     h2 = magnetic(planes(e2_ref), planes(h1_ref))
     for c in range(3):
         for z in range(nz):
             h2_ref[c, z] = h2[c][z]
-    rows, m = ext_ref.shape
-    n = out_ref.shape[0]
-    d = iota((n, rows), 1) - iota((n, rows), 0)
-    d = jnp.where(d > rows // 2, d - rows, jnp.where(d < -(rows // 2), d + rows, d))
-    along = jnp.dot(tap(d), ext_ref[...], precision=HIGHEST, preferred_element_type=F32)
-    e = iota((m, m), 0) - iota((m, m), 1)
-    out_ref[...] = jnp.dot(along, tap(e), precision=HIGHEST, preferred_element_type=F32)
-
-
-def y_kernel(left_ref, right_ref, lo_ref, hi_ref, dr_ref, e2_ref, h2_ref, inner_ref,
-             e_ref, h_ref, out_ref, gt_ref, dc_ref):
+    band = tap(cyclic(iota((n, rows), 1) - iota((n, rows), 0), rows))
+    along = jnp.dot(band, ext_ref[...], precision=HIGHEST, preferred_element_type=F32)
+    out_ref[...] = jnp.dot(along, tap(iota((m, m), 0) - iota((m, m), 1)), precision=HIGHEST, preferred_element_type=F32)
+    band_ref[...] = tap(cyclic(iota((rows, n), 0) - iota((rows, n), 1), rows))
+    k = iota(spread_ref.shape, 0)
+    column = jnp.where(k < FILT, m + k, jnp.where(k < 2 * FILT + 2, k - 2 * FILT, m - 1))
+    spread_ref[...] = jnp.where(k < 2 * FILT + 3, tap(column - iota(spread_ref.shape, 1)), 0.0)
+
+
+def y_kernel(left_ref, right_ref, lo_ref, hi_ref, dr_ref, e2_ref, h2_ref, inner_ref, band_ref, spread_ref,
+             e_hbm, h_hbm, out_hbm, gt_ref, dc_ref, out_ref, e_ref, h_ref, sems):
     n, m = inner_ref.shape
     right, left = right_ref[...], left_ref[...]
     rows = right.shape[1]
     a, b = seam_inputs(left, hi_ref[...], lo_ref[...], right)
     d = seam(1.0, a, b, lambda f: pltpu.roll(f, rows - 1, 1), lambda f: pltpu.roll(f, 1, 1))
-
-    gb0, gb1, ga = d["gb0"], d["gb1"], d["ga"]
-    top = iota((8, rows), 0)
-    gt_ref[0:8] = right[0:8] + jnp.where(top == 0, gb0[2:3], jnp.where(top == 1, gb1[2:3], 0.0))
-    gt_ref[8:16] = right[8:16]
-    gt_ref[16:24] = left[0:8]
-    gt_ref[24:32] = left[8:16] + jnp.where(top == 7, ga[0:1], 0.0)
-    gt_ref[32:40] = jnp.where(top == 0, gb0[0:1], jnp.where(top == 1, gb1[0:1], jnp.where(top == 2, ga[2:3], 0.0)))
 
     for f, field in enumerate(("e", "h")):
         for c, name in enumerate(("t", "n", "z")):
@@ -538,26 +523,33 @@
     columns = dc_ref[...].T
     lane = iota((n, 128), 1)
     sub = iota((8, m), 0)
-    for f, (src, dst) in enumerate(((e2_ref, e_ref), (h2_ref, h_ref))):
+    copies = []
+    for f, (src, ref, dst) in enumerate(((e2_ref, e_ref, e_hbm), (h2_ref, h_ref, h_hbm))):
         for c in range(3):
             for z in range(2):
                 p = 4 * (6 * f + 2 * c + z)
                 moved = pltpu.roll(columns, (126 - p) % 128, 1)
-                low = src[c, z, :, 0:128] + jnp.where(lane < 2, moved, 0.0)
-                high = src[c, z, :, m - 128 : m] + jnp.where(lane >= 126, moved, 0.0)
-                dst[c, z, :, 0:128] = low
-                dst[c, z, :, m - 128 : m] = high
-                dst[c, z, 0:8] += jnp.where(sub == 0, dr_ref[p + 2 : p + 3], jnp.where(sub == 1, dr_ref[p + 3 : p + 4], 0.0))
-                dst[c, z, n - 8 : n] += jnp.where(sub == 6, dr_ref[p : p + 1], jnp.where(sub == 7, dr_ref[p + 1 : p + 2], 0.0))
-
-    d = iota((rows, n), 0) - iota((rows, n), 1)
-    d = jnp.where(d > rows // 2, d - rows, jnp.where(d < -(rows // 2), d + rows, d))
-    along = jnp.dot(gt_ref[...], tap(d), precision=HIGHEST, preferred_element_type=F32)
-    k = iota((40, m), 0)
-    place = jnp.where(k < 16, m + k, jnp.where(k < 32, k - 32, jnp.where(k < 34, k - 32, m - 1)))
-    spread = jnp.where(k < 35, tap(place - iota((40, m), 1)), 0.0)
-    extra = lax.dot_general(along, spread, (((0,), (0,)), ((), ())), precision=HIGHEST, preferred_element_type=F32)
+                ref[c, z, :, 0:128] = src[c, z, :, 0:128] + jnp.where(lane < 2, moved, 0.0)
+                ref[c, z, :, m - 128 : m] = src[c, z, :, m - 128 : m] + jnp.where(lane >= 126, moved, 0.0)
+                ref[c, z, 0:8] += jnp.where(sub == 0, dr_ref[p + 2 : p + 3], jnp.where(sub == 1, dr_ref[p + 3 : p + 4], 0.0))
+                ref[c, z, n - 8 : n] += jnp.where(sub == 6, dr_ref[p : p + 1], jnp.where(sub == 7, dr_ref[p + 1 : p + 2], 0.0))
+            copies.append(pltpu.make_async_copy(ref.at[c], dst.at[c], sems.at[len(copies)]))
+            copies[-1].start()
+
+    gb0, gb1, ga = d["gb0"], d["gb1"], d["ga"]
+    top = iota((8, rows), 0)
+    gt_ref[0:8] = right[0:8] + jnp.where(top == 0, gb0[2:3], jnp.where(top == 1, gb1[2:3], 0.0))
+    gt_ref[8:16] = right[8:16]
+    gt_ref[16:24] = left[0:8]
+    gt_ref[24:32] = left[8:16] + jnp.where(top == 7, ga[0:1], 0.0)
+    gt_ref[32:40] = jnp.where(top == 0, gb0[0:1], jnp.where(top == 1, gb1[0:1], jnp.where(top == 2, ga[2:3], 0.0)))
+    along = jnp.dot(gt_ref[...], band_ref[...], precision=HIGHEST, preferred_element_type=F32)
+    extra = lax.dot_general(along, spread_ref[...], (((0,), (0,)), ((), ())), precision=HIGHEST, preferred_element_type=F32)
     out_ref[...] = inner_ref[...] + extra
+    copies.append(pltpu.make_async_copy(out_ref, out_hbm, sems.at[len(copies)]))
+    copies[-1].start()
+    for copy in copies:
+        copy.wait()
 
 
 def swap_pairs(count, which):
@@ -566,7 +558,7 @@
     return [(i, (i - 1) % count if i % 2 == 0 else (i + 1) % count) for i in range(count)]
 
 
-def call(kernel, shapes, ins, scratch=(), far=(), sems=0):
+def call(kernel, shapes, ins, scratch=(), far=(), sems=0, far_out=False):
     vmem = pl.BlockSpec(memory_space=pltpu.VMEM)
     hbm = pl.BlockSpec(memory_space=pltpu.HBM)
     smem = pl.BlockSpec(memory_space=pltpu.SMEM)
@@ -576,9 +568,9 @@
         scratches.append(pltpu.SemaphoreType.DMA((sems,)))
     return pl.pallas_call(
         kernel,
-        out_shape=[jax.ShapeDtypeStruct(s, F32) for s in shapes],
+        out_shape=[s if hasattr(s, "dtype") else jax.ShapeDtypeStruct(s, F32) for s in shapes],
         in_specs=[hbm if k in far else smem if x.shape == (NMAT,) else vmem for k, x in enumerate(ins)],
-        out_specs=[vmem] * len(shapes),
+        out_specs=[hbm if far_out else vmem] * len(shapes),
         scratch_shapes=scratches,
         compiler_params=pltpu.CompilerParams(vmem_limit_bytes=24 * 1024 * 1024),
     )(*ins)
@@ -587,14 +579,13 @@
 def body(adj_e, adj_h, fwd_e, labels, eps_table, density):
     n, m = labels.shape
     block = adj_e.shape
-    nz = block[1]
     ins = [adj_e, adj_h, fwd_e, labels, density, eps_table]
     message = (2 * LO_ROWS + 8, 128)
+    nz = block[1]
     strip = (2 * EXT, m)
-    edges = (3, nz, 2 * DONE, m)
-    xa, xb, lo, hi, *solved = call(
+    xa, xb, lo, hi, table = call(
         edge_kernel,
-        [message, message, (LO_ROWS, m), (HI_ROWS, m), edges, edges, (2 * DONE, m), (2 * DONE, 128)],
+        [message, message, (LO_ROWS, m), (HI_ROWS, m), (NMAT, m)],
         ins,
         [(3, nz, *strip), (3, nz, *strip), (STEPS, 3, nz, *strip), pltpu.VMEM(strip, jnp.int32), strip, pltpu.SMEM((NMAT,), F32)],
         range(6),
@@ -604,7 +595,7 @@
     got_a = lax.ppermute(xa, "gx", swap_pairs(gx, 0))
     got_b = lax.ppermute(xb, "gx", swap_pairs(gx, 1))
     plo, phi, grad, e2, h1 = call(
-        solve_kernel, [(LO_ROWS, n), (HI_ROWS, n), (n, m), block, block], ins + solved
+        solve_kernel, [(LO_ROWS, n), (HI_ROWS, n), (n, m), block, block], ins[:-1] + [table]
     )
     column = (LO_ROWS, 2 * n)
     yhi, ylo, ext, dr = call(
@@ -614,13 +605,15 @@
     )
     left = lax.ppermute(yhi, "gy", [(i, (i + 1) % gy) for i in range(gy)])
     right = lax.ppermute(ylo, "gy", [(i, (i - 1) % gy) for i in range(gy)])
-    inner, h2 = call(inner_kernel, [(n, m), block], [ext, e2, h1])
+    inner, h2, band, spread = call(inner_kernel, [(n, m), block, (2 * n, n), (40, m)], [ext, e2, h1])
     return tuple(
         call(
             y_kernel,
             [block, block, (n, m)],
-            [left, right, ylo, yhi, dr, e2, h2, inner],
-            [(40, 2 * n), (128, n)],
+            [left, right, ylo, yhi, dr, e2, h2, inner, band, spread],
+            [(40, 2 * n), (128, n), (n, m), block, block],
+            sems=7,
+            far_out=True,
         )
     )
 

time: 16.5 us -> 16.3 us (0.988)
  Pallas kernels: 6.69 us -> 6.34 us
    pallas_call x5, Pallas kernels: 6.69 us -> 6.34 us  [call(): pl.pallas_call(kernel, out_shape=[s if hasattr(s, 'dtype') else jax.Shape...]
    ppermute x1, waiting for transfers between devices: 0.26 us -> 0.43 us  [body(): got_b = lax.ppermute(xb, 'gx', swap_pairs(gx, 1))]
  transfers between devices with their start and end apart: 4 -> 4, of which waited for: 3 -> 3; matrix products, arithmetic and copies ran while one was open for 0% -> 0% of each run, Pallas kernels for 15% -> 14%
where the time goes in v5:
time: 16.3 us; the launch traced here: 16.1 us
  starting transfers between devices  7.01 us (43%)
  Pallas kernels  6.34 us (39%)
  waiting for transfers between devices  2.02 us (12%)
  between operations  0.72 us (4%)
    pallas_call x5, Pallas kernels, call(): pl.pallas_call(kernel, out_shape=[s if hasattr(s, 'dtype') else jax.Shape...  6.34 us
    ppermute x1, starting transfers between devices, body(): got_b = lax.ppermute(xb, 'gx', swap_pairs(gx, 1))  2.61 us
    ppermute x1, starting transfers between devices, body(): right = lax.ppermute(ylo, 'gy', [(i, (i - 1) % gy) for i in range(gy)])  2.25 us
    ppermute x1, starting transfers between devices, body(): left = lax.ppermute(yhi, 'gy', [(i, (i + 1) % gy) for i in range(gy)])  1.63 us
    ppermute x1, waiting for transfers between devices, body(): left = lax.ppermute(yhi, 'gy', [(i, (i + 1) % gy) for i in range(gy)])  1.32 us
    ppermute x1, starting transfers between devices, body(): got_a = lax.ppermute(xa, 'gx', swap_pairs(gx, 0))  0.52 us
    ppermute x1, waiting for transfers between devices, body(): got_b = lax.ppermute(xb, 'gx', swap_pairs(gx, 1))  0.43 us
  transfers between devices with their start and end apart: 4, of which 3 were waited for; matrix products, arithmetic and copies ran while one was open for 0% of the time, Pallas kernels for 14%

profile of v5, /device:TPU:0, one launch (start us, length us, event | category | flops | bytes accessed | tf_op | source)
XLA Modules:
  0.0 16.1 jit_solution(245357890015033361)
XLA Ops:
  0.6 0.0 copy-start.4
  0.6 0.0 copy-start.3
  0.7 0.0 copy-start
  0.7 0.0 copy-start.2
  0.7 0.0 copy-start.1
  0.7 2.0 %shard_map.85 = (f32[88,128]{1,0:T(8,128)S(1)}, f32[88,128]{1,0:T(8,128)S(1)}, f32[40,256]{1,0:T(8,128)S(1)}, f32[32,256]{1,0:T(8,128)S(1)}, f32[8,256]{1,0:T(8,128)S(1)}) custom-call(f32[3,2,128,256]{3,2,1,0:T(8,128)} %e_ref.1, f32[3,2,128,256]{3,2,1,0:T(8,128)} %h_ref.1, f32[2,3,2,128,256]{4,3,2,1,0:T(8,128)} %f_ref.1, s32[128,256]{1,0:T(8,128)} %lab_ref.1, ...), custom_call_target="tpu_custom_call" | custom-call | tf_op jit(solution)/shard_map/pallas_call | solution.py:569
  2.7 0.5 %collective-permute-start = (f32[88,128]{1,0:T(8,128)S(1)}, f32[88,128]{1,0:T(8,128)S(1)}, u32[]{:S(2)}, u32[]{:S(2)}) collective-permute-start(f32[88,128]{1,0:T(8,128)S(1)} %get-tuple-element.21), channel_id=1, source_target_pairs={{0,4},{4,0},{8,12},{12,8},{1,5},{5,1},{9,13},{13,9},{2,6},{6,2},{1... | collective-permute-start | bytes 135176 | tf_op jit(solution)/shard_map/ppermute | solution.py:595
  3.2 2.6 %collective-permute-start.1 = (f32[88,128]{1,0:T(8,128)S(1)}, f32[88,128]{1,0:T(8,128)S(1)}, u32[]{:S(2)}, u32[]{:S(2)}) collective-permute-start(f32[88,128]{1,0:T(8,128)S(1)} %get-tuple-element.22), channel_id=1, source_target_pairs={{0,12},{4,8},{8,4},{12,0},{1,13},{5,9},{9,5},{13,1},{2,14},{6,10},... | collective-permute-start | bytes 135176 | tf_op jit(solution)/shard_map/ppermute | solution.py:596
  5.8 0.0 copy-done.4
  5.8 0.0 copy-done.3
  5.8 0.0 copy-done
  5.8 0.0 copy-done.2
  5.8 0.0 copy-done.1
  5.8 1.5 %shard_map.86 = (f32[40,128]{1,0:T(8,128)S(1)}, f32[32,128]{1,0:T(8,128)S(1)}, f32[128,256]{1,0:T(8,128)S(1)}, f32[3,2,128,256]{3,2,1,0:T(8,128)S(1)}, f32[3,2,128,256]{3,2,1,0:T(8,128)S(1)}) custom-call(f32[3,2,128,256]{3,2,1,0:T(8,128)S(1)} %copy-done.1, f32[3,2,128,256]{3,2,1,0:T(8,128)S(1)} %copy-done.2, f32[2,3,2,128,256]{4,3,2,1,0:T(8,128)S(1)} %copy-done, ...), custom_call_target="tpu_custom_call" | custom-call | tf_op jit(solution)/shard_map/pallas_call | solution.py:569
  7.3 0.0 collective-permute-done.ra_ref
  7.3 0.4 %collective-permute-done.1.rb_ref = f32[88,128]{1,0:T(8,128)S(1)} collective-permute-done((f32[88,128]{1,0:T(8,128)S(1)}, f32[88,128]{1,0:T(8,128)S(1)}, u32[]{:S(2)}, u32[]{:S(2)}) %collective-permute-start.1) | collective-permute-done | bytes 45088 | tf_op jit(solution)/shard_map/ppermute | solution.py:596
  7.7 0.4 %shard_map.87 = (f32[40,256]{1,0:T(8,128)S(1)}, f32[40,256]{1,0:T(8,128)S(1)}, f32[256,256]{1,0:T(8,128)S(1)}, f32[48,256]{1,0:T(8,128)S(1)}) custom-call(f32[88,128]{1,0:T(8,128)S(1)} %collective-permute-done.ra_ref, f32[88,128]{1,0:T(8,128)S(1)} %collective-permute-done.1.rb_ref, f32[40,256]{1,0:T(8,128)S(1)} %get-tuple-element.23.lo_ref, ...), custom_call_target="tpu_custom_call" | custom-call | tf_op jit(solution)/shard_map/pallas_call | solution.py:569
  8.1 1.6 %collective-permute-start.2 = (f32[40,256]{1,0:T(8,128)S(1)}, f32[40,256]{1,0:T(8,128)S(1)}, u32[]{:S(2)}, u32[]{:S(2)}) collective-permute-start(f32[40,256]{1,0:T(8,128)S(1)} %get-tuple-element.29.hi_ref), channel_id=1, source_target_pairs={{0,1},{1,2},{2,3},{3,0},{4,5},{5,6},{6,7},{7,4},{8,9},{9,10},{10,1... | collective-permute-start | bytes 122888 | tf_op jit(solution)/shard_map/ppermute | solution.py:606
  9.8 2.3 %collective-permute-start.3 = (f32[40,256]{1,0:T(8,128)S(1)}, f32[40,256]{1,0:T(8,128)S(1)}, u32[]{:S(2)}, u32[]{:S(2)}) collective-permute-start(f32[40,256]{1,0:T(8,128)S(1)} %get-tuple-element.30.lo_ref), channel_id=1, source_target_pairs={{0,3},{1,0},{2,1},{3,2},{4,7},{5,4},{6,5},{7,6},{8,11},{9,8},{10,9... | collective-permute-start | bytes 122888 | tf_op jit(solution)/shard_map/ppermute | solution.py:607
  12.0 0.8 %shard_map.88 = (f32[128,256]{1,0:T(8,128)S(1)}, f32[3,2,128,256]{3,2,1,0:T(8,128)S(1)}, f32[256,128]{1,0:T(8,128)S(1)}, f32[40,256]{1,0:T(8,128)S(1)}) custom-call(f32[256,256]{1,0:T(8,128)S(1)} %get-tuple-element.33.ext_ref, f32[3,2,128,256]{3,2,1,0:T(8,128)S(1)} %get-tuple-element.32.e2_ref, f32[3,2,128,256]{3,2,1,0:T(8,128)S(1)} %get-tuple-element.34.h1_ref), custom_call_target="tpu_custom_call" | custom-call | tf_op jit(solution)/shard_map/pallas_call | solution.py:569
  12.8 1.3 %collective-permute-done.2.left_ref = f32[40,256]{1,0:T(8,128)S(1)} collective-permute-done((f32[40,256]{1,0:T(8,128)S(1)}, f32[40,256]{1,0:T(8,128)S(1)}, u32[]{:S(2)}, u32[]{:S(2)}) %collective-permute-start.2) | collective-permute-done | bytes 40992 | tf_op jit(solution)/shard_map/ppermute | solution.py:606
  14.1 0.3 %collective-permute-done.3.right_ref = f32[40,256]{1,0:T(8,128)S(1)} collective-permute-done((f32[40,256]{1,0:T(8,128)S(1)}, f32[40,256]{1,0:T(8,128)S(1)}, u32[]{:S(2)}, u32[]{:S(2)}) %collective-permute-start.3) | collective-permute-done | bytes 40992 | tf_op jit(solution)/shard_map/ppermute | solution.py:607
  14.4 1.7 %shard_map.89 = (f32[3,2,128,256]{3,2,1,0:T(8,128)}, f32[3,2,128,256]{3,2,1,0:T(8,128)}, f32[128,256]{1,0:T(8,128)}) custom-call(f32[40,256]{1,0:T(8,128)S(1)} %collective-permute-done.2.left_ref, f32[40,256]{1,0:T(8,128)S(1)} %collective-permute-done.3.right_ref, f32[40,256]{1,0:T(8,128)S(1)} %get-tuple-element.30.lo_ref, ...), custom_call_target="tpu_custom_call" | custom-call | tf_op jit(solution)/shard_map/pallas_call | solution.py:569
Async XLA Ops:
  0.6 5.2 %copy-start.4 = (f32[128,256]{1,0:T(8,128)S(1)}, f32[128,256]{1,0:T(8,128)}, u32[]{:S(2)}) copy-start(f32[128,256]{1,0:T(8,128)} %den_ref.1) | copy-start | bytes 393220
  0.6 5.2 %copy-start.3 = (s32[128,256]{1,0:T(8,128)S(1)}, s32[128,256]{1,0:T(8,128)}, u32[]{:S(2)}) copy-start(s32[128,256]{1,0:T(8,128)} %lab_ref.1) | copy-start | bytes 393220
  0.7 5.2 %copy-start = (f32[2,3,2,128,256]{4,3,2,1,0:T(8,128)S(1)}, f32[2,3,2,128,256]{4,3,2,1,0:T(8,128)}, u32[]{:S(2)}) copy-start(f32[2,3,2,128,256]{4,3,2,1,0:T(8,128)} %f_ref.1) | copy-start | bytes 4718596
  0.7 5.2 %copy-start.2 = (f32[3,2,128,256]{3,2,1,0:T(8,128)S(1)}, f32[3,2,128,256]{3,2,1,0:T(8,128)}, u32[]{:S(2)}) copy-start(f32[3,2,128,256]{3,2,1,0:T(8,128)} %h_ref.1) | copy-start | bytes 2359300
  0.7 5.1 %copy-start.1 = (f32[3,2,128,256]{3,2,1,0:T(8,128)S(1)}, f32[3,2,128,256]{3,2,1,0:T(8,128)}, u32[]{:S(2)}) copy-start(f32[3,2,128,256]{3,2,1,0:T(8,128)} %e_ref.1) | copy-start | bytes 2359300
  2.7 4.6 %collective-permute-start = (f32[88,128]{1,0:T(8,128)S(1)}, f32[88,128]{1,0:T(8,128)S(1)}, u32[]{:S(2)}, u32[]{:S(2)}) collective-permute-start(f32[88,128]{1,0:T(8,128)S(1)} %get-tuple-element.21), channel_id=1, source_target_pairs={{0,4},{4,0},{8,12},{12,8},{1,5},{5,1},{9,13},{13,9},{2,6},{6,2},{1... | collective-permute-start | bytes 135176 | tf_op jit(solution)/shard_map/ppermute | solution.py:595
  3.2 4.5 %collective-permute-start.1 = (f32[88,128]{1,0:T(8,128)S(1)}, f32[88,128]{1,0:T(8,128)S(1)}, u32[]{:S(2)}, u32[]{:S(2)}) collective-permute-start(f32[88,128]{1,0:T(8,128)S(1)} %get-tuple-element.22), channel_id=1, source_target_pairs={{0,12},{4,8},{8,4},{12,0},{1,13},{5,9},{9,5},{13,1},{2,14},{6,10},... | collective-permute-start | bytes 135176 | tf_op jit(solution)/shard_map/ppermute | solution.py:596
  8.1 6.0 %collective-permute-start.2 = (f32[40,256]{1,0:T(8,128)S(1)}, f32[40,256]{1,0:T(8,128)S(1)}, u32[]{:S(2)}, u32[]{:S(2)}) collective-permute-start(f32[40,256]{1,0:T(8,128)S(1)} %get-tuple-element.29.hi_ref), channel_id=1, source_target_pairs={{0,1},{1,2},{2,3},{3,0},{4,5},{5,6},{6,7},{7,4},{8,9},{9,10},{10,1... | collective-permute-start | bytes 122888 | tf_op jit(solution)/shard_map/ppermute | solution.py:606
  9.8 4.6 %collective-permute-start.3 = (f32[40,256]{1,0:T(8,128)S(1)}, f32[40,256]{1,0:T(8,128)S(1)}, u32[]{:S(2)}, u32[]{:S(2)}) collective-permute-start(f32[40,256]{1,0:T(8,128)S(1)} %get-tuple-element.30.lo_ref), channel_id=1, source_target_pairs={{0,3},{1,0},{2,1},{3,2},{4,7},{5,4},{6,5},{7,6},{8,11},{9,8},{10,9... | collective-permute-start | bytes 122888 | tf_op jit(solution)/shard_map/ppermute | solution.py:607

commit v6 on v5

--- a/solution.py
+++ b/solution.py
@@ -40,6 +40,7 @@
     + [PACK_R, PACK_END]
 )
 CORNER = PACK_END - PACK_F1
+REACH = FILT + 2
 
 
 def tap(distance):
@@ -280,11 +281,15 @@
     return pack
 
 
+def saved_scale(ratio):
+    return jnp.where(iota((ratio.shape[0], 128), 1) == 0, 1.0, fold(ratio, ratio))
+
+
 def pack_saved(pack, ratio, fwd):
     lane = iota(pack.shape, 1)
     for j, (c, z) in enumerate((c, z) for c in (0, 2) for z in range(2)):
         pack = jnp.where(lane == PACK_F0 + j, pltpu.roll(fwd[0][c][z][:, 0:128], PACK_F0 + j, 1), pack)
-    scale = jnp.where(lane == 0, 1.0, fold(ratio, ratio))
+    scale = saved_scale(ratio)
     for k, (c, z) in enumerate((c, z) for c in range(3) for z in range(2)):
         pack = place(pack, fold(fwd[1][c][z], fwd[1][c][z]) * scale, PACK_F1 + 3 * k)
     return pack
@@ -333,14 +338,33 @@
     e1 = less(planes(e_ref), change)
     h1 = magnetic(e1, h0)
     e2 = less(e1, turn(h1, ratio))
-    pack = pack_fields(jnp.zeros((2 * EXT, 128), F32), ratio, e1, h0, h1, e2)
+    lane = iota((8, 128), 1)
+    corners = [[jnp.zeros((8, 128), F32) for _ in range(3)] for _ in range(2)]
+
+    def put_corner(values, base, first=0, count=3):
+        for end in range(2):
+            for k in range(3):
+                at = CORNER * k + base - PACK_F1
+                tile = values[EXT * end + 8 * k : EXT * end + 8 * k + 8]
+                moved = pltpu.roll(tile, (at + 1) % 128, 1)
+                corners[end][k] = jnp.where((lane >= at + first) & (lane < at + count), moved, corners[end][k])
+
+    sides = [(c, z) for c in (0, 2) for z in range(nz)]
+    put_corner(fold(ratio, ratio), PACK_R)
+    for j, (c, z) in enumerate(sides):
+        put_corner(fold(e1[c][z], h0[c][z]), PACK_PAIR + 2 * j, 0, 2)
+        put_corner(h1[c][z][:, m - 128 : m], PACK_PAIR + 8 + 2 * j, 0, 1)
     wait(9, 11)
     fwd = [planes(f_ref, 0)]
     grad = product(e1, fwd[0])
+    for j, (c, z) in enumerate(sides):
+        put_corner(fwd[0][c][z][:, 0:128], PACK_F0 + j - 1, 1, 2)
     wait(11, 13)
     fwd.append(planes(f_ref, 1))
     grad = grad + product(e2, fwd[1])
-    pack = pack_saved(pack, ratio, fwd)
+    scale = saved_scale(ratio)
+    for k, (c, z) in enumerate((c, z) for c in range(3) for z in range(nz)):
+        put_corner(fold(fwd[1][c][z], fwd[1][c][z]) * scale, PACK_F1 + 3 * k)
     rows = 2 * EXT
 
     def line(item, at):
@@ -355,16 +379,10 @@
         for k, (item, at) in enumerate(group):
             ref[FILT + k : FILT + k + 1] = line(item, at)
     hi_ref[HI_ROWS - 1 : HI_ROWS] = jnp.zeros((1, m), F32)
-    lane = iota((8, 128), 1)
-
-    def corner(part):
-        out = pltpu.roll(part[0:8], 128 - PACK_F1, 1)
-        for k in range(1, 3):
-            out = jnp.where(lane < CORNER * k, out, pltpu.roll(part[8 * k : 8 * k + 8], CORNER * k - PACK_F1, 1))
-        return out
-
     first_even = even("gx")
-    lo_corner, hi_corner = corner(pack[0:EXT]), corner(pack[EXT:rows])
+    lo_corner, hi_corner = (
+        jnp.where(lane < CORNER, part[0], jnp.where(lane < 2 * CORNER, part[1], part[2])) for part in corners
+    )
     for half in range(2):
         at, cols = half * LO_ROWS, slice(128 * half, 128 * half + 128)
         low, high = lo_ref[:, cols], hi_ref[:, cols]
@@ -392,7 +410,7 @@
 
 
 def x_kernel(ra_ref, rb_ref, lo_ref, hi_ref, plo_ref, phi_ref, grad_ref,
-             yhi_ref, ylo_ref, ext_ref, dr_ref):
+             yhi_ref, down_ref, ylo_ref, ext_ref, dr_ref):
     n, m = grad_ref.shape
     first_even = even("gx")
     got_right = jnp.where(first_even, ra_ref[...], rb_ref[...])
@@ -477,7 +495,11 @@
         at = iota((count, n), 1)
         moved = pltpu.roll(ref[0:count, n : 2 * n], (n - EXT - 1) % n, 1)
         ref[0:count, 0:n] = mine[...] + jnp.where((at < 2) | (at == n - 1), moved, 0.0)
-    yhi_ref[HI_ROWS:LO_ROWS] = jnp.zeros((LO_ROWS - HI_ROWS, 2 * n), F32)
+    down_ref[0:LO_ROWS] = ylo_ref[:, 0:n]
+    for k in range(LO_ROWS // 8):
+        moved = pltpu.roll(ylo_ref[8 * k : 8 * k + 8, n : 2 * n], REACH + 2 * REACH * (k % 3), 1)
+        at = LO_ROWS + 8 * (k // 3)
+        down_ref[at : at + 8] = moved if k % 3 == 0 else jnp.where(wide < 2 * REACH * (k % 3), down_ref[at : at + 8], moved)
 
 
 def cyclic(d, count):
@@ -505,8 +527,15 @@
 def y_kernel(left_ref, right_ref, lo_ref, hi_ref, dr_ref, e2_ref, h2_ref, inner_ref, band_ref, spread_ref,
              e_hbm, h_hbm, out_hbm, gt_ref, dc_ref, out_ref, e_ref, h_ref, sems):
     n, m = inner_ref.shape
-    right, left = right_ref[...], left_ref[...]
-    rows = right.shape[1]
+    left = left_ref[...]
+    rows = left.shape[1]
+    tile_lane = iota((8, 128), 1)
+    outer = []
+    for k in range(LO_ROWS // 8):
+        at = LO_ROWS + 8 * (k // 3)
+        moved = pltpu.roll(right_ref[at : at + 8], 128 - REACH - 2 * REACH * (k % 3), 1)
+        outer.append(jnp.where((tile_lane < REACH) | (tile_lane >= 128 - REACH), moved, 0.0))
+    right = jnp.concatenate([right_ref[0:LO_ROWS], jnp.concatenate(outer, axis=0)], axis=1)
     a, b = seam_inputs(left, hi_ref[...], lo_ref[...], right)
     d = seam(1.0, a, b, lambda f: pltpu.roll(f, rows - 1, 1), lambda f: pltpu.roll(f, 1, 1))
 
@@ -533,8 +562,8 @@
                 ref[c, z, :, m - 128 : m] = src[c, z, :, m - 128 : m] + jnp.where(lane >= 126, moved, 0.0)
                 ref[c, z, 0:8] += jnp.where(sub == 0, dr_ref[p + 2 : p + 3], jnp.where(sub == 1, dr_ref[p + 3 : p + 4], 0.0))
                 ref[c, z, n - 8 : n] += jnp.where(sub == 6, dr_ref[p : p + 1], jnp.where(sub == 7, dr_ref[p + 1 : p + 2], 0.0))
-            copies.append(pltpu.make_async_copy(ref.at[c], dst.at[c], sems.at[len(copies)]))
-            copies[-1].start()
+                copies.append(pltpu.make_async_copy(ref.at[c, z], dst.at[c, z], sems.at[len(copies)]))
+                copies[-1].start()
 
     gb0, gb1, ga = d["gb0"], d["gb1"], d["ga"]
     top = iota((8, rows), 0)
@@ -597,14 +626,13 @@
     plo, phi, grad, e2, h1 = call(
         solve_kernel, [(LO_ROWS, n), (HI_ROWS, n), (n, m), block, block], ins[:-1] + [table]
     )
-    column = (LO_ROWS, 2 * n)
-    yhi, ylo, ext, dr = call(
+    yhi, down, ylo, ext, dr = call(
         x_kernel,
-        [column, column, (2 * n, m), (48, m)],
+        [(HI_ROWS, 2 * n), (LO_ROWS + 16, n), (LO_ROWS, 2 * n), (2 * n, m), (48, m)],
         [got_a, got_b, lo, hi, plo, phi, grad],
     )
     left = lax.ppermute(yhi, "gy", [(i, (i + 1) % gy) for i in range(gy)])
-    right = lax.ppermute(ylo, "gy", [(i, (i - 1) % gy) for i in range(gy)])
+    right = lax.ppermute(down, "gy", [(i, (i - 1) % gy) for i in range(gy)])
     inner, h2, band, spread = call(inner_kernel, [(n, m), block, (2 * n, n), (40, m)], [ext, e2, h1])
     return tuple(
         call(
@@ -612,7 +640,7 @@
             [block, block, (n, m)],
             [left, right, ylo, yhi, dr, e2, h2, inner, band, spread],
             [(40, 2 * n), (128, n), (n, m), block, block],
-            sems=7,
+            sems=13,
             far_out=True,
         )
     )

time: 16.3 us -> 16 us (0.982)
  waiting for transfers between devices: 2.02 us -> 1.72 us
    ppermute x1, waiting for transfers between devices: 1.32 us -> 0.01 us  [body(): left = lax.ppermute(yhi, 'gy', [(i, (i + 1) % gy) for i in range(gy)])]
    ppermute x1, waiting for transfers between devices: 0.27 us -> 1.28 us  [body(): right = lax.ppermute(down, 'gy', [(i, (i - 1) % gy) for i in range(gy)])]
  transfers between devices with their start and end apart: 4 -> 4, of which waited for: 3 -> 2; matrix products, arithmetic and copies ran while one was open for 0% -> 0% of each run, Pallas kernels for 14% -> 14%
where the time goes in v6:
time: 16 us; the launch traced here: 15.9 us
  starting transfers between devices  7.01 us (44%)
  Pallas kernels  6.39 us (40%)
  waiting for transfers between devices  1.72 us (11%)
  between operations  0.72 us (4%)
    pallas_call x5, Pallas kernels, call(): pl.pallas_call(kernel, out_shape=[s if hasattr(s, 'dtype') else jax.Shape...  6.39 us
    ppermute x1, starting transfers between devices, body(): got_b = lax.ppermute(xb, 'gx', swap_pairs(gx, 1))  2.61 us
    ppermute x1, starting transfers between devices, body(): right = lax.ppermute(down, 'gy', [(i, (i - 1) % gy) for i in range(gy)])  2.25 us
    ppermute x1, starting transfers between devices, body(): left = lax.ppermute(yhi, 'gy', [(i, (i + 1) % gy) for i in range(gy)])  1.63 us
    ppermute x1, waiting for transfers between devices, body(): right = lax.ppermute(down, 'gy', [(i, (i - 1) % gy) for i in range(gy)])  1.28 us
    ppermute x1, starting transfers between devices, body(): got_a = lax.ppermute(xa, 'gx', swap_pairs(gx, 0))  0.52 us
    ppermute x1, waiting for transfers between devices, body(): got_b = lax.ppermute(xb, 'gx', swap_pairs(gx, 1))  0.43 us
  transfers between devices with their start and end apart: 4, of which 2 were waited for; matrix products, arithmetic and copies ran while one was open for 0% of the time, Pallas kernels for 14%

profile of v6, /device:TPU:0, one launch (start us, length us, event | category | flops | bytes accessed | tf_op | source)
XLA Modules:
  0.0 15.9 jit_solution(13391698830660029272)
XLA Ops:
  0.6 0.0 copy-start.4
  0.6 0.0 copy-start.3
  0.7 0.0 copy-start
  0.7 0.0 copy-start.2
  0.7 0.0 copy-start.1
  0.7 1.9 %shard_map.85 = (f32[88,128]{1,0:T(8,128)S(1)}, f32[88,128]{1,0:T(8,128)S(1)}, f32[40,256]{1,0:T(8,128)S(1)}, f32[32,256]{1,0:T(8,128)S(1)}, f32[8,256]{1,0:T(8,128)S(1)}) custom-call(f32[3,2,128,256]{3,2,1,0:T(8,128)} %e_ref.1, f32[3,2,128,256]{3,2,1,0:T(8,128)} %h_ref.1, f32[2,3,2,128,256]{4,3,2,1,0:T(8,128)} %f_ref.1, s32[128,256]{1,0:T(8,128)} %lab_ref.1, ...), custom_call_target="tpu_custom_call" | custom-call | tf_op jit(solution)/shard_map/pallas_call | solution.py:598
  2.6 0.5 %collective-permute-start = (f32[88,128]{1,0:T(8,128)S(1)}, f32[88,128]{1,0:T(8,128)S(1)}, u32[]{:S(2)}, u32[]{:S(2)}) collective-permute-start(f32[88,128]{1,0:T(8,128)S(1)} %get-tuple-element.22), channel_id=1, source_target_pairs={{0,4},{4,0},{8,12},{12,8},{1,5},{5,1},{9,13},{13,9},{2,6},{6,2},{1... | collective-permute-start | bytes 135176 | tf_op jit(solution)/shard_map/ppermute | solution.py:624
  3.2 2.6 %collective-permute-start.1 = (f32[88,128]{1,0:T(8,128)S(1)}, f32[88,128]{1,0:T(8,128)S(1)}, u32[]{:S(2)}, u32[]{:S(2)}) collective-permute-start(f32[88,128]{1,0:T(8,128)S(1)} %get-tuple-element.23), channel_id=1, source_target_pairs={{0,12},{4,8},{8,4},{12,0},{1,13},{5,9},{9,5},{13,1},{2,14},{6,10},... | collective-permute-start | bytes 135176 | tf_op jit(solution)/shard_map/ppermute | solution.py:625
  5.8 0.0 copy-done.4
  5.8 0.0 copy-done.3
  5.8 0.0 copy-done
  5.8 0.0 copy-done.2
  5.8 0.0 copy-done.1
  5.8 1.5 %shard_map.86 = (f32[40,128]{1,0:T(8,128)S(1)}, f32[32,128]{1,0:T(8,128)S(1)}, f32[128,256]{1,0:T(8,128)S(1)}, f32[3,2,128,256]{3,2,1,0:T(8,128)S(1)}, f32[3,2,128,256]{3,2,1,0:T(8,128)S(1)}) custom-call(f32[3,2,128,256]{3,2,1,0:T(8,128)S(1)} %copy-done.1, f32[3,2,128,256]{3,2,1,0:T(8,128)S(1)} %copy-done.2, f32[2,3,2,128,256]{4,3,2,1,0:T(8,128)S(1)} %copy-done, ...), custom_call_target="tpu_custom_call" | custom-call | tf_op jit(solution)/shard_map/pallas_call | solution.py:598
  7.3 0.0 collective-permute-done.ra_ref
  7.3 0.4 %collective-permute-done.1.rb_ref = f32[88,128]{1,0:T(8,128)S(1)} collective-permute-done((f32[88,128]{1,0:T(8,128)S(1)}, f32[88,128]{1,0:T(8,128)S(1)}, u32[]{:S(2)}, u32[]{:S(2)}) %collective-permute-start.1) | collective-permute-done | bytes 45088 | tf_op jit(solution)/shard_map/ppermute | solution.py:625
  7.7 0.4 %shard_map.87 = (f32[32,256]{1,0:T(8,128)S(1)}, f32[56,128]{1,0:T(8,128)S(1)}, f32[40,256]{1,0:T(8,128)S(1)}, f32[256,256]{1,0:T(8,128)S(1)}, f32[48,256]{1,0:T(8,128)S(1)}) custom-call(f32[88,128]{1,0:T(8,128)S(1)} %collective-permute-done.ra_ref, f32[88,128]{1,0:T(8,128)S(1)} %collective-permute-done.1.rb_ref, f32[40,256]{1,0:T(8,128)S(1)} %get-tuple-element.24.lo_ref, ...), custom_call_target="tpu_custom_call" | custom-call | tf_op jit(solution)/shard_map/pallas_call | solution.py:598
  8.1 1.6 %collective-permute-start.2 = (f32[32,256]{1,0:T(8,128)S(1)}, f32[32,256]{1,0:T(8,128)S(1)}, u32[]{:S(2)}, u32[]{:S(2)}) collective-permute-start(f32[32,256]{1,0:T(8,128)S(1)} %get-tuple-element.30.hi_ref), channel_id=1, source_target_pairs={{0,1},{1,2},{2,3},{3,0},{4,5},{5,6},{6,7},{7,4},{8,9},{9,10},{10,1... | collective-permute-start | bytes 98312 | tf_op jit(solution)/shard_map/ppermute | solution.py:634
  9.7 2.3 %collective-permute-start.3 = (f32[56,128]{1,0:T(8,128)S(1)}, f32[56,128]{1,0:T(8,128)S(1)}, u32[]{:S(2)}, u32[]{:S(2)}) collective-permute-start(f32[56,128]{1,0:T(8,128)S(1)} %get-tuple-element.31), channel_id=1, source_target_pairs={{0,3},{1,0},{2,1},{3,2},{4,7},{5,4},{6,5},{7,6},{8,11},{9,8},{10,9... | collective-permute-start | bytes 86024 | tf_op jit(solution)/shard_map/ppermute | solution.py:635
  12.0 0.8 %shard_map.88 = (f32[128,256]{1,0:T(8,128)S(1)}, f32[3,2,128,256]{3,2,1,0:T(8,128)S(1)}, f32[256,128]{1,0:T(8,128)S(1)}, f32[40,256]{1,0:T(8,128)S(1)}) custom-call(f32[256,256]{1,0:T(8,128)S(1)} %get-tuple-element.35.ext_ref, f32[3,2,128,256]{3,2,1,0:T(8,128)S(1)} %get-tuple-element.34.e2_ref, f32[3,2,128,256]{3,2,1,0:T(8,128)S(1)} %get-tuple-element.36.h1_ref), custom_call_target="tpu_custom_call" | custom-call | tf_op jit(solution)/shard_map/pallas_call | solution.py:598
  12.8 1.3 %collective-permute-done.3.right_ref = f32[56,128]{1,0:T(8,128)S(1)} collective-permute-done((f32[56,128]{1,0:T(8,128)S(1)}, f32[56,128]{1,0:T(8,128)S(1)}, u32[]{:S(2)}, u32[]{:S(2)}) %collective-permute-start.3) | collective-permute-done | bytes 28704 | tf_op jit(solution)/shard_map/ppermute | solution.py:635
  14.1 0.0 collective-permute-done.2.left_ref
  14.1 1.8 %shard_map.89 = (f32[3,2,128,256]{3,2,1,0:T(8,128)}, f32[3,2,128,256]{3,2,1,0:T(8,128)}, f32[128,256]{1,0:T(8,128)}) custom-call(f32[32,256]{1,0:T(8,128)S(1)} %collective-permute-done.2.left_ref, f32[56,128]{1,0:T(8,128)S(1)} %collective-permute-done.3.right_ref, f32[40,256]{1,0:T(8,128)S(1)} %get-tuple-element.32.lo_ref, ...), custom_call_target="tpu_custom_call" | custom-call | tf_op jit(solution)/shard_map/pallas_call | solution.py:598
Async XLA Ops:
  0.6 5.1 %copy-start.4 = (f32[128,256]{1,0:T(8,128)S(1)}, f32[128,256]{1,0:T(8,128)}, u32[]{:S(2)}) copy-start(f32[128,256]{1,0:T(8,128)} %den_ref.1) | copy-start | bytes 393220
  0.6 5.1 %copy-start.3 = (s32[128,256]{1,0:T(8,128)S(1)}, s32[128,256]{1,0:T(8,128)}, u32[]{:S(2)}) copy-start(s32[128,256]{1,0:T(8,128)} %lab_ref.1) | copy-start | bytes 393220
  0.7 5.1 %copy-start = (f32[2,3,2,128,256]{4,3,2,1,0:T(8,128)S(1)}, f32[2,3,2,128,256]{4,3,2,1,0:T(8,128)}, u32[]{:S(2)}) copy-start(f32[2,3,2,128,256]{4,3,2,1,0:T(8,128)} %f_ref.1) | copy-start | bytes 4718596
  0.7 5.1 %copy-start.2 = (f32[3,2,128,256]{3,2,1,0:T(8,128)S(1)}, f32[3,2,128,256]{3,2,1,0:T(8,128)}, u32[]{:S(2)}) copy-start(f32[3,2,128,256]{3,2,1,0:T(8,128)} %h_ref.1) | copy-start | bytes 2359300
  0.7 5.1 %copy-start.1 = (f32[3,2,128,256]{3,2,1,0:T(8,128)S(1)}, f32[3,2,128,256]{3,2,1,0:T(8,128)}, u32[]{:S(2)}) copy-start(f32[3,2,128,256]{3,2,1,0:T(8,128)} %e_ref.1) | copy-start | bytes 2359300
  2.6 4.6 %collective-permute-start = (f32[88,128]{1,0:T(8,128)S(1)}, f32[88,128]{1,0:T(8,128)S(1)}, u32[]{:S(2)}, u32[]{:S(2)}) collective-permute-start(f32[88,128]{1,0:T(8,128)S(1)} %get-tuple-element.22), channel_id=1, source_target_pairs={{0,4},{4,0},{8,12},{12,8},{1,5},{5,1},{9,13},{13,9},{2,6},{6,2},{1... | collective-permute-start | bytes 135176 | tf_op jit(solution)/shard_map/ppermute | solution.py:624
  3.2 4.5 %collective-permute-start.1 = (f32[88,128]{1,0:T(8,128)S(1)}, f32[88,128]{1,0:T(8,128)S(1)}, u32[]{:S(2)}, u32[]{:S(2)}) collective-permute-start(f32[88,128]{1,0:T(8,128)S(1)} %get-tuple-element.23), channel_id=1, source_target_pairs={{0,12},{4,8},{8,4},{12,0},{1,13},{5,9},{9,5},{13,1},{2,14},{6,10},... | collective-permute-start | bytes 135176 | tf_op jit(solution)/shard_map/ppermute | solution.py:625
  8.1 6.0 %collective-permute-start.2 = (f32[32,256]{1,0:T(8,128)S(1)}, f32[32,256]{1,0:T(8,128)S(1)}, u32[]{:S(2)}, u32[]{:S(2)}) collective-permute-start(f32[32,256]{1,0:T(8,128)S(1)} %get-tuple-element.30.hi_ref), channel_id=1, source_target_pairs={{0,1},{1,2},{2,3},{3,0},{4,5},{5,6},{6,7},{7,4},{8,9},{9,10},{10,1... | collective-permute-start | bytes 98312 | tf_op jit(solution)/shard_map/ppermute | solution.py:634
  9.7 4.3 %collective-permute-start.3 = (f32[56,128]{1,0:T(8,128)S(1)}, f32[56,128]{1,0:T(8,128)S(1)}, u32[]{:S(2)}, u32[]{:S(2)}) collective-permute-start(f32[56,128]{1,0:T(8,128)S(1)} %get-tuple-element.31), channel_id=1, source_target_pairs={{0,3},{1,0},{2,1},{3,2},{4,7},{5,4},{6,5},{7,6},{8,11},{9,8},{10,9... | collective-permute-start | bytes 86024 | tf_op jit(solution)/shard_map/ppermute | solution.py:635

commit v7 on v5

v7 whole, which is shorter than its diff:
```python
import math

import jax
import jax.numpy as jnp
from jax import lax
from jax.experimental import pallas as pl
from jax.experimental.pallas import tpu as pltpu
from jax.sharding import PartitionSpec as P

STEPS = 2
NMAT = 8
FILT = 16

courant = 0.5
spread_ratio = 0.6

F32 = jnp.float32

LO_G, LO_E1T, LO_E1Z, LO_E2T, LO_E2Z = 0, 16, 18, 20, 22
LO_F0T, LO_F0Z, LO_F1T, LO_F1N, LO_F1Z = 24, 26, 28, 30, 32
LO_W1T, LO_W1Z, LO_R0, LO_R1, LO_ROWS = 34, 36, 38, 39, 40
HI_G, HI_H0T, HI_H0Z, HI_H1T, HI_H1Z = 0, 16, 18, 20, 22
HI_WT, HI_WN, HI_WZ, HI_R, HI_ROWS = 24, 26, 28, 30, 32
PACK_F1, PACK_R, PACK_PAIR, PACK_F0, PACK_END = 16, 34, 37, 53, 57
LO_LANES = (
    list(range(FILT))
    + [PACK_PAIR + 2 * j + 1 for j in range(8)]
    + [PACK_F0 + j for j in range(4)]
    + [PACK_F1 + 3 * k + 1 for k in range(6)]
    + [PACK_F1 + 3 * k + 2 for k in (0, 1, 4, 5)]
    + [PACK_R + 1, PACK_R + 2]
)
HI_LANES = (
    list(range(128 - FILT, 128))
    + [PACK_PAIR + 2 * j for j in range(8)]
    + [PACK_F1 + 3 * k for k in range(6)]
    + [PACK_R, PACK_END]
)
REACH = FILT + 2
GROUP = 24
EDGE = 24
LO_REST, HI_REST = LO_ROWS - FILT, HI_ROWS - FILT - 1

TURN_G, TURN_OWN, TURN_X = 48, 80, 88


def filter_taps():
    spread = spread_ratio * FILT
    norm = math.sqrt(sum(math.exp(-d * d / (spread * spread)) for d in range(-FILT, FILT + 1)))
    return [math.exp(-d * d / (2.0 * spread * spread)) / norm for d in range(FILT + 1)]


def tap(distance):
    spread = spread_ratio * FILT
    norm = math.sqrt(sum(math.exp(-d * d / (spread * spread)) for d in range(-FILT, FILT + 1)))
    far = distance.astype(F32)
    value = jnp.exp(-far * far / (2.0 * spread * spread)) / norm
    return jnp.where(jnp.abs(distance) <= FILT, value, F32(0.0))


def halves(x):
    high = x.astype(jnp.bfloat16)
    return high, (x - high.astype(F32)).astype(jnp.bfloat16)


def dot3(a, b):
    terms = [jnp.dot(x, y, preferred_element_type=F32) for x, y in ((a[0], b[1]), (a[1], b[0]), (a[0], b[0]))]
    return terms[0] + terms[1] + terms[2]


def iota(shape, dim):
    return lax.broadcasted_iota(jnp.int32, shape, dim)


def updates(n, m, nz):
    row, col = iota((n, m), 0), iota((n, m), 1)

    def lx(f):
        return jnp.where(row == 0, 0.0, pltpu.roll(f, 1, 0))

    def ux(f):
        return jnp.where(row == n - 1, 0.0, pltpu.roll(f, n - 1, 0))

    def ly(f):
        return jnp.where(col == 0, 0.0, pltpu.roll(f, 1, 1))

    def uy(f):
        return jnp.where(col == m - 1, 0.0, pltpu.roll(f, m - 1, 1))

    def turn(h, ratio):
        out = [[None] * nz for _ in range(3)]
        for z in range(nz):
            hx, hy, hz = h[0][z], h[1][z], h[2][z]
            dzx = hx - h[0][z - 1] if z > 0 else hx
            dzy = hy - h[1][z - 1] if z > 0 else hy
            out[0][z] = ratio * ((hz - ly(hz)) - dzy)
            out[1][z] = ratio * (dzx - (hz - lx(hz)))
            out[2][z] = ratio * ((hy - lx(hy)) - (hx - ly(hx)))
        return out

    def magnetic(e, h):
        out = [[None] * nz for _ in range(3)]
        for z in range(nz):
            ex, ey, ez = e[0][z], e[1][z], e[2][z]
            dzx = e[0][z + 1] - ex if z < nz - 1 else -ex
            dzy = e[1][z + 1] - ey if z < nz - 1 else -ey
            out[0][z] = h[0][z] + courant * ((uy(ez) - ez) - dzy)
            out[1][z] = h[1][z] + courant * (dzx - (ux(ez) - ez))
            out[2][z] = h[2][z] + courant * ((ux(ey) - ey) - (uy(ex) - ex))
        return out

    return turn, magnetic


def less(e, change):
    return [[a - b for a, b in zip(one, other, strict=True)] for one, other in zip(e, change, strict=True)]


def product(e, f):
    total = None
    for c in range(3):
        for z in range(len(e[c])):
            term = e[c][z] * f[c][z]
            total = term if total is None else total + term
    return total


def local_solve(e0, h0, saved, ratio):
    turn, magnetic = updates(*ratio.shape, len(e0[0]))
    e1 = less(e0, turn(h0, ratio))
    h1 = magnetic(e1, h0)
    fwd = [saved(0)]
    grad = product(e1, fwd[0])
    e2 = less(e1, turn(h1, ratio))
    fwd.append(saved(1))
    grad = grad + product(e2, fwd[1])
    return e1, h1, e2, grad, fwd


def seam(sgn, a, b, up, down):
    odd = iota(a["h0t"].shape, 0) % 2 == 1
    half = sgn * courant

    def uz(f):
        return jnp.where(odd, 0.0, pltpu.roll(f, 7, 0))

    def lz(f):
        return jnp.where(odd, pltpu.roll(f, 1, 0), 0.0)

    rb, rb1, ra = sgn * b["r0"], sgn * b["r1"], sgn * a["r"]
    d = {}
    e1t = rb * a["h0z"]
    e1z = -rb * a["h0t"]
    e1t_b = b["e1t"] + e1t
    e1z_b = b["e1z"] + e1z
    ah1t = half * e1z_b
    ah1z = -half * e1t_b
    h1t_a = a["h1t"] + ah1t
    h1z_a = a["h1z"] + ah1z
    bh1t = -half * e1z
    bh1n = half * ((uz(e1t) - e1t) - (up(e1z) - e1z))
    bh1z = half * e1t
    e2t = e1t - rb * ((bh1z - h1z_a) - (bh1n - lz(bh1n)))
    e2n = -rb * ((bh1t - lz(bh1t)) - (bh1z - down(bh1z)))
    e2z = e1z - rb * ((bh1n - down(bh1n)) - (bh1t - h1t_a))
    f2t = rb1 * bh1z
    f2z = -rb1 * bh1t
    at = ah1z
    an = (ah1t - lz(ah1t)) - (ah1z - down(ah1z))
    az = -ah1t
    g2t, g2n, g2z = -ra * at, -ra * an, -ra * az
    gb0 = b["f0t"] * e1t + b["f0z"] * e1z + b["f1t"] * e2t + b["f1n"] * e2n + b["f1z"] * e2z
    gb1 = sgn * (b["w1t"] * bh1z - b["w1z"] * bh1t)
    ga = -sgn * (a["wt"] * at + a["wn"] * an + a["wz"] * az)
    e2t_b = b["e2t"] + e2t
    e2z_b = b["e2z"] + e2z
    d["b_e1z"], d["b_h1n"], d["b_h1z"], d["a_h1z"] = e1z, bh1n, bh1z, ah1z
    none = jnp.zeros_like(e1t)
    d["e"] = {"t": (none, g2t, e2t, f2t), "n": (none, g2n, e2n, none), "z": (none, g2z, e2z, f2z)}
    d["h"] = {
        "t": (
            half * g2z,
            ah1t + half * ((e2z_b - g2z) - (uz(g2n) - g2n)),
            bh1t + half * ((f2z - e2z) - (uz(e2n) - e2n)),
            -half * f2z,
        ),
        "n": (
            none,
            half * ((uz(g2t) - g2t) - (up(g2z) - g2z)),
            bh1n + half * ((uz(e2t) - e2t) - (up(e2z) - e2z)),
            half * ((uz(f2t) - f2t) - (up(f2z) - f2z)),
        ),
        "z": (
            -half * g2t,
            ah1z + half * ((up(g2n) - g2n) - (e2t_b - g2t)),
            bh1z + half * ((up(e2n) - e2n) - (f2t - e2t)),
            half * f2t,
        ),
    }
    d["gb0"], d["gb1"], d["ga"] = (g + pltpu.roll(g, 7, 0) for g in (gb0, gb1, ga))
    return d


def two(first, second, at, count=2):
    if count == 1:
        one, other = first[at : at + 1], second[at : at + 1]
        parts = [one, one, other, other]
    else:
        parts = [first[at : at + 2], second[at : at + 2]]
    parts.append(jnp.zeros((4, first.shape[1]), F32))
    return jnp.concatenate(parts, axis=0)


def seam_inputs(left_hi, my_hi, my_lo, right_lo):
    a = {
        "h0t": two(left_hi, my_hi, HI_H0T),
        "h0z": two(left_hi, my_hi, HI_H0Z),
        "h1t": two(left_hi, my_hi, HI_H1T),
        "h1z": two(left_hi, my_hi, HI_H1Z),
        "wt": two(left_hi, my_hi, HI_WT),
        "wn": two(left_hi, my_hi, HI_WN),
        "wz": two(left_hi, my_hi, HI_WZ),
        "r": two(left_hi, my_hi, HI_R, 1),
    }
    b = {
        "e1t": two(my_lo, right_lo, LO_E1T),
        "e1z": two(my_lo, right_lo, LO_E1Z),
        "e2t": two(my_lo, right_lo, LO_E2T),
        "e2z": two(my_lo, right_lo, LO_E2Z),
        "f0t": two(my_lo, right_lo, LO_F0T),
        "f0z": two(my_lo, right_lo, LO_F0Z),
        "f1t": two(my_lo, right_lo, LO_F1T),
        "f1n": two(my_lo, right_lo, LO_F1N),
        "f1z": two(my_lo, right_lo, LO_F1Z),
        "w1t": two(my_lo, right_lo, LO_W1T),
        "w1z": two(my_lo, right_lo, LO_W1Z),
        "r0": two(my_lo, right_lo, LO_R0, 1),
        "r1": two(my_lo, right_lo, LO_R1, 1),
    }
    return a, b


def even(axis):
    return lax.axis_index(axis) % 2 == 0


def ratio_of(labels, density, table):
    eps = jnp.broadcast_to(table[0], labels.shape)
    for k in range(1, NMAT):
        eps = jnp.where(labels == k, table[k], eps)
    return courant / (eps + density)


def planes(ref, *lead):
    return [[ref[(*lead, c, z)] for z in range(ref.shape[-3])] for c in range(3)]


def edge_lists(t, nrm, e1, h0, h1, e2, fwd, ratio):
    zs = range(len(e1[0]))
    lo = (
        [(e1[c][z], 0) for c in (t, 2) for z in zs]
        + [(e2[c][z], 0) for c in (t, 2) for z in zs]
        + [(fwd[0][c][z], 0) for c in (t, 2) for z in zs]
        + [(fwd[1][c][z], 0) for c in (t, nrm, 2) for z in zs]
        + [((ratio, fwd[1][c][z]), 1) for c in (t, 2) for z in zs]
        + [(ratio, 0), (ratio, 1)]
    )
    hi = (
        [(h0[c][z], -1) for c in (t, 2) for z in zs]
        + [(h1[c][z], -1) for c in (t, 2) for z in zs]
        + [((ratio, fwd[1][c][z]), -1) for c in (t, nrm, 2) for z in zs]
        + [(ratio, -1)]
    )
    return lo, hi


def fold(plane):
    m = plane.shape[1]
    lane = iota((plane.shape[0], 128), 1)
    return jnp.where(lane < 64, plane[:, 0:128], plane[:, m - 128 : m])


def place(pack, values, base, count=3):
    lane = iota(pack.shape, 1)
    return jnp.where((lane >= base) & (lane < base + count), pltpu.roll(values, base + 1, 1), pack)


def unpack_rows(packed, lanes, ref):
    ref[0:FILT] = packed[lanes[0] : lanes[0] + FILT]
    for k in range(FILT, len(lanes)):
        ref[k : k + 1] = packed[lanes[k] : lanes[k] + 1]


def line(item, at):
    if isinstance(item, tuple):
        return line(item[0], at) * line(item[1], at)
    at = at % item.shape[0]
    return item[at : at + 1]


def side_by_side(tiles, width, first):
    lane = iota((8, 128), 1)
    out = None
    for k, tile in enumerate(tiles):
        moved = pltpu.roll(tile, (width * k - first) % 128, 1)
        out = moved if out is None else jnp.where(lane < width * k, out, moved)
    return out


def first_kernel(e_hbm, h_hbm, f_hbm, lab_hbm, den_hbm, eps_hbm,
                 up_ref, down_ref, lo_ref, hi_ref, e_ref, h_ref, f_ref, lab_ref, den_ref, table_ref,
                 tab_ref, sems):
    n, m = lab_hbm.shape
    nz = e_hbm.shape[1]
    copies = []
    for src, dst in ((h_hbm, h_ref), (lab_hbm, lab_ref), (den_hbm, den_ref), (eps_hbm, tab_ref), (e_hbm, e_ref),
                     (f_hbm.at[0], f_ref.at[0]), (f_hbm.at[1], f_ref.at[1])):
        copies.append(pltpu.make_async_copy(src, dst, sems.at[len(copies)]))
        copies[-1].start()

    def folded(ref, *lead):
        return [[fold(plane) for plane in comp] for comp in planes(ref, *lead)]

    turn, magnetic = updates(n, 128, nz)
    sides = [(c, z) for c in (0, 2) for z in range(nz)]
    lane = iota((n, 128), 1)
    for copy in copies[1:4]:
        copy.wait()
    ratio = ratio_of(fold(lab_ref[...]), fold(den_ref[...]), tab_ref)
    copies[0].wait()
    h0 = folded(h_ref)
    change = turn(h0, ratio)
    copies[4].wait()
    e1 = less(folded(e_ref), change)
    h1 = magnetic(e1, h0)
    e2 = less(e1, turn(h1, ratio))
    pack = place(jnp.zeros((n, 128), F32), ratio, PACK_R)
    for k, (first, last) in enumerate(((e1, h0), (e2, h1))):
        for j, (c, z) in enumerate(sides):
            pack = place(pack, jnp.where(lane < 64, first[c][z], last[c][z]), PACK_PAIR + 8 * k + 2 * j, 2)
    copies[5].wait()
    fwd = [folded(f_ref, 0)]
    grad = product(e1, fwd[0])
    for j, (c, z) in enumerate(sides):
        pack = jnp.where(lane == PACK_F0 + j, pltpu.roll(fwd[0][c][z], PACK_F0 + j, 1), pack)
    copies[6].wait()
    fwd.append(folded(f_ref, 1))
    grad = grad + product(e2, fwd[1])
    pack = jnp.where((lane < FILT) | (lane >= 128 - FILT), grad, pack)
    scale = jnp.where(lane == 0, 1.0, ratio)
    for k, (c, z) in enumerate((c, z) for c in range(3) for z in range(nz)):
        pack = place(pack, fwd[1][c][z] * scale, PACK_F1 + 3 * k)
    packed = pack.T
    unpack_rows(packed, LO_LANES, lo_ref)
    unpack_rows(packed, HI_LANES, hi_ref)
    lo, hi = edge_lists(1, 0, e1, h0, h1, e2, fwd, ratio)
    rest = [line(*entry) for entry in lo + hi]
    rest = jnp.concatenate(rest + [jnp.zeros((1, 128), F32)], axis=0)
    tiles = [rest[8 * k : 8 * k + 8] for k in range(rest.shape[0] // 8)]
    down_ref[0:LO_ROWS] = lo_ref[...]
    down_ref[LO_ROWS : LO_ROWS + 8] = side_by_side(tiles, GROUP, 0)
    up_ref[0:HI_ROWS] = hi_ref[...]
    up_ref[HI_ROWS:LO_ROWS] = jnp.zeros((LO_ROWS - HI_ROWS, n), F32)
    up_ref[LO_ROWS : LO_ROWS + 8] = side_by_side(tiles, GROUP, 128 - REACH)
    for k in range(NMAT):
        table_ref[k : k + 1] = jnp.full((1, m), tab_ref[k], F32)


def solve_kernel(e_ref, h_ref, f_ref, lab_ref, den_ref, table_ref,
                 lo_ref, hi_ref, grad_ref, e2_ref, h2_ref, across_high, across_low, along_ref, around_ref, near_ref):
    n, m = lab_ref.shape
    nz = e_ref.shape[1]
    ratio = ratio_of(lab_ref[...], den_ref[...], [table_ref[k : k + 1] for k in range(NMAT)])
    h0 = planes(h_ref)
    e1, h1, e2, grad, fwd = local_solve(planes(e_ref), h0, lambda step: planes(f_ref, step), ratio)
    grad_ref[...] = grad
    lo, hi = edge_lists(1, 0, e1, h0, h1, e2, fwd, ratio)
    for ref, group, strip in ((hi_ref, hi, grad[n - FILT : n]), (lo_ref, lo, grad[0:FILT])):
        ref[0:FILT] = strip
        for k, (item, at) in enumerate(group):
            ref[FILT + k : FILT + k + 1] = line(item, at)
    hi_ref[HI_ROWS - 1 : HI_ROWS] = jnp.zeros((1, m), F32)
    _, magnetic = updates(n, m, nz)
    h2 = magnetic(e2, h1)
    for c in range(3):
        for z in range(nz):
            e2_ref[c, z] = e2[c][z]
            h2_ref[c, z] = h2[c][z]
    wide = across_high.shape[0]
    across_high[...], across_low[...] = halves(tap(cyclic(iota((wide, m), 0) - iota((wide, m), 1), wide)))
    around_ref[...] = tap(iota((n, n), 0) - iota((n, n), 1))
    k, r = iota(along_ref.shape, 1), iota(along_ref.shape, 0)
    same = (k < FILT) == (r < FILT)
    along_ref[...] = jnp.where(same, tap(k - r + jnp.where(r < FILT, -FILT, FILT)), 0.0)
    r = iota((EDGE, m), 0)
    for k in range(3):
        near_ref[k] = tap(r - (k - 1))
        near_ref[3 + k] = tap(r - EDGE - (k - 1))


def y_kernel(left_ref, right_ref, lo_ref, hi_ref, xlo_ref, xhi_ref, grad_ref,
             a_ref, b_ref, lo_ext, hi_ext, grad_ext, cols_ref, turned_ref):
    n, m = grad_ref.shape
    right, left = right_ref[0:LO_ROWS], left_ref[0:HI_ROWS]
    a, b = seam_inputs(left, hi_ref[...], lo_ref[...], right)
    lane = iota((8, n), 1)
    d = seam(
        1.0, a, b,
        lambda f: jnp.where(lane == n - 1, 0.0, pltpu.roll(f, n - 1, 1)),
        lambda f: jnp.where(lane == 0, 0.0, pltpu.roll(f, 1, 1)),
    )
    for f, field in enumerate(("e", "h")):
        for c, name in enumerate(("t", "n", "z")):
            before, end, begin, after = d[field][name]
            for z in range(2):
                p = 4 * (6 * f + 2 * c + z)
                turned_ref[p : p + 1] = before[2 + z : 3 + z]
                turned_ref[p + 1 : p + 2] = end[2 + z : 3 + z]
                turned_ref[p + 2 : p + 3] = begin[z : z + 1]
                turned_ref[p + 3 : p + 4] = after[z : z + 1]
    gb0, gb1, ga = d["gb0"], d["gb1"], d["ga"]
    top = iota((8, n), 0)
    at = TURN_G
    turned_ref[at : at + 8] = right[0:8] + jnp.where(top == 0, gb0[2:3], jnp.where(top == 1, gb1[2:3], 0.0))
    turned_ref[at + 8 : at + 16] = right[8:16]
    turned_ref[at + 16 : at + 24] = left[0:8]
    turned_ref[at + 24 : at + 32] = left[8:16] + jnp.where(top == 7, ga[0:1], 0.0)
    turned_ref[TURN_OWN : TURN_OWN + 8] = jnp.where(
        top == 0, ga[2:3], jnp.where(top == 1, gb0[0:1], jnp.where(top == 2, gb1[0:1], 0.0))
    )
    none = jnp.zeros((8, n), F32)
    for k, (last, first) in enumerate(((none, d["b_e1z"]), (none, d["b_h1n"]), (d["a_h1z"], d["b_h1z"]))):
        for z in range(2):
            p = TURN_X + 4 * (2 * k + z)
            turned_ref[p : p + 1] = last[2 + z : 3 + z]
            turned_ref[p + 1 : p + 2] = first[z : z + 1]
            turned_ref[p + 2 : p + 3] = last[z : z + 1]
            turned_ref[p + 3 : p + 4] = first[2 + z : 3 + z]
    turned_ref[TURN_X + 24 : 128] = jnp.zeros((128 - TURN_X - 24, n), F32)
    columns = turned_ref[...].T
    cols_ref[...] = columns

    wide = iota((n, 128), 1)
    own = pltpu.roll(columns, 128 - TURN_OWN - 1, 1)
    grad_ext[:, 0:128] = grad_ref[:, 0:128] + jnp.where(wide < 2, own, 0.0)
    grad_ext[:, m - 128 : m] = grad_ref[:, m - 128 : m] + jnp.where(wide == 127, own, 0.0)
    outside = jnp.where(wide < FILT, pltpu.roll(columns, 128 - TURN_G, 1), 0.0)
    grad_ext[:, m : m + 128] = jnp.where(wide >= 128 - FILT, pltpu.roll(columns, 128 - TURN_G - 2 * FILT, 1), outside)

    lane = iota((8, 128), 1)
    right_tile, left_tile = right_ref[LO_ROWS : LO_ROWS + 8], left_ref[LO_ROWS : LO_ROWS + 8]
    rest = []
    for k in range(LO_ROWS // 8):
        part = jnp.where(lane < REACH, pltpu.roll(right_tile, (128 - GROUP * k) % 128, 1), 0.0)
        rest.append(jnp.where(lane >= 128 - REACH, pltpu.roll(left_tile, (128 - REACH - GROUP * k) % 128, 1), part))
    rest = jnp.concatenate(rest, axis=0)
    for ref, mine, strip, halo in (
        (lo_ext, xlo_ref, slice(0, FILT), rest[0:LO_REST]),
        (hi_ext, xhi_ref, slice(n - FILT, n), rest[LO_REST : LO_REST + HI_REST]),
    ):
        count = mine.shape[0]
        ref[0:FILT] = grad_ext[strip]
        ref[FILT:count, 0:m] = mine[FILT:count]
        ref[FILT : FILT + halo.shape[0], m : m + 128] = halo
    hi_ext[HI_ROWS - 1 : HI_ROWS, m : m + 128] = jnp.zeros((1, 128), F32)
    one = iota((1, 128), 1)
    first, last = columns[0:1], columns[n - 1 : n]

    def add(ref, k, row, at, halo=True):
        inner = pltpu.roll(row, (127 - at) % 128, 1)
        ref[k : k + 1, 0:128] += jnp.where(one < (1 if halo else 2), inner, 0.0)
        ref[k : k + 1, m - 128 : m] += jnp.where(one == 127, inner, 0.0)
        if halo:
            outer = pltpu.roll(row, (125 - at) % 128, 1)
            ref[k : k + 1, m : m + 128] += jnp.where((one == 127) | (one == 0), outer, 0.0)

    for z in range(2):
        add(lo_ext, LO_E1Z + z, first, TURN_X + 4 * z)
        add(hi_ext, HI_H1T + z, last, TURN_X + 8 + 4 * z)
        add(hi_ext, HI_H1Z + z, last, TURN_X + 16 + 4 * z)
        add(lo_ext, LO_E2T + z, first, 4 * (2 + z) + 1, False)
        add(lo_ext, LO_E2Z + z, first, 4 * (4 + z) + 1, False)

    first_even = even("gx")
    low = lo_ext[...]
    high = jnp.concatenate([hi_ext[...], jnp.zeros((LO_ROWS - HI_ROWS, m + 128), F32)], axis=0)
    for ref, part in ((a_ref, jnp.where(first_even, high, low)), (b_ref, jnp.where(first_even, low, high))):
        ref[0:LO_ROWS] = part[:, 0:128]
        ref[LO_ROWS : 2 * LO_ROWS] = part[:, 128:256]
        tiles = [part[8 * k : 8 * k + 8, m : m + 128] for k in range(LO_ROWS // 8)]
        ref[2 * LO_ROWS : 2 * LO_ROWS + 8] = side_by_side(tiles[:3], 2 * REACH, 128 - REACH)
        ref[2 * LO_ROWS + 8 : 2 * LO_ROWS + 16] = side_by_side(tiles[3:], 2 * REACH, 128 - REACH)


def cyclic(d, count):
    return jnp.where(d > count // 2, d - count, jnp.where(d < -(count // 2), d + count, d))


def patch_kernel(cols_ref, e2_ref, h2_ref, grad_ext, across_high, across_low, around_ref,
                 e_hbm, h_hbm, out_hbm, e_rows, h_rows, inner_ref,
                 e_ref, h_ref, sems):
    n, wide = grad_ext.shape
    m = inner_ref.shape[1]
    lane = iota((n, 128), 1)
    columns = cols_ref[...]
    copies = []
    for f, (src, ref, dst, rows) in enumerate(((e2_ref, e_ref, e_hbm, e_rows), (h2_ref, h_ref, h_hbm, h_rows))):
        for c in range(3):
            for z in range(2):
                p = 4 * (6 * f + 2 * c + z)
                moved = pltpu.roll(columns, (126 - p) % 128, 1)
                ref[c, z, :, 0:128] = src[c, z, :, 0:128] + jnp.where(lane < 2, moved, 0.0)
                ref[c, z, :, m - 128 : m] = src[c, z, :, m - 128 : m] + jnp.where(lane >= 126, moved, 0.0)
                rows[c, z, 0:8] = ref[c, z, 0:8]
                rows[c, z, 8:16] = ref[c, z, n - 8 : n]
                copies.append(pltpu.make_async_copy(ref.at[c, z], dst.at[c, z], sems.at[len(copies)]))
                copies[-1].start()
    part = dot3(halves(grad_ext[...]), (across_high[...], across_low[...]))
    inner_ref[...] = dot3(halves(around_ref[...]), halves(part))
    rows = pl.ds(EDGE, n - 2 * EDGE)
    copies.append(pltpu.make_async_copy(inner_ref.at[rows], out_hbm.at[rows], sems.at[len(copies)]))
    copies[-1].start()
    for copy in copies:
        copy.wait()


def x_kernel(ra_ref, rb_ref, lo_ref, hi_ref, e_rows, h_rows, inner_ref, across_high, across_low, along_ref, near_ref,
             e_in, h_in, out_in, e_hbm, h_hbm, out_hbm, ends_ref, out_ref, sems):
    n, m = inner_ref.shape
    wide = lo_ref.shape[1]
    first_even = even("gx")
    tile_lane = iota((8, 128), 1)

    def unfold(message):
        outer = []
        for k in range(LO_ROWS // 8):
            at = 2 * LO_ROWS + 8 * (k // 3)
            moved = pltpu.roll(message[at : at + 8], 128 - REACH - 2 * REACH * (k % 3), 1)
            outer.append(jnp.where((tile_lane < REACH) | (tile_lane >= 128 - REACH), moved, 0.0))
        return jnp.concatenate([message[0:LO_ROWS], message[LO_ROWS : 2 * LO_ROWS], jnp.concatenate(outer, axis=0)], axis=1)

    right = unfold(jnp.where(first_even, ra_ref[...], rb_ref[...]))
    left = unfold(jnp.where(first_even, rb_ref[...], ra_ref[...]))
    a, b = seam_inputs(left, hi_ref[...], lo_ref[...], right)
    raw = jnp.concatenate([left[0:FILT], right[0:FILT]], axis=0)
    part = dot3(halves(raw), (across_high[...], across_low[...]))
    far = dot3(halves(along_ref[...]), halves(part))
    d = seam(-1.0, a, b, lambda f: pltpu.roll(f, wide - 1, 1), lambda f: pltpu.roll(f, 1, 1))
    gb0, gb1, ga = d["gb0"], d["gb1"], d["ga"]
    top = iota((8, wide), 0)
    change = jnp.zeros((8, wide), F32)
    for k, row in enumerate((ga[0:1], gb0[0:1], gb1[0:1], ga[2:3], gb0[2:3], gb1[2:3])):
        change = jnp.where(top == k, row, change)
    taps = filter_taps()
    moved = change[:, 0:m] * taps[0]
    for k in range(1, FILT + 1):
        moved = moved + taps[k] * (pltpu.roll(change, k, 1)[:, 0:m] + pltpu.roll(change, wide - k, 1)[:, 0:m])
    for side, at in ((0, 0), (1, n - EDGE)):
        rows = inner_ref[at : at + EDGE]
        for k in range(3 * side, 3 * side + 3):
            rows = rows + near_ref[k] * moved[k : k + 1]
        out_ref[side] = rows
    out_ref[0, 0:FILT] += far[0:FILT]
    out_ref[1, EDGE - FILT : EDGE] += far[FILT : 2 * FILT]
    copies = []
    for side, at in ((0, 0), (1, n - EDGE)):
        copies.append(pltpu.make_async_copy(out_ref.at[side], out_hbm.at[pl.ds(at, EDGE)], sems.at[side]))
        copies[-1].start()
    sub = iota((8, m), 0)
    for f, (field, rows, dst) in enumerate((("e", e_rows, e_hbm), ("h", h_rows, h_hbm))):
        for c, name in enumerate(("n", "t", "z")):
            before, end, begin, after = (value[:, 0:m] for value in d[field][name])
            for z in range(2):
                ends_ref[0, f, c, z] = rows[c, z, 0:8] + jnp.where(
                    sub == 0, begin[z : z + 1], jnp.where(sub == 1, after[z : z + 1], 0.0)
                )
                ends_ref[1, f, c, z] = rows[c, z, 8:16] + jnp.where(
                    sub == 6, before[2 + z : 3 + z], jnp.where(sub == 7, end[2 + z : 3 + z], 0.0)
                )
        for side, at in ((0, 0), (1, n - 8)):
            dst_rows = dst.at[:, :, pl.ds(at, 8)]
            copies.append(pltpu.make_async_copy(ends_ref.at[side, f], dst_rows, sems.at[len(copies)]))
            copies[-1].start()
    for copy in copies:
        copy.wait()


def swap_pairs(count, which):
    if which == 0:
        return [(i, i ^ 1) for i in range(count)]
    return [(i, (i - 1) % count if i % 2 == 0 else (i + 1) % count) for i in range(count)]


def call(kernel, shapes, ins, scratch=(), far=(), sems=0, far_out=(), aliases=None):
    vmem = pl.BlockSpec(memory_space=pltpu.VMEM)
    hbm = pl.BlockSpec(memory_space=pltpu.HBM)
    ins = [pltpu.with_memory_space_constraint(x, pltpu.HBM) if k in far else x for k, x in enumerate(ins)]
    scratches = [s if hasattr(s, "dtype") else pltpu.VMEM(s, F32) for s in scratch]
    if sems:
        scratches.append(pltpu.SemaphoreType.DMA((sems,)))
    return pl.pallas_call(
        kernel,
        out_shape=[s if hasattr(s, "dtype") else jax.ShapeDtypeStruct(s, F32) for s in shapes],
        in_specs=[hbm if k in far else vmem for k in range(len(ins))],
        out_specs=[hbm if k in far_out else vmem for k in range(len(shapes))],
        scratch_shapes=scratches,
        input_output_aliases=aliases or {},
        compiler_params=pltpu.CompilerParams(vmem_limit_bytes=24 * 1024 * 1024),
    )(*ins)


def body(adj_e, adj_h, fwd_e, labels, eps_table, density):
    n, m = labels.shape
    block = adj_e.shape
    nz = block[1]
    gx, gy = lax.axis_size("gx"), lax.axis_size("gy")
    message = (LO_ROWS + 8, n)
    labels_in = jax.ShapeDtypeStruct((n, m), jnp.int32)
    up, down, ylo, yhi, *fetched = call(
        first_kernel,
        [message, message, (LO_ROWS, n), (HI_ROWS, n), block, block, fwd_e.shape, labels_in, (n, m), (NMAT, m)],
        [adj_e, adj_h, fwd_e, labels, density, eps_table],
        [pltpu.SMEM((NMAT,), F32)],
        range(6),
        7,
    )
    left = lax.ppermute(up, "gy", [(i, (i + 1) % gy) for i in range(gy)])
    right = lax.ppermute(down, "gy", [(i, (i - 1) % gy) for i in range(gy)])
    wide = m + 128
    bands = jax.ShapeDtypeStruct((wide, m), jnp.bfloat16)
    xlo, xhi, grad, e2, h2, across_high, across_low, along, around, near = call(
        solve_kernel,
        [(LO_ROWS, m), (HI_ROWS, m), (n, m), block, block, bands, bands, (2 * FILT, 2 * FILT), (n, n), (6, EDGE, m)],
        fetched,
    )
    message = (2 * LO_ROWS + 16, 128)
    xa, xb, lo_ext, hi_ext, grad_ext, cols = call(
        y_kernel,
        [message, message, (LO_ROWS, wide), (HI_ROWS, wide), (n, wide), (n, 128)],
        [left, right, ylo, yhi, xlo, xhi, grad],
        [(128, n)],
    )
    got_a = lax.ppermute(xa, "gx", swap_pairs(gx, 0))
    got_b = lax.ppermute(xb, "gx", swap_pairs(gx, 1))
    ends = (3, nz, 16, m)
    electric, magnetic, filtered, e_rows, h_rows, inner = call(
        patch_kernel,
        [block, block, (n, m), ends, ends, (n, m)],
        [cols, e2, h2, grad_ext, across_high, across_low, around],
        [block, block],
        sems=13,
        far_out=(0, 1, 2),
    )
    return tuple(
        call(
            x_kernel,
            [block, block, (n, m)],
            [got_a, got_b, lo_ext, hi_ext, e_rows, h_rows, inner, across_high, across_low, along, near]
            + [electric, magnetic, filtered],
            [(2, 2, 3, nz, 8, m), (2, EDGE, m)],
            (11, 12, 13),
            6,
            (0, 1, 2),
            {11: 0, 12: 1, 13: 2},
        )
    )


def solution(mesh):
    return jax.shard_map(
        body,
        mesh=mesh,
        in_specs=(
            P("design", None, "gx", "gy"),
            P("design", None, "gx", "gy"),
            P("design", None, None, "gx", "gy"),
            P(("design", "gx"), "gy"),
            P(),
            P(("design", "gx"), "gy"),
        ),
        out_specs=(
            P("design", None, "gx", "gy"),
            P("design", None, "gx", "gy"),
            P(("design", "gx"), "gy"),
        ),
        check_vma=False,
    )
```

time: 16.3 us -> 15.7 us (0.963)
  waiting for transfers between devices: 2.02 us -> 0.88 us
  Pallas kernels: 6.34 us -> 7.12 us
  starting transfers between devices: 7.01 us -> 6.82 us
    ppermute x2, starting transfers between devices: 3.88 us -> 5.17 us  [the longest x1 3.08 us: body(): left = lax.ppermute(up, 'gy', [(i, (i + 1) % gy) for i in range(gy)])]
    ppermute x2, waiting for transfers between devices: 1.59 us -> 0.43 us  [the longest x1 0.27 us: body(): left = lax.ppermute(up, 'gy', [(i, (i + 1) % gy) for i in range(gy)])]
    ppermute x1, starting transfers between devices: 2.61 us -> 1.61 us  [body(): got_b = lax.ppermute(xb, 'gx', swap_pairs(gx, 1))]
    pallas_call x5, Pallas kernels: 6.34 us -> 7.12 us  [call(): pl.pallas_call(kernel, out_shape=[s if hasattr(s, 'dtype') else jax.Shape...]
    ppermute x1, starting transfers between devices: 0.52 us -> 0.05 us  [body(): got_a = lax.ppermute(xa, 'gx', swap_pairs(gx, 0))]
  transfers between devices with their start and end apart: 4 -> 4, of which waited for: 3 -> 3; matrix products, arithmetic and copies ran while one was open for 0% -> 0% of each run, Pallas kernels for 14% -> 20%
where the time goes in v7:
time: 15.7 us; the launch traced here: 15.5 us
  Pallas kernels  7.12 us (45%)
  starting transfers between devices  6.82 us (43%)
  waiting for transfers between devices  0.88 us (6%)
  between operations  0.67 us (4%)
    pallas_call x5, Pallas kernels, call(): pl.pallas_call(kernel, out_shape=[s if hasattr(s, 'dtype') else jax.Shape...  7.12 us
    ppermute x1, starting transfers between devices, body(): left = lax.ppermute(up, 'gy', [(i, (i + 1) % gy) for i in range(gy)])  3.08 us
    ppermute x1, starting transfers between devices, body(): right = lax.ppermute(down, 'gy', [(i, (i - 1) % gy) for i in range(gy)])  2.09 us
    ppermute x1, starting transfers between devices, body(): got_b = lax.ppermute(xb, 'gx', swap_pairs(gx, 1))  1.61 us
    ppermute x1, waiting for transfers between devices, body(): got_b = lax.ppermute(xb, 'gx', swap_pairs(gx, 1))  0.45 us
  transfers between devices with their start and end apart: 4, of which 3 were waited for; matrix products, arithmetic and copies ran while one was open for 0% of the time, Pallas kernels for 20%

profile of v7, /device:TPU:0, one launch (start us, length us, event | category | flops | bytes accessed | tf_op | source)
XLA Modules:
  0.0 15.5 jit_solution(2907440155154386097)
XLA Ops:
  0.6 2.4 %shard_map.85 = (f32[48,128]{1,0:T(8,128)S(1)}, f32[48,128]{1,0:T(8,128)S(1)}, f32[40,128]{1,0:T(8,128)S(1)}, f32[32,128]{1,0:T(8,128)S(1)}, f32[3,2,128,256]{3,...) custom-call(f32[3,2,128,256]{3,2,1,0:T(8,128)} %e_hbm.1, ...), custom_call_target="tpu_custom_call" | custom-call | tf_op jit(solution)/shard_map/pallas_call | solution.py:601
  3.0 3.1 %collective-permute-start = (f32[48,128]{1,0:T(8,128)S(1)}, f32[48,128]{1,0:T(8,128)S(1)}, u32[]{:S(2)}, u32[]{:S(2)}) collective-permute-start(f32[48,128]{1,0:T(8,128)S(1)} %get-tuple-element.35), channel_id=1, source_target_pairs={{0,1},{1,2},{2,3},{3,0},{4,5},{5,6},{6,7},{7,4},{8,9},{9,10},{10,1... | collective-permute-start | bytes 73736 | tf_op jit(solution)/shard_map/ppermute | solution.py:627
  6.1 2.1 %collective-permute-start.1 = (f32[48,128]{1,0:T(8,128)S(1)}, f32[48,128]{1,0:T(8,128)S(1)}, u32[]{:S(2)}, u32[]{:S(2)}) collective-permute-start(f32[48,128]{1,0:T(8,128)S(1)} %get-tuple-element.36), channel_id=1, source_target_pairs={{0,3},{1,0},{2,1},{3,2},{4,7},{5,4},{6,5},{7,6},{8,11},{9,8},{10,9... | collective-permute-start | bytes 73736 | tf_op jit(solution)/shard_map/ppermute | solution.py:628
  8.2 1.6 %shard_map.86 = (f32[40,256]{1,0:T(8,128)S(1)}, f32[32,256]{1,0:T(8,128)S(1)}, f32[128,256]{1,0:T(8,128)S(1)}, f32[3,2,128,256]{3,2,1,0:T(8,128)S(1)}, f32[3,2,1...) custom-call(f32[3,2,128,256]{3,2,1,0:T(8,128)S(1)} %get-tuple-elemen, ...), custom_call_target="tpu_custom_call" | custom-call | tf_op jit(solution)/shard_map/pallas_call | solution.py:601
  9.8 0.3 %collective-permute-done.left_ref = f32[48,128]{1,0:T(8,128)S(1)} collective-permute-done((f32[48,128]{1,0:T(8,128)S(1)}, f32[48,128]{1,0:T(8,128)S(1)}, u32[]{:S(2)}, u32[]{:S(2)}) %collective-permute-start) | collective-permute-done | bytes 24608 | tf_op jit(solution)/shard_map/ppermute | solution.py:627
  10.0 0.2 collective-permute-done.1.right_ref
  10.2 0.5 %shard_map.87 = (f32[96,128]{1,0:T(8,128)S(1)}, f32[96,128]{1,0:T(8,128)S(1)}, f32[40,384]{1,0:T(8,128)S(1)}, f32[32,384]{1,0:T(8,128)S(1)}, f32[128,384]{1,0:T(8,128)S(1)}, /*index=5*/f32[128,128]{1,0:T(8,128)S(1)}) custom-call(f32[48,128]{1,0:T(8,128)S(1)} %collective-permute-done.left_ref, f32[48,128]{1,0:T(8,128)S(1)} %collective-permute-done.1.right_ref, ...), custom_call_target="tpu_custom_call" | custom-call | tf_op jit(solution)/shard_map/pallas_call | solution.py:601
  10.7 0.0 collective-permute-start.2
  10.7 1.6 %collective-permute-start.3 = (f32[96,128]{1,0:T(8,128)S(1)}, f32[96,128]{1,0:T(8,128)S(1)}, u32[]{:S(2)}, u32[]{:S(2)}) collective-permute-start(f32[96,128]{1,0:T(8,128)S(1)} %get-tuple-element.49), channel_id=1, source_target_pairs={{0,12},{4,8},{8,4},{12,0},{1,13},{5,9},{9,5},{13,1},{2,14},{6,10},... | collective-permute-start | bytes 147464 | tf_op jit(solution)/shard_map/ppermute | solution.py:644
  12.3 1.5 %shard_map.88 = (f32[3,2,128,256]{3,2,1,0:T(8,128)}, f32[3,2,128,256]{3,2,1,0:T(8,128)}, f32[128,256]{1,0:T(8,128)}, f32[3,2,16,256]{3,2,1,0:T(8,128)S(1)}, f32[...) custom-call(f32[128,128]{1,0:T(8,128)S(1)} %get-tuple-element.52.cols_ref, ...), custom_call_target="tpu_custom_call" | custom-call | tf_op jit(solution)/shard_map/pallas_call | solution.py:601
  13.8 0.0 collective-permute-done.2.ra_ref
  13.9 0.4 %collective-permute-done.3.rb_ref = f32[96,128]{1,0:T(8,128)S(1)} collective-permute-done((f32[96,128]{1,0:T(8,128)S(1)}, f32[96,128]{1,0:T(8,128)S(1)}, u32[]{:S(2)}, u32[]{:S(2)}) %collective-permute-start.3) | collective-permute-done | bytes 49184 | tf_op jit(solution)/shard_map/ppermute | solution.py:644
  14.3 1.2 %shard_map.89 = (f32[3,2,128,256]{3,2,1,0:T(8,128)}, f32[3,2,128,256]{3,2,1,0:T(8,128)}, f32[128,256]{1,0:T(8,128)}) custom-call(f32[96,128]{1,0:T(8,128)S(1)} %collective-permute-done.2.ra_ref, f32[96,128]{1,0:T(8,128)S(1)} %collective-permute-done.3.rb_ref, ...), custom_call_target="tpu_custom_call", output_to_operand_aliasing={{0}: (11, {}), {1}: (12, {}), {2}: (13, {})} | custom-call | tf_op jit(solution)/shard_map/pallas_call | solution.py:601
Async XLA Ops:
  3.0 7.0 %collective-permute-start = (f32[48,128]{1,0:T(8,128)S(1)}, f32[48,128]{1,0:T(8,128)S(1)}, u32[]{:S(2)}, u32[]{:S(2)}) collective-permute-start(f32[48,128]{1,0:T(8,128)S(1)} %get-tuple-element.35), channel_id=1, source_target_pairs={{0,1},{1,2},{2,3},{3,0},{4,5},{5,6},{6,7},{7,4},{8,9},{9,10},{10,1... | collective-permute-start | bytes 73736 | tf_op jit(solution)/shard_map/ppermute | solution.py:627
  6.1 4.1 %collective-permute-start.1 = (f32[48,128]{1,0:T(8,128)S(1)}, f32[48,128]{1,0:T(8,128)S(1)}, u32[]{:S(2)}, u32[]{:S(2)}) collective-permute-start(f32[48,128]{1,0:T(8,128)S(1)} %get-tuple-element.36), channel_id=1, source_target_pairs={{0,3},{1,0},{2,1},{3,2},{4,7},{5,4},{6,5},{7,6},{8,11},{9,8},{10,9... | collective-permute-start | bytes 73736 | tf_op jit(solution)/shard_map/ppermute | solution.py:628
  10.7 3.2 %collective-permute-start.2 = (f32[96,128]{1,0:T(8,128)S(1)}, f32[96,128]{1,0:T(8,128)S(1)}, u32[]{:S(2)}, u32[]{:S(2)}) collective-permute-start(f32[96,128]{1,0:T(8,128)S(1)} %get-tuple-element.48), channel_id=1, source_target_pairs={{0,4},{4,0},{8,12},{12,8},{1,5},{5,1},{9,13},{13,9},{2,6},{6,2},{1... | collective-permute-start | bytes 147464 | tf_op jit(solution)/shard_map/ppermute | solution.py:643
  10.7 3.6 %collective-permute-start.3 = (f32[96,128]{1,0:T(8,128)S(1)}, f32[96,128]{1,0:T(8,128)S(1)}, u32[]{:S(2)}, u32[]{:S(2)}) collective-permute-start(f32[96,128]{1,0:T(8,128)S(1)} %get-tuple-element.49), channel_id=1, source_target_pairs={{0,12},{4,8},{8,4},{12,0},{1,13},{5,9},{9,5},{13,1},{2,14},{6,10},... | collective-permute-start | bytes 147464 | tf_op jit(solution)/shard_map/ppermute | solution.py:644

commit v8 on v7

--- a/solution.py
+++ b/solution.py
@@ -137,16 +137,45 @@
     return e1, h1, e2, grad, fwd
 
 
+def depth_shifts(shape):
+    odd = iota(shape, 0) % 2 == 1
+    return (
+        lambda f: jnp.where(odd, 0.0, pltpu.roll(f, 7, 0)),
+        lambda f: jnp.where(odd, pltpu.roll(f, 1, 0), 0.0),
+    )
+
+
+def seam_magnetic(sgn, v, up):
+    half = sgn * courant
+    uz, _ = depth_shifts(v[0].shape)
+    e2t, e2n, e2z, f2t, f2z, g2t, g2n, g2z, ah1t, ah1z, bh1t, bh1n, bh1z, e2t_b, e2z_b = v
+    none = jnp.zeros_like(e2t)
+    return {
+        "t": (
+            half * g2z,
+            ah1t + half * ((e2z_b - g2z) - (uz(g2n) - g2n)),
+            bh1t + half * ((f2z - e2z) - (uz(e2n) - e2n)),
+            -half * f2z,
+        ),
+        "n": (
+            none,
+            half * ((uz(g2t) - g2t) - (up(g2z) - g2z)),
+            bh1n + half * ((uz(e2t) - e2t) - (up(e2z) - e2z)),
+            half * ((uz(f2t) - f2t) - (up(f2z) - f2z)),
+        ),
+        "z": (
+            -half * g2t,
+            ah1z + half * ((up(g2n) - g2n) - (e2t_b - g2t)),
+            bh1z + half * ((up(e2n) - e2n) - (f2t - e2t)),
+            half * f2t,
+        ),
+    }
+
+
 def seam(sgn, a, b, up, down):
     odd = iota(a["h0t"].shape, 0) % 2 == 1
     half = sgn * courant
-
-    def uz(f):
-        return jnp.where(odd, 0.0, pltpu.roll(f, 7, 0))
-
-    def lz(f):
-        return jnp.where(odd, pltpu.roll(f, 1, 0), 0.0)
-
+    uz, lz = depth_shifts(a["h0t"].shape)
     rb, rb1, ra = sgn * b["r0"], sgn * b["r1"], sgn * a["r"]
     d = {}
     e1t = rb * a["h0z"]
@@ -177,26 +206,7 @@
     d["b_e1z"], d["b_h1n"], d["b_h1z"], d["a_h1z"] = e1z, bh1n, bh1z, ah1z
     none = jnp.zeros_like(e1t)
     d["e"] = {"t": (none, g2t, e2t, f2t), "n": (none, g2n, e2n, none), "z": (none, g2z, e2z, f2z)}
-    d["h"] = {
-        "t": (
-            half * g2z,
-            ah1t + half * ((e2z_b - g2z) - (uz(g2n) - g2n)),
-            bh1t + half * ((f2z - e2z) - (uz(e2n) - e2n)),
-            -half * f2z,
-        ),
-        "n": (
-            none,
-            half * ((uz(g2t) - g2t) - (up(g2z) - g2z)),
-            bh1n + half * ((uz(e2t) - e2t) - (up(e2z) - e2z)),
-            half * ((uz(f2t) - f2t) - (up(f2z) - f2z)),
-        ),
-        "z": (
-            -half * g2t,
-            ah1z + half * ((up(g2n) - g2n) - (e2t_b - g2t)),
-            bh1z + half * ((up(e2n) - e2n) - (f2t - e2t)),
-            half * f2t,
-        ),
-    }
+    d["v"] = (e2t, e2n, e2z, f2t, f2z, g2t, g2n, g2z, ah1t, ah1z, bh1t, bh1n, bh1z, e2t_b, e2z_b)
     d["gb0"], d["gb1"], d["ga"] = (g + pltpu.roll(g, 7, 0) for g in (gb0, gb1, ga))
     return d
 
@@ -398,8 +408,31 @@
         near_ref[3 + k] = tap(r - EDGE - (k - 1))
 
 
+def put_lines(ref, lines):
+    for c, name in enumerate(("t", "n", "z")):
+        before, end, begin, after = lines[name]
+        for z in range(2):
+            p = 4 * (2 * c + z)
+            ref[p : p + 1] = before[2 + z : 3 + z]
+            ref[p + 1 : p + 2] = end[2 + z : 3 + z]
+            ref[p + 2 : p + 3] = begin[z : z + 1]
+            ref[p + 3 : p + 4] = after[z : z + 1]
+
+
+def extended(grad, columns):
+    m = grad.shape[1]
+    lane = iota(columns.shape, 1)
+    own = pltpu.roll(columns, 128 - TURN_OWN - 1, 1)
+    outside = jnp.where(lane < FILT, pltpu.roll(columns, 128 - TURN_G, 1), 0.0)
+    return [
+        grad[:, 0:128] + jnp.where(lane < 2, own, 0.0),
+        grad[:, m - 128 : m] + jnp.where(lane == 127, own, 0.0),
+        jnp.where(lane >= 128 - FILT, pltpu.roll(columns, 128 - TURN_G - 2 * FILT, 1), outside),
+    ]
+
+
 def y_kernel(left_ref, right_ref, lo_ref, hi_ref, xlo_ref, xhi_ref, grad_ref,
-             a_ref, b_ref, lo_ext, hi_ext, grad_ext, cols_ref, turned_ref):
+             a_ref, b_ref, lo_ext, hi_ext, cols_ref, seam_ref, turned_ref):
     n, m = grad_ref.shape
     right, left = right_ref[0:LO_ROWS], left_ref[0:HI_ROWS]
     a, b = seam_inputs(left, hi_ref[...], lo_ref[...], right)
@@ -409,15 +442,10 @@
         lambda f: jnp.where(lane == n - 1, 0.0, pltpu.roll(f, n - 1, 1)),
         lambda f: jnp.where(lane == 0, 0.0, pltpu.roll(f, 1, 1)),
     )
-    for f, field in enumerate(("e", "h")):
-        for c, name in enumerate(("t", "n", "z")):
-            before, end, begin, after = d[field][name]
-            for z in range(2):
-                p = 4 * (6 * f + 2 * c + z)
-                turned_ref[p : p + 1] = before[2 + z : 3 + z]
-                turned_ref[p + 1 : p + 2] = end[2 + z : 3 + z]
-                turned_ref[p + 2 : p + 3] = begin[z : z + 1]
-                turned_ref[p + 3 : p + 4] = after[z : z + 1]
+    for k, value in enumerate(d["v"]):
+        seam_ref[k] = value
+    put_lines(turned_ref, d["e"])
+    turned_ref[24:TURN_G] = jnp.zeros((TURN_G - 24, n), F32)
     gb0, gb1, ga = d["gb0"], d["gb1"], d["ga"]
     top = iota((8, n), 0)
     at = TURN_G
@@ -439,13 +467,6 @@
     turned_ref[TURN_X + 24 : 128] = jnp.zeros((128 - TURN_X - 24, n), F32)
     columns = turned_ref[...].T
     cols_ref[...] = columns
-
-    wide = iota((n, 128), 1)
-    own = pltpu.roll(columns, 128 - TURN_OWN - 1, 1)
-    grad_ext[:, 0:128] = grad_ref[:, 0:128] + jnp.where(wide < 2, own, 0.0)
-    grad_ext[:, m - 128 : m] = grad_ref[:, m - 128 : m] + jnp.where(wide == 127, own, 0.0)
-    outside = jnp.where(wide < FILT, pltpu.roll(columns, 128 - TURN_G, 1), 0.0)
-    grad_ext[:, m : m + 128] = jnp.where(wide >= 128 - FILT, pltpu.roll(columns, 128 - TURN_G - 2 * FILT, 1), outside)
 
     lane = iota((8, 128), 1)
     right_tile, left_tile = right_ref[LO_ROWS : LO_ROWS + 8], left_ref[LO_ROWS : LO_ROWS + 8]
@@ -459,7 +480,8 @@
         (hi_ext, xhi_ref, slice(n - FILT, n), rest[LO_REST : LO_REST + HI_REST]),
     ):
         count = mine.shape[0]
-        ref[0:FILT] = grad_ext[strip]
+        for k, tile in enumerate(extended(grad_ref[strip], columns[strip])):
+            ref[0:FILT, 128 * k : 128 * k + 128] = tile
         ref[FILT:count, 0:m] = mine[FILT:count]
         ref[FILT : FILT + halo.shape[0], m : m + 128] = halo
     hi_ext[HI_ROWS - 1 : HI_ROWS, m : m + 128] = jnp.zeros((1, 128), F32)
@@ -496,18 +518,18 @@
     return jnp.where(d > count // 2, d - count, jnp.where(d < -(count // 2), d + count, d))
 
 
-def patch_kernel(cols_ref, e2_ref, h2_ref, grad_ext, across_high, across_low, around_ref,
+def patch_kernel(cols_ref, seam_ref, e2_ref, h2_ref, grad_ref, across_high, across_low, around_ref,
                  e_hbm, h_hbm, out_hbm, e_rows, h_rows, inner_ref,
-                 e_ref, h_ref, sems):
-    n, wide = grad_ext.shape
-    m = inner_ref.shape[1]
+                 e_ref, h_ref, turned_ref, sems):
+    n, m = grad_ref.shape
     lane = iota((n, 128), 1)
     columns = cols_ref[...]
     copies = []
-    for f, (src, ref, dst, rows) in enumerate(((e2_ref, e_ref, e_hbm, e_rows), (h2_ref, h_ref, h_hbm, h_rows))):
+
+    def patch(columns, src, ref, dst, rows):
         for c in range(3):
             for z in range(2):
-                p = 4 * (6 * f + 2 * c + z)
+                p = 4 * (2 * c + z)
                 moved = pltpu.roll(columns, (126 - p) % 128, 1)
                 ref[c, z, :, 0:128] = src[c, z, :, 0:128] + jnp.where(lane < 2, moved, 0.0)
                 ref[c, z, :, m - 128 : m] = src[c, z, :, m - 128 : m] + jnp.where(lane >= 126, moved, 0.0)
@@ -515,7 +537,15 @@
                 rows[c, z, 8:16] = ref[c, z, n - 8 : n]
                 copies.append(pltpu.make_async_copy(ref.at[c, z], dst.at[c, z], sems.at[len(copies)]))
                 copies[-1].start()
-    part = dot3(halves(grad_ext[...]), (across_high[...], across_low[...]))
+
+    patch(columns, e2_ref, e_ref, e_hbm, e_rows)
+    row = iota((8, n), 1)
+    up = lambda f: jnp.where(row == n - 1, 0.0, pltpu.roll(f, n - 1, 1))
+    put_lines(turned_ref, seam_magnetic(1.0, [seam_ref[k] for k in range(15)], up))
+    turned_ref[24:128] = jnp.zeros((104, n), F32)
+    patch(turned_ref[...].T, h2_ref, h_ref, h_hbm, h_rows)
+    grad_ext = jnp.concatenate(extended(grad_ref[...], columns), axis=1)
+    part = dot3(halves(grad_ext), (across_high[...], across_low[...]))
     inner_ref[...] = dot3(halves(around_ref[...]), halves(part))
     rows = pl.ds(EDGE, n - 2 * EDGE)
     copies.append(pltpu.make_async_copy(inner_ref.at[rows], out_hbm.at[rows], sems.at[len(copies)]))
@@ -567,9 +597,10 @@
         copies.append(pltpu.make_async_copy(out_ref.at[side], out_hbm.at[pl.ds(at, EDGE)], sems.at[side]))
         copies[-1].start()
     sub = iota((8, m), 0)
-    for f, (field, rows, dst) in enumerate((("e", e_rows, e_hbm), ("h", h_rows, h_hbm))):
+    magnetic = seam_magnetic(-1.0, d["v"], lambda f: pltpu.roll(f, wide - 1, 1))
+    for f, (field, rows, dst) in enumerate(((d["e"], e_rows, e_hbm), (magnetic, h_rows, h_hbm))):
         for c, name in enumerate(("n", "t", "z")):
-            before, end, begin, after = (value[:, 0:m] for value in d[field][name])
+            before, end, begin, after = (value[:, 0:m] for value in field[name])
             for z in range(2):
                 ends_ref[0, f, c, z] = rows[c, z, 0:8] + jnp.where(
                     sub == 0, begin[z : z + 1], jnp.where(sub == 1, after[z : z + 1], 0.0)
@@ -634,9 +665,9 @@
         fetched,
     )
     message = (2 * LO_ROWS + 16, 128)
-    xa, xb, lo_ext, hi_ext, grad_ext, cols = call(
+    xa, xb, lo_ext, hi_ext, cols, seams = call(
         y_kernel,
-        [message, message, (LO_ROWS, wide), (HI_ROWS, wide), (n, wide), (n, 128)],
+        [message, message, (LO_ROWS, wide), (HI_ROWS, wide), (n, 128), (15, 8, n)],
         [left, right, ylo, yhi, xlo, xhi, grad],
         [(128, n)],
     )
@@ -646,8 +677,8 @@
     electric, magnetic, filtered, e_rows, h_rows, inner = call(
         patch_kernel,
         [block, block, (n, m), ends, ends, (n, m)],
-        [cols, e2, h2, grad_ext, across_high, across_low, around],
-        [block, block],
+        [cols, seams, e2, h2, grad, across_high, across_low, around],
+        [block, block, (128, n)],
         sems=13,
         far_out=(0, 1, 2),
     )

time: 15.7 us -> 15.6 us (level)
  Pallas kernels: 7.12 us -> 6.96 us
    pallas_call x5, Pallas kernels: 7.12 us -> 6.96 us  [call(): pl.pallas_call(kernel, out_shape=[s if hasattr(s, 'dtype') else jax.Shape...]
  transfers between devices with their start and end apart: 4 -> 4, of which waited for: 3 -> 3; matrix products, arithmetic and copies ran while one was open for 0% -> 0% of each run, Pallas kernels for 20% -> 19%
where the time goes in v8:
time: 15.6 us; the launch traced here: 15.5 us
  Pallas kernels  6.96 us (45%)
  starting transfers between devices  6.85 us (44%)
  waiting for transfers between devices  0.95 us (6%)
  between operations  0.68 us (4%)
    pallas_call x5, Pallas kernels, call(): pl.pallas_call(kernel, out_shape=[s if hasattr(s, 'dtype') else jax.Shape...  6.96 us
    ppermute x1, starting transfers between devices, body(): left = lax.ppermute(up, 'gy', [(i, (i + 1) % gy) for i in range(gy)])  3.08 us
    ppermute x1, starting transfers between devices, body(): right = lax.ppermute(down, 'gy', [(i, (i - 1) % gy) for i in range(gy)])  2.09 us
    ppermute x1, starting transfers between devices, body(): got_b = lax.ppermute(xb, 'gx', swap_pairs(gx, 1))  1.61 us
    ppermute x1, waiting for transfers between devices, body(): got_b = lax.ppermute(xb, 'gx', swap_pairs(gx, 1))  0.52 us
  transfers between devices with their start and end apart: 4, of which 3 were waited for; matrix products, arithmetic and copies ran while one was open for 0% of the time, Pallas kernels for 19%

profile of v8, /device:TPU:0, one launch (start us, length us, event | category | flops | bytes accessed | tf_op | source)
XLA Modules:
  0.0 15.5 jit_solution(15186528631894568789)
XLA Ops:
  0.6 2.4 %shard_map.85 = (f32[48,128]{1,0:T(8,128)S(1)}, f32[48,128]{1,0:T(8,128)S(1)}, f32[40,128]{1,0:T(8,128)S(1)}, f32[32,128]{1,0:T(8,128)S(1)}, f32[3,2,128,256]{3,...) custom-call(f32[3,2,128,256]{3,2,1,0:T(8,128)} %e_hbm.1, ...), custom_call_target="tpu_custom_call" | custom-call | tf_op jit(solution)/shard_map/pallas_call | solution.py:632
  3.0 3.1 %collective-permute-start = (f32[48,128]{1,0:T(8,128)S(1)}, f32[48,128]{1,0:T(8,128)S(1)}, u32[]{:S(2)}, u32[]{:S(2)}) collective-permute-start(f32[48,128]{1,0:T(8,128)S(1)} %get-tuple-element.35), channel_id=1, source_target_pairs={{0,1},{1,2},{2,3},{3,0},{4,5},{5,6},{6,7},{7,4},{8,9},{9,10},{10,1... | collective-permute-start | bytes 73736 | tf_op jit(solution)/shard_map/ppermute | solution.py:658
  6.1 2.1 %collective-permute-start.1 = (f32[48,128]{1,0:T(8,128)S(1)}, f32[48,128]{1,0:T(8,128)S(1)}, u32[]{:S(2)}, u32[]{:S(2)}) collective-permute-start(f32[48,128]{1,0:T(8,128)S(1)} %get-tuple-element.36), channel_id=1, source_target_pairs={{0,3},{1,0},{2,1},{3,2},{4,7},{5,4},{6,5},{7,6},{8,11},{9,8},{10,9... | collective-permute-start | bytes 73736 | tf_op jit(solution)/shard_map/ppermute | solution.py:659
  8.2 1.6 %shard_map.86 = (f32[40,256]{1,0:T(8,128)S(1)}, f32[32,256]{1,0:T(8,128)S(1)}, f32[128,256]{1,0:T(8,128)S(1)}, f32[3,2,128,256]{3,2,1,0:T(8,128)S(1)}, f32[3,2,1...) custom-call(f32[3,2,128,256]{3,2,1,0:T(8,128)S(1)} %get-tuple-elemen, ...), custom_call_target="tpu_custom_call" | custom-call | tf_op jit(solution)/shard_map/pallas_call | solution.py:632
  9.8 0.3 %collective-permute-done.left_ref = f32[48,128]{1,0:T(8,128)S(1)} collective-permute-done((f32[48,128]{1,0:T(8,128)S(1)}, f32[48,128]{1,0:T(8,128)S(1)}, u32[]{:S(2)}, u32[]{:S(2)}) %collective-permute-start) | collective-permute-done | bytes 24608 | tf_op jit(solution)/shard_map/ppermute | solution.py:658
  10.0 0.2 collective-permute-done.1.right_ref
  10.2 0.4 %shard_map.87 = (f32[96,128]{1,0:T(8,128)S(1)}, f32[96,128]{1,0:T(8,128)S(1)}, f32[40,384]{1,0:T(8,128)S(1)}, f32[32,384]{1,0:T(8,128)S(1)}, f32[128,128]{1,0:T(8,128)S(1)}, /*index=5*/f32[15,8,128]{2,1,0:T(8,128)S(1)}) custom-call(f32[48,128]{1,0:T(8,128)S(1)} %collective-permute-done.left_ref, f32[48,128]{1,0:T(8,128)S(1)} %collective-permute-done.1.right_ref, ...), custom_call_target="tpu_custom_call" | custom-call | tf_op jit(solution)/shard_map/pallas_call | solution.py:632
  10.6 0.1 collective-permute-start.2
  10.7 1.6 %collective-permute-start.3 = (f32[96,128]{1,0:T(8,128)S(1)}, f32[96,128]{1,0:T(8,128)S(1)}, u32[]{:S(2)}, u32[]{:S(2)}) collective-permute-start(f32[96,128]{1,0:T(8,128)S(1)} %get-tuple-element.49), channel_id=1, source_target_pairs={{0,12},{4,8},{8,4},{12,0},{1,13},{5,9},{9,5},{13,1},{2,14},{6,10},... | collective-permute-start | bytes 147464 | tf_op jit(solution)/shard_map/ppermute | solution.py:675
  12.3 1.4 %shard_map.88 = (f32[3,2,128,256]{3,2,1,0:T(8,128)}, f32[3,2,128,256]{3,2,1,0:T(8,128)}, f32[128,256]{1,0:T(8,128)}, f32[3,2,16,256]{3,2,1,0:T(8,128)S(1)}, f32[...) custom-call(f32[128,128]{1,0:T(8,128)S(1)} %get-tuple-element.52.cols_ref, ...), custom_call_target="tpu_custom_call" | custom-call | tf_op jit(solution)/shard_map/pallas_call | solution.py:632
  13.7 0.0 collective-permute-done.2.ra_ref
  13.7 0.5 %collective-permute-done.3.rb_ref = f32[96,128]{1,0:T(8,128)S(1)} collective-permute-done((f32[96,128]{1,0:T(8,128)S(1)}, f32[96,128]{1,0:T(8,128)S(1)}, u32[]{:S(2)}, u32[]{:S(2)}) %collective-permute-start.3) | collective-permute-done | bytes 49184 | tf_op jit(solution)/shard_map/ppermute | solution.py:675
  14.3 1.2 %shard_map.89 = (f32[3,2,128,256]{3,2,1,0:T(8,128)}, f32[3,2,128,256]{3,2,1,0:T(8,128)}, f32[128,256]{1,0:T(8,128)}) custom-call(f32[96,128]{1,0:T(8,128)S(1)} %collective-permute-done.2.ra_ref, f32[96,128]{1,0:T(8,128)S(1)} %collective-permute-done.3.rb_ref, ...), custom_call_target="tpu_custom_call", output_to_operand_aliasing={{0}: (11, {}), {1}: (12, {}), {2}: (13, {})} | custom-call | tf_op jit(solution)/shard_map/pallas_call | solution.py:632
Async XLA Ops:
  3.0 7.0 %collective-permute-start = (f32[48,128]{1,0:T(8,128)S(1)}, f32[48,128]{1,0:T(8,128)S(1)}, u32[]{:S(2)}, u32[]{:S(2)}) collective-permute-start(f32[48,128]{1,0:T(8,128)S(1)} %get-tuple-element.35), channel_id=1, source_target_pairs={{0,1},{1,2},{2,3},{3,0},{4,5},{5,6},{6,7},{7,4},{8,9},{9,10},{10,1... | collective-permute-start | bytes 73736 | tf_op jit(solution)/shard_map/ppermute | solution.py:658
  6.1 4.1 %collective-permute-start.1 = (f32[48,128]{1,0:T(8,128)S(1)}, f32[48,128]{1,0:T(8,128)S(1)}, u32[]{:S(2)}, u32[]{:S(2)}) collective-permute-start(f32[48,128]{1,0:T(8,128)S(1)} %get-tuple-element.36), channel_id=1, source_target_pairs={{0,3},{1,0},{2,1},{3,2},{4,7},{5,4},{6,5},{7,6},{8,11},{9,8},{10,9... | collective-permute-start | bytes 73736 | tf_op jit(solution)/shard_map/ppermute | solution.py:659
  10.6 3.1 %collective-permute-start.2 = (f32[96,128]{1,0:T(8,128)S(1)}, f32[96,128]{1,0:T(8,128)S(1)}, u32[]{:S(2)}, u32[]{:S(2)}) collective-permute-start(f32[96,128]{1,0:T(8,128)S(1)} %get-tuple-element.48), channel_id=1, source_target_pairs={{0,4},{4,0},{8,12},{12,8},{1,5},{5,1},{9,13},{13,9},{2,6},{6,2},{1... | collective-permute-start | bytes 147464 | tf_op jit(solution)/shard_map/ppermute | solution.py:674
  10.7 3.6 %collective-permute-start.3 = (f32[96,128]{1,0:T(8,128)S(1)}, f32[96,128]{1,0:T(8,128)S(1)}, u32[]{:S(2)}, u32[]{:S(2)}) collective-permute-start(f32[96,128]{1,0:T(8,128)S(1)} %get-tuple-element.49), channel_id=1, source_target_pairs={{0,12},{4,8},{8,4},{12,0},{1,13},{5,9},{9,5},{13,1},{2,14},{6,10},... | collective-permute-start | bytes 147464 | tf_op jit(solution)/shard_map/ppermute | solution.py:675

commit v9 on v8

--- a/solution.py
+++ b/solution.py
@@ -58,14 +58,8 @@
     return jnp.where(jnp.abs(distance) <= FILT, value, F32(0.0))
 
 
-def halves(x):
-    high = x.astype(jnp.bfloat16)
-    return high, (x - high.astype(F32)).astype(jnp.bfloat16)
-
-
-def dot3(a, b):
-    terms = [jnp.dot(x, y, preferred_element_type=F32) for x, y in ((a[0], b[1]), (a[1], b[0]), (a[0], b[0]))]
-    return terms[0] + terms[1] + terms[2]
+def exact_dot(a, b):
+    return jnp.dot(a, b, precision=lax.Precision.HIGHEST, preferred_element_type=F32)
 
 
 def iota(shape, dim):
@@ -377,7 +371,7 @@
 
 
 def solve_kernel(e_ref, h_ref, f_ref, lab_ref, den_ref, table_ref,
-                 lo_ref, hi_ref, grad_ref, e2_ref, h2_ref, across_high, across_low, along_ref, around_ref, near_ref):
+                 lo_ref, hi_ref, grad_ref, e2_ref, h2_ref, across_ref, along_ref, around_ref, near_ref):
     n, m = lab_ref.shape
     nz = e_ref.shape[1]
     ratio = ratio_of(lab_ref[...], den_ref[...], [table_ref[k : k + 1] for k in range(NMAT)])
@@ -396,8 +390,8 @@
         for z in range(nz):
             e2_ref[c, z] = e2[c][z]
             h2_ref[c, z] = h2[c][z]
-    wide = across_high.shape[0]
-    across_high[...], across_low[...] = halves(tap(cyclic(iota((wide, m), 0) - iota((wide, m), 1), wide)))
+    wide = across_ref.shape[0]
+    across_ref[...] = tap(cyclic(iota((wide, m), 0) - iota((wide, m), 1), wide))
     around_ref[...] = tap(iota((n, n), 0) - iota((n, n), 1))
     k, r = iota(along_ref.shape, 1), iota(along_ref.shape, 0)
     same = (k < FILT) == (r < FILT)
@@ -518,7 +512,7 @@
     return jnp.where(d > count // 2, d - count, jnp.where(d < -(count // 2), d + count, d))
 
 
-def patch_kernel(cols_ref, seam_ref, e2_ref, h2_ref, grad_ref, across_high, across_low, around_ref,
+def patch_kernel(cols_ref, seam_ref, e2_ref, h2_ref, grad_ref, across_ref, around_ref,
                  e_hbm, h_hbm, out_hbm, e_rows, h_rows, inner_ref,
                  e_ref, h_ref, turned_ref, sems):
     n, m = grad_ref.shape
@@ -545,8 +539,8 @@
     turned_ref[24:128] = jnp.zeros((104, n), F32)
     patch(turned_ref[...].T, h2_ref, h_ref, h_hbm, h_rows)
     grad_ext = jnp.concatenate(extended(grad_ref[...], columns), axis=1)
-    part = dot3(halves(grad_ext), (across_high[...], across_low[...]))
-    inner_ref[...] = dot3(halves(around_ref[...]), halves(part))
+    part = exact_dot(grad_ext, across_ref[...])
+    inner_ref[...] = exact_dot(around_ref[...], part)
     rows = pl.ds(EDGE, n - 2 * EDGE)
     copies.append(pltpu.make_async_copy(inner_ref.at[rows], out_hbm.at[rows], sems.at[len(copies)]))
     copies[-1].start()
@@ -554,7 +548,7 @@
         copy.wait()
 
 
-def x_kernel(ra_ref, rb_ref, lo_ref, hi_ref, e_rows, h_rows, inner_ref, across_high, across_low, along_ref, near_ref,
+def x_kernel(ra_ref, rb_ref, lo_ref, hi_ref, e_rows, h_rows, inner_ref, across_ref, along_ref, near_ref,
              e_in, h_in, out_in, e_hbm, h_hbm, out_hbm, ends_ref, out_ref, sems):
     n, m = inner_ref.shape
     wide = lo_ref.shape[1]
@@ -573,8 +567,8 @@
     left = unfold(jnp.where(first_even, rb_ref[...], ra_ref[...]))
     a, b = seam_inputs(left, hi_ref[...], lo_ref[...], right)
     raw = jnp.concatenate([left[0:FILT], right[0:FILT]], axis=0)
-    part = dot3(halves(raw), (across_high[...], across_low[...]))
-    far = dot3(halves(along_ref[...]), halves(part))
+    part = exact_dot(raw, across_ref[...])
+    far = exact_dot(along_ref[...], part)
     d = seam(-1.0, a, b, lambda f: pltpu.roll(f, wide - 1, 1), lambda f: pltpu.roll(f, 1, 1))
     gb0, gb1, ga = d["gb0"], d["gb1"], d["ga"]
     top = iota((8, wide), 0)
@@ -658,10 +652,9 @@
     left = lax.ppermute(up, "gy", [(i, (i + 1) % gy) for i in range(gy)])
     right = lax.ppermute(down, "gy", [(i, (i - 1) % gy) for i in range(gy)])
     wide = m + 128
-    bands = jax.ShapeDtypeStruct((wide, m), jnp.bfloat16)
-    xlo, xhi, grad, e2, h2, across_high, across_low, along, around, near = call(
+    xlo, xhi, grad, e2, h2, across_ref, along, around, near = call(
         solve_kernel,
-        [(LO_ROWS, m), (HI_ROWS, m), (n, m), block, block, bands, bands, (2 * FILT, 2 * FILT), (n, n), (6, EDGE, m)],
+        [(LO_ROWS, m), (HI_ROWS, m), (n, m), block, block, (wide, m), (2 * FILT, 2 * FILT), (n, n), (6, EDGE, m)],
         fetched,
     )
     message = (2 * LO_ROWS + 16, 128)
@@ -677,7 +670,7 @@
     electric, magnetic, filtered, e_rows, h_rows, inner = call(
         patch_kernel,
         [block, block, (n, m), ends, ends, (n, m)],
-        [cols, seams, e2, h2, grad, across_high, across_low, around],
+        [cols, seams, e2, h2, grad, across_ref, around],
         [block, block, (128, n)],
         sems=13,
         far_out=(0, 1, 2),
@@ -686,13 +679,13 @@
         call(
             x_kernel,
             [block, block, (n, m)],
-            [got_a, got_b, lo_ext, hi_ext, e_rows, h_rows, inner, across_high, across_low, along, near]
+            [got_a, got_b, lo_ext, hi_ext, e_rows, h_rows, inner, across_ref, along, near]
             + [electric, magnetic, filtered],
             [(2, 2, 3, nz, 8, m), (2, EDGE, m)],
-            (11, 12, 13),
+            (10, 11, 12),
             6,
             (0, 1, 2),
-            {11: 0, 12: 1, 13: 2},
+            {10: 0, 11: 1, 12: 2},
         )
     )
 

time: 15.6 us -> 15.7 us (level)
  Pallas kernels: 6.96 us -> 7.12 us
    ppermute x1, waiting for transfers between devices: 0.52 us -> 0.32 us  [body(): got_b = lax.ppermute(xb, 'gx', swap_pairs(gx, 1))]
    pallas_call x5, Pallas kernels: 6.96 us -> 7.12 us  [call(): pl.pallas_call(kernel, out_shape=[s if hasattr(s, 'dtype') else jax.Shape...]
  transfers between devices with their start and end apart: 4 -> 4, of which waited for: 3 -> 3; matrix products, arithmetic and copies ran while one was open for 0% -> 0% of each run, Pallas kernels for 19% -> 20%
where the time goes in v9:
time: 15.7 us; the launch traced here: 15.5 us
  Pallas kernels  7.12 us (45%)
  starting transfers between devices  6.85 us (44%)
  waiting for transfers between devices  0.85 us (5%)
  between operations  0.68 us (4%)
    pallas_call x5, Pallas kernels, call(): pl.pallas_call(kernel, out_shape=[s if hasattr(s, 'dtype') else jax.Shape...  7.12 us
    ppermute x1, starting transfers between devices, body(): left = lax.ppermute(up, 'gy', [(i, (i + 1) % gy) for i in range(gy)])  3.08 us
    ppermute x1, starting transfers between devices, body(): right = lax.ppermute(down, 'gy', [(i, (i - 1) % gy) for i in range(gy)])  2.09 us
    ppermute x1, starting transfers between devices, body(): got_b = lax.ppermute(xb, 'gx', swap_pairs(gx, 1))  1.61 us
    ppermute x1, waiting for transfers between devices, body(): left = lax.ppermute(up, 'gy', [(i, (i + 1) % gy) for i in range(gy)])  0.37 us
    ppermute x1, waiting for transfers between devices, body(): got_b = lax.ppermute(xb, 'gx', swap_pairs(gx, 1))  0.32 us
  transfers between devices with their start and end apart: 4, of which 3 were waited for; matrix products, arithmetic and copies ran while one was open for 0% of the time, Pallas kernels for 20%

profile of v9, /device:TPU:0, one launch (start us, length us, event | category | flops | bytes accessed | tf_op | source)
XLA Modules:
  0.0 15.5 jit_solution(6760705124403792178)
XLA Ops:
  0.6 2.4 %shard_map.85 = (f32[48,128]{1,0:T(8,128)S(1)}, f32[48,128]{1,0:T(8,128)S(1)}, f32[40,128]{1,0:T(8,128)S(1)}, f32[32,128]{1,0:T(8,128)S(1)}, f32[3,2,128,256]{3,...) custom-call(f32[3,2,128,256]{3,2,1,0:T(8,128)} %e_hbm.1, ...), custom_call_target="tpu_custom_call" | custom-call | tf_op jit(solution)/shard_map/pallas_call | solution.py:626
  3.0 3.1 %collective-permute-start = (f32[48,128]{1,0:T(8,128)S(1)}, f32[48,128]{1,0:T(8,128)S(1)}, u32[]{:S(2)}, u32[]{:S(2)}) collective-permute-start(f32[48,128]{1,0:T(8,128)S(1)} %get-tuple-element.34), channel_id=1, source_target_pairs={{0,1},{1,2},{2,3},{3,0},{4,5},{5,6},{6,7},{7,4},{8,9},{9,10},{10,1... | collective-permute-start | bytes 73736 | tf_op jit(solution)/shard_map/ppermute | solution.py:652
  6.1 2.1 %collective-permute-start.1 = (f32[48,128]{1,0:T(8,128)S(1)}, f32[48,128]{1,0:T(8,128)S(1)}, u32[]{:S(2)}, u32[]{:S(2)}) collective-permute-start(f32[48,128]{1,0:T(8,128)S(1)} %get-tuple-element.35), channel_id=1, source_target_pairs={{0,3},{1,0},{2,1},{3,2},{4,7},{5,4},{6,5},{7,6},{8,11},{9,8},{10,9... | collective-permute-start | bytes 73736 | tf_op jit(solution)/shard_map/ppermute | solution.py:653
  8.2 1.5 %shard_map.86 = (f32[40,256]{1,0:T(8,128)S(1)}, f32[32,256]{1,0:T(8,128)S(1)}, f32[128,256]{1,0:T(8,128)S(1)}, f32[3,2,128,256]{3,2,1,0:T(8,128)S(1)}, f32[3,2,1...) custom-call(f32[3,2,128,256]{3,2,1,0:T(8,128)S(1)} %get-tuple-elemen, ...), custom_call_target="tpu_custom_call" | custom-call | tf_op jit(solution)/shard_map/pallas_call | solution.py:626
  9.6 0.4 %collective-permute-done.left_ref = f32[48,128]{1,0:T(8,128)S(1)} collective-permute-done((f32[48,128]{1,0:T(8,128)S(1)}, f32[48,128]{1,0:T(8,128)S(1)}, u32[]{:S(2)}, u32[]{:S(2)}) %collective-permute-start) | collective-permute-done | bytes 24608 | tf_op jit(solution)/shard_map/ppermute | solution.py:652
  10.0 0.2 collective-permute-done.1.right_ref
  10.2 0.4 %shard_map.87 = (f32[96,128]{1,0:T(8,128)S(1)}, f32[96,128]{1,0:T(8,128)S(1)}, f32[40,384]{1,0:T(8,128)S(1)}, f32[32,384]{1,0:T(8,128)S(1)}, f32[128,128]{1,0:T(8,128)S(1)}, /*index=5*/f32[15,8,128]{2,1,0:T(8,128)S(1)}) custom-call(f32[48,128]{1,0:T(8,128)S(1)} %collective-permute-done.left_ref, f32[48,128]{1,0:T(8,128)S(1)} %collective-permute-done.1.right_ref, ...), custom_call_target="tpu_custom_call" | custom-call | tf_op jit(solution)/shard_map/pallas_call | solution.py:626
  10.6 0.1 collective-permute-start.2
  10.7 1.6 %collective-permute-start.3 = (f32[96,128]{1,0:T(8,128)S(1)}, f32[96,128]{1,0:T(8,128)S(1)}, u32[]{:S(2)}, u32[]{:S(2)}) collective-permute-start(f32[96,128]{1,0:T(8,128)S(1)} %get-tuple-element.48), channel_id=1, source_target_pairs={{0,12},{4,8},{8,4},{12,0},{1,13},{5,9},{9,5},{13,1},{2,14},{6,10},... | collective-permute-start | bytes 147464 | tf_op jit(solution)/shard_map/ppermute | solution.py:668
  12.3 1.6 %shard_map.88 = (f32[3,2,128,256]{3,2,1,0:T(8,128)}, f32[3,2,128,256]{3,2,1,0:T(8,128)}, f32[128,256]{1,0:T(8,128)}, f32[3,2,16,256]{3,2,1,0:T(8,128)S(1)}, f32[...) custom-call(f32[128,128]{1,0:T(8,128)S(1)} %get-tuple-element.51.cols_ref, ...), custom_call_target="tpu_custom_call" | custom-call | tf_op jit(solution)/shard_map/pallas_call | solution.py:626
  13.9 0.0 collective-permute-done.2.ra_ref
  13.9 0.3 %collective-permute-done.3.rb_ref = f32[96,128]{1,0:T(8,128)S(1)} collective-permute-done((f32[96,128]{1,0:T(8,128)S(1)}, f32[96,128]{1,0:T(8,128)S(1)}, u32[]{:S(2)}, u32[]{:S(2)}) %collective-permute-start.3) | collective-permute-done | bytes 49184 | tf_op jit(solution)/shard_map/ppermute | solution.py:668
  14.3 1.2 %shard_map.89 = (f32[3,2,128,256]{3,2,1,0:T(8,128)}, f32[3,2,128,256]{3,2,1,0:T(8,128)}, f32[128,256]{1,0:T(8,128)}) custom-call(f32[96,128]{1,0:T(8,128)S(1)} %collective-permute-done.2.ra_ref, f32[96,128]{1,0:T(8,128)S(1)} %collective-permute-done.3.rb_ref, ...), custom_call_target="tpu_custom_call", output_to_operand_aliasing={{0}: (10, {}), {1}: (11, {}), {2}: (12, {})} | custom-call | tf_op jit(solution)/shard_map/pallas_call | solution.py:626
Async XLA Ops:
  3.0 7.0 %collective-permute-start = (f32[48,128]{1,0:T(8,128)S(1)}, f32[48,128]{1,0:T(8,128)S(1)}, u32[]{:S(2)}, u32[]{:S(2)}) collective-permute-start(f32[48,128]{1,0:T(8,128)S(1)} %get-tuple-element.34), channel_id=1, source_target_pairs={{0,1},{1,2},{2,3},{3,0},{4,5},{5,6},{6,7},{7,4},{8,9},{9,10},{10,1... | collective-permute-start | bytes 73736 | tf_op jit(solution)/shard_map/ppermute | solution.py:652
  6.1 4.1 %collective-permute-start.1 = (f32[48,128]{1,0:T(8,128)S(1)}, f32[48,128]{1,0:T(8,128)S(1)}, u32[]{:S(2)}, u32[]{:S(2)}) collective-permute-start(f32[48,128]{1,0:T(8,128)S(1)} %get-tuple-element.35), channel_id=1, source_target_pairs={{0,3},{1,0},{2,1},{3,2},{4,7},{5,4},{6,5},{7,6},{8,11},{9,8},{10,9... | collective-permute-start | bytes 73736 | tf_op jit(solution)/shard_map/ppermute | solution.py:653
  10.6 3.3 %collective-permute-start.2 = (f32[96,128]{1,0:T(8,128)S(1)}, f32[96,128]{1,0:T(8,128)S(1)}, u32[]{:S(2)}, u32[]{:S(2)}) collective-permute-start(f32[96,128]{1,0:T(8,128)S(1)} %get-tuple-element.47), channel_id=1, source_target_pairs={{0,4},{4,0},{8,12},{12,8},{1,5},{5,1},{9,13},{13,9},{2,6},{6,2},{1... | collective-permute-start | bytes 147464 | tf_op jit(solution)/shard_map/ppermute | solution.py:667
  10.7 3.6 %collective-permute-start.3 = (f32[96,128]{1,0:T(8,128)S(1)}, f32[96,128]{1,0:T(8,128)S(1)}, u32[]{:S(2)}, u32[]{:S(2)}) collective-permute-start(f32[96,128]{1,0:T(8,128)S(1)} %get-tuple-element.48), channel_id=1, source_target_pairs={{0,12},{4,8},{8,4},{12,0},{1,13},{5,9},{9,5},{13,1},{2,14},{6,10},... | collective-permute-start | bytes 147464 | tf_op jit(solution)/shard_map/ppermute | solution.py:668

commit v10 on v9

--- a/solution.py
+++ b/solution.py
@@ -570,6 +570,23 @@
     part = exact_dot(raw, across_ref[...])
     far = exact_dot(along_ref[...], part)
     d = seam(-1.0, a, b, lambda f: pltpu.roll(f, wide - 1, 1), lambda f: pltpu.roll(f, 1, 1))
+    copies = []
+    sub = iota((8, m), 0)
+    magnetic = seam_magnetic(-1.0, d["v"], lambda f: pltpu.roll(f, wide - 1, 1))
+    for f, (field, rows, dst) in enumerate(((d["e"], e_rows, e_hbm), (magnetic, h_rows, h_hbm))):
+        for c, name in enumerate(("n", "t", "z")):
+            before, end, begin, after = (value[:, 0:m] for value in field[name])
+            for z in range(2):
+                ends_ref[0, f, c, z] = rows[c, z, 0:8] + jnp.where(
+                    sub == 0, begin[z : z + 1], jnp.where(sub == 1, after[z : z + 1], 0.0)
+                )
+                ends_ref[1, f, c, z] = rows[c, z, 8:16] + jnp.where(
+                    sub == 6, before[2 + z : 3 + z], jnp.where(sub == 7, end[2 + z : 3 + z], 0.0)
+                )
+        for side, at in ((0, 0), (1, n - 8)):
+            dst_rows = dst.at[:, :, pl.ds(at, 8)]
+            copies.append(pltpu.make_async_copy(ends_ref.at[side, f], dst_rows, sems.at[len(copies)]))
+            copies[-1].start()
     gb0, gb1, ga = d["gb0"], d["gb1"], d["ga"]
     top = iota((8, wide), 0)
     change = jnp.zeros((8, wide), F32)
@@ -586,26 +603,9 @@
         out_ref[side] = rows
     out_ref[0, 0:FILT] += far[0:FILT]
     out_ref[1, EDGE - FILT : EDGE] += far[FILT : 2 * FILT]
-    copies = []
     for side, at in ((0, 0), (1, n - EDGE)):
-        copies.append(pltpu.make_async_copy(out_ref.at[side], out_hbm.at[pl.ds(at, EDGE)], sems.at[side]))
+        copies.append(pltpu.make_async_copy(out_ref.at[side], out_hbm.at[pl.ds(at, EDGE)], sems.at[len(copies)]))
         copies[-1].start()
-    sub = iota((8, m), 0)
-    magnetic = seam_magnetic(-1.0, d["v"], lambda f: pltpu.roll(f, wide - 1, 1))
-    for f, (field, rows, dst) in enumerate(((d["e"], e_rows, e_hbm), (magnetic, h_rows, h_hbm))):
-        for c, name in enumerate(("n", "t", "z")):
-            before, end, begin, after = (value[:, 0:m] for value in field[name])
-            for z in range(2):
-                ends_ref[0, f, c, z] = rows[c, z, 0:8] + jnp.where(
-                    sub == 0, begin[z : z + 1], jnp.where(sub == 1, after[z : z + 1], 0.0)
-                )
-                ends_ref[1, f, c, z] = rows[c, z, 8:16] + jnp.where(
-                    sub == 6, before[2 + z : 3 + z], jnp.where(sub == 7, end[2 + z : 3 + z], 0.0)
-                )
-        for side, at in ((0, 0), (1, n - 8)):
-            dst_rows = dst.at[:, :, pl.ds(at, 8)]
-            copies.append(pltpu.make_async_copy(ends_ref.at[side, f], dst_rows, sems.at[len(copies)]))
-            copies[-1].start()
     for copy in copies:
         copy.wait()
 

time: 15.7 us -> 15.6 us (level)
  no operation moved by 1% of the time
where the time goes in v10:
time: 15.6 us; the launch traced here: 15.5 us
  Pallas kernels  7.07 us (45%)
  starting transfers between devices  6.85 us (44%)
  waiting for transfers between devices  0.85 us (5%)
  between operations  0.68 us (4%)
    pallas_call x5, Pallas kernels, call(): pl.pallas_call(kernel, out_shape=[s if hasattr(s, 'dtype') else jax.Shape...  7.07 us
    ppermute x1, starting transfers between devices, body(): left = lax.ppermute(up, 'gy', [(i, (i + 1) % gy) for i in range(gy)])  3.08 us
    ppermute x1, starting transfers between devices, body(): right = lax.ppermute(down, 'gy', [(i, (i - 1) % gy) for i in range(gy)])  2.09 us
    ppermute x1, starting transfers between devices, body(): got_b = lax.ppermute(xb, 'gx', swap_pairs(gx, 1))  1.61 us
    ppermute x1, waiting for transfers between devices, body(): left = lax.ppermute(up, 'gy', [(i, (i + 1) % gy) for i in range(gy)])  0.37 us
    ppermute x1, waiting for transfers between devices, body(): got_b = lax.ppermute(xb, 'gx', swap_pairs(gx, 1))  0.32 us
  transfers between devices with their start and end apart: 4, of which 3 were waited for; matrix products, arithmetic and copies ran while one was open for 0% of the time, Pallas kernels for 20%

profile of v10, /device:TPU:0, one launch (start us, length us, event | category | flops | bytes accessed | tf_op | source)
XLA Modules:
  0.0 15.5 jit_solution(18031626868156366460)
XLA Ops:
  0.6 2.4 %shard_map.85 = (f32[48,128]{1,0:T(8,128)S(1)}, f32[48,128]{1,0:T(8,128)S(1)}, f32[40,128]{1,0:T(8,128)S(1)}, f32[32,128]{1,0:T(8,128)S(1)}, f32[3,2,128,256]{3,...) custom-call(f32[3,2,128,256]{3,2,1,0:T(8,128)} %e_hbm.1, ...), custom_call_target="tpu_custom_call" | custom-call | tf_op jit(solution)/shard_map/pallas_call | solution.py:626
  3.0 3.1 %collective-permute-start = (f32[48,128]{1,0:T(8,128)S(1)}, f32[48,128]{1,0:T(8,128)S(1)}, u32[]{:S(2)}, u32[]{:S(2)}) collective-permute-start(f32[48,128]{1,0:T(8,128)S(1)} %get-tuple-element.34), channel_id=1, source_target_pairs={{0,1},{1,2},{2,3},{3,0},{4,5},{5,6},{6,7},{7,4},{8,9},{9,10},{10,1... | collective-permute-start | bytes 73736 | tf_op jit(solution)/shard_map/ppermute | solution.py:652
  6.1 2.1 %collective-permute-start.1 = (f32[48,128]{1,0:T(8,128)S(1)}, f32[48,128]{1,0:T(8,128)S(1)}, u32[]{:S(2)}, u32[]{:S(2)}) collective-permute-start(f32[48,128]{1,0:T(8,128)S(1)} %get-tuple-element.35), channel_id=1, source_target_pairs={{0,3},{1,0},{2,1},{3,2},{4,7},{5,4},{6,5},{7,6},{8,11},{9,8},{10,9... | collective-permute-start | bytes 73736 | tf_op jit(solution)/shard_map/ppermute | solution.py:653
  8.2 1.5 %shard_map.86 = (f32[40,256]{1,0:T(8,128)S(1)}, f32[32,256]{1,0:T(8,128)S(1)}, f32[128,256]{1,0:T(8,128)S(1)}, f32[3,2,128,256]{3,2,1,0:T(8,128)S(1)}, f32[3,2,1...) custom-call(f32[3,2,128,256]{3,2,1,0:T(8,128)S(1)} %get-tuple-elemen, ...), custom_call_target="tpu_custom_call" | custom-call | tf_op jit(solution)/shard_map/pallas_call | solution.py:626
  9.6 0.4 %collective-permute-done.left_ref = f32[48,128]{1,0:T(8,128)S(1)} collective-permute-done((f32[48,128]{1,0:T(8,128)S(1)}, f32[48,128]{1,0:T(8,128)S(1)}, u32[]{:S(2)}, u32[]{:S(2)}) %collective-permute-start) | collective-permute-done | bytes 24608 | tf_op jit(solution)/shard_map/ppermute | solution.py:652
  10.0 0.2 collective-permute-done.1.right_ref
  10.2 0.4 %shard_map.87 = (f32[96,128]{1,0:T(8,128)S(1)}, f32[96,128]{1,0:T(8,128)S(1)}, f32[40,384]{1,0:T(8,128)S(1)}, f32[32,384]{1,0:T(8,128)S(1)}, f32[128,128]{1,0:T(8,128)S(1)}, /*index=5*/f32[15,8,128]{2,1,0:T(8,128)S(1)}) custom-call(f32[48,128]{1,0:T(8,128)S(1)} %collective-permute-done.left_ref, f32[48,128]{1,0:T(8,128)S(1)} %collective-permute-done.1.right_ref, ...), custom_call_target="tpu_custom_call" | custom-call | tf_op jit(solution)/shard_map/pallas_call | solution.py:626
  10.6 0.1 collective-permute-start.2
  10.7 1.6 %collective-permute-start.3 = (f32[96,128]{1,0:T(8,128)S(1)}, f32[96,128]{1,0:T(8,128)S(1)}, u32[]{:S(2)}, u32[]{:S(2)}) collective-permute-start(f32[96,128]{1,0:T(8,128)S(1)} %get-tuple-element.48), channel_id=1, source_target_pairs={{0,12},{4,8},{8,4},{12,0},{1,13},{5,9},{9,5},{13,1},{2,14},{6,10},... | collective-permute-start | bytes 147464 | tf_op jit(solution)/shard_map/ppermute | solution.py:668
  12.3 1.6 %shard_map.88 = (f32[3,2,128,256]{3,2,1,0:T(8,128)}, f32[3,2,128,256]{3,2,1,0:T(8,128)}, f32[128,256]{1,0:T(8,128)}, f32[3,2,16,256]{3,2,1,0:T(8,128)S(1)}, f32[...) custom-call(f32[128,128]{1,0:T(8,128)S(1)} %get-tuple-element.51.cols_ref, ...), custom_call_target="tpu_custom_call" | custom-call | tf_op jit(solution)/shard_map/pallas_call | solution.py:626
  13.9 0.0 collective-permute-done.2.ra_ref
  13.9 0.3 %collective-permute-done.3.rb_ref = f32[96,128]{1,0:T(8,128)S(1)} collective-permute-done((f32[96,128]{1,0:T(8,128)S(1)}, f32[96,128]{1,0:T(8,128)S(1)}, u32[]{:S(2)}, u32[]{:S(2)}) %collective-permute-start.3) | collective-permute-done | bytes 49184 | tf_op jit(solution)/shard_map/ppermute | solution.py:668
  14.3 1.2 %shard_map.89 = (f32[3,2,128,256]{3,2,1,0:T(8,128)}, f32[3,2,128,256]{3,2,1,0:T(8,128)}, f32[128,256]{1,0:T(8,128)}) custom-call(f32[96,128]{1,0:T(8,128)S(1)} %collective-permute-done.2.ra_ref, f32[96,128]{1,0:T(8,128)S(1)} %collective-permute-done.3.rb_ref, ...), custom_call_target="tpu_custom_call", output_to_operand_aliasing={{0}: (10, {}), {1}: (11, {}), {2}: (12, {})} | custom-call | tf_op jit(solution)/shard_map/pallas_call | solution.py:626
Async XLA Ops:
  3.0 7.0 %collective-permute-start = (f32[48,128]{1,0:T(8,128)S(1)}, f32[48,128]{1,0:T(8,128)S(1)}, u32[]{:S(2)}, u32[]{:S(2)}) collective-permute-start(f32[48,128]{1,0:T(8,128)S(1)} %get-tuple-element.34), channel_id=1, source_target_pairs={{0,1},{1,2},{2,3},{3,0},{4,5},{5,6},{6,7},{7,4},{8,9},{9,10},{10,1... | collective-permute-start | bytes 73736 | tf_op jit(solution)/shard_map/ppermute | solution.py:652
  6.1 4.1 %collective-permute-start.1 = (f32[48,128]{1,0:T(8,128)S(1)}, f32[48,128]{1,0:T(8,128)S(1)}, u32[]{:S(2)}, u32[]{:S(2)}) collective-permute-start(f32[48,128]{1,0:T(8,128)S(1)} %get-tuple-element.35), channel_id=1, source_target_pairs={{0,3},{1,0},{2,1},{3,2},{4,7},{5,4},{6,5},{7,6},{8,11},{9,8},{10,9... | collective-permute-start | bytes 73736 | tf_op jit(solution)/shard_map/ppermute | solution.py:653
  10.6 3.3 %collective-permute-start.2 = (f32[96,128]{1,0:T(8,128)S(1)}, f32[96,128]{1,0:T(8,128)S(1)}, u32[]{:S(2)}, u32[]{:S(2)}) collective-permute-start(f32[96,128]{1,0:T(8,128)S(1)} %get-tuple-element.47), channel_id=1, source_target_pairs={{0,4},{4,0},{8,12},{12,8},{1,5},{5,1},{9,13},{13,9},{2,6},{6,2},{1... | collective-permute-start | bytes 147464 | tf_op jit(solution)/shard_map/ppermute | solution.py:667
  10.7 3.6 %collective-permute-start.3 = (f32[96,128]{1,0:T(8,128)S(1)}, f32[96,128]{1,0:T(8,128)S(1)}, u32[]{:S(2)}, u32[]{:S(2)}) collective-permute-start(f32[96,128]{1,0:T(8,128)S(1)} %get-tuple-element.48), channel_id=1, source_target_pairs={{0,12},{4,8},{8,4},{12,0},{1,13},{5,9},{9,5},{13,1},{2,14},{6,10},... | collective-permute-start | bytes 147464 | tf_op jit(solution)/shard_map/ppermute | solution.py:668

commit v11 on v10

--- a/solution.py
+++ b/solution.py
@@ -56,6 +56,17 @@
     far = distance.astype(F32)
     value = jnp.exp(-far * far / (2.0 * spread * spread)) / norm
     return jnp.where(jnp.abs(distance) <= FILT, value, F32(0.0))
+
+
+def thirds(x):
+    high = x.astype(jnp.bfloat16)
+    rest = x - high.astype(F32)
+    middle = rest.astype(jnp.bfloat16)
+    return high, middle, (rest - middle.astype(F32)).astype(jnp.bfloat16)
+
+
+def narrow_dot(a, b):
+    return jnp.dot(a, b, preferred_element_type=F32)
 
 
 def exact_dot(a, b):
@@ -285,7 +296,7 @@
 
 
 def place(pack, values, base, count=3):
-    lane = iota(pack.shape, 1)
+    lane = iota((1, 128), 1)
     return jnp.where((lane >= base) & (lane < base + count), pltpu.roll(values, base + 1, 1), pack)
 
 
@@ -371,7 +382,7 @@
 
 
 def solve_kernel(e_ref, h_ref, f_ref, lab_ref, den_ref, table_ref,
-                 lo_ref, hi_ref, grad_ref, e2_ref, h2_ref, across_ref, along_ref, around_ref, near_ref):
+                 lo_ref, hi_ref, grad_ref, e2_ref, h2_ref, across_ref, across_thirds, along_ref, around_ref, near_ref):
     n, m = lab_ref.shape
     nz = e_ref.shape[1]
     ratio = ratio_of(lab_ref[...], den_ref[...], [table_ref[k : k + 1] for k in range(NMAT)])
@@ -391,11 +402,15 @@
             e2_ref[c, z] = e2[c][z]
             h2_ref[c, z] = h2[c][z]
     wide = across_ref.shape[0]
-    across_ref[...] = tap(cyclic(iota((wide, m), 0) - iota((wide, m), 1), wide))
+    across = tap(cyclic(iota((wide, m), 0) - iota((wide, m), 1), wide))
+    across_ref[...] = across
+    for k, third in enumerate(thirds(across)):
+        across_thirds[k] = third
     around_ref[...] = tap(iota((n, n), 0) - iota((n, n), 1))
-    k, r = iota(along_ref.shape, 1), iota(along_ref.shape, 0)
+    k, r = iota((2 * FILT, 2 * FILT), 1), iota((2 * FILT, 2 * FILT), 0)
     same = (k < FILT) == (r < FILT)
-    along_ref[...] = jnp.where(same, tap(k - r + jnp.where(r < FILT, -FILT, FILT)), 0.0)
+    high, middle, low = thirds(jnp.where(same, tap(k - r + jnp.where(r < FILT, -FILT, FILT)), 0.0))
+    along_ref[...] = jnp.concatenate([high, middle, low, high, middle, high], axis=1)
     r = iota((EDGE, m), 0)
     for k in range(3):
         near_ref[k] = tap(r - (k - 1))
@@ -548,7 +563,7 @@
         copy.wait()
 
 
-def x_kernel(ra_ref, rb_ref, lo_ref, hi_ref, e_rows, h_rows, inner_ref, across_ref, along_ref, near_ref,
+def x_kernel(ra_ref, rb_ref, lo_ref, hi_ref, e_rows, h_rows, inner_ref, across_thirds, along_ref, near_ref,
              e_in, h_in, out_in, e_hbm, h_hbm, out_hbm, ends_ref, out_ref, sems):
     n, m = inner_ref.shape
     wide = lo_ref.shape[1]
@@ -567,8 +582,14 @@
     left = unfold(jnp.where(first_even, rb_ref[...], ra_ref[...]))
     a, b = seam_inputs(left, hi_ref[...], lo_ref[...], right)
     raw = jnp.concatenate([left[0:FILT], right[0:FILT]], axis=0)
-    part = exact_dot(raw, across_ref[...])
-    far = exact_dot(along_ref[...], part)
+    high, middle, low = thirds(raw)
+    one = narrow_dot(jnp.concatenate([high, middle, low], axis=0), across_thirds[0])
+    two_ = narrow_dot(jnp.concatenate([high, middle], axis=0), across_thirds[1])
+    three = narrow_dot(high, across_thirds[2])
+    k = 2 * FILT
+    part = ((one[2 * k : 3 * k] + two_[k : 2 * k] + three) + (one[k : 2 * k] + two_[0:k])) + one[0:k]
+    high, middle, low = thirds(part)
+    far = narrow_dot(along_ref[...], jnp.concatenate([low, middle, high, middle, high, high], axis=0))
     d = seam(-1.0, a, b, lambda f: pltpu.roll(f, wide - 1, 1), lambda f: pltpu.roll(f, 1, 1))
     copies = []
     sub = iota((8, m), 0)
@@ -593,16 +614,18 @@
     for k, row in enumerate((ga[0:1], gb0[0:1], gb1[0:1], ga[2:3], gb0[2:3], gb1[2:3])):
         change = jnp.where(top == k, row, change)
     taps = filter_taps()
-    moved = change[:, 0:m] * taps[0]
+    terms = [change[:, 0:m] * taps[0]]
     for k in range(1, FILT + 1):
-        moved = moved + taps[k] * (pltpu.roll(change, k, 1)[:, 0:m] + pltpu.roll(change, wide - k, 1)[:, 0:m])
+        terms.append(taps[k] * (pltpu.roll(change, k, 1)[:, 0:m] + pltpu.roll(change, wide - k, 1)[:, 0:m]))
+    while len(terms) > 1:
+        terms = [x + y for x, y in zip(terms[::2], terms[1::2])] + terms[len(terms) // 2 * 2 :]
+    moved = terms[0]
     for side, at in ((0, 0), (1, n - EDGE)):
         rows = inner_ref[at : at + EDGE]
         for k in range(3 * side, 3 * side + 3):
             rows = rows + near_ref[k] * moved[k : k + 1]
-        out_ref[side] = rows
-    out_ref[0, 0:FILT] += far[0:FILT]
-    out_ref[1, EDGE - FILT : EDGE] += far[FILT : 2 * FILT]
+        gap, here = jnp.zeros((EDGE - FILT, m), F32), far[FILT * side : FILT * side + FILT]
+        out_ref[side] = rows + jnp.concatenate([gap, here] if side else [here, gap], axis=0)
     for side, at in ((0, 0), (1, n - EDGE)):
         copies.append(pltpu.make_async_copy(out_ref.at[side], out_hbm.at[pl.ds(at, EDGE)], sems.at[len(copies)]))
         copies[-1].start()
@@ -652,9 +675,11 @@
     left = lax.ppermute(up, "gy", [(i, (i + 1) % gy) for i in range(gy)])
     right = lax.ppermute(down, "gy", [(i, (i - 1) % gy) for i in range(gy)])
     wide = m + 128
-    xlo, xhi, grad, e2, h2, across_ref, along, around, near = call(
+    bands = jax.ShapeDtypeStruct((3, wide, m), jnp.bfloat16)
+    along_bands = jax.ShapeDtypeStruct((2 * FILT, 12 * FILT), jnp.bfloat16)
+    xlo, xhi, grad, e2, h2, across_ref, across_thirds, along, around, near = call(
         solve_kernel,
-        [(LO_ROWS, m), (HI_ROWS, m), (n, m), block, block, (wide, m), (2 * FILT, 2 * FILT), (n, n), (6, EDGE, m)],
+        [(LO_ROWS, m), (HI_ROWS, m), (n, m), block, block, (wide, m), bands, along_bands, (n, n), (6, EDGE, m)],
         fetched,
     )
     message = (2 * LO_ROWS + 16, 128)
@@ -679,7 +704,7 @@
         call(
             x_kernel,
             [block, block, (n, m)],
-            [got_a, got_b, lo_ext, hi_ext, e_rows, h_rows, inner, across_ref, along, near]
+            [got_a, got_b, lo_ext, hi_ext, e_rows, h_rows, inner, across_thirds, along, near]
             + [electric, magnetic, filtered],
             [(2, 2, 3, nz, 8, m), (2, EDGE, m)],
             (10, 11, 12),

time: 15.6 us -> 15.6 us (level)
  transfers between devices with their start and end apart: 4 -> 4, of which waited for: 3 -> 3; matrix products, arithmetic and copies ran while one was open for 0% -> 0% of each run, Pallas kernels for 20% -> 21%
where the time goes in v11:
time: 15.6 us; the launch traced here: 15.4 us
  Pallas kernels  7.09 us (45%)
  starting transfers between devices  6.85 us (44%)
  waiting for transfers between devices  0.78 us (5%)
  between operations  0.68 us (4%)
    pallas_call x5, Pallas kernels, call(): pl.pallas_call(kernel, out_shape=[s if hasattr(s, 'dtype') else jax.Shape...  7.09 us
    ppermute x1, starting transfers between devices, body(): left = lax.ppermute(up, 'gy', [(i, (i + 1) % gy) for i in range(gy)])  3.08 us
    ppermute x1, starting transfers between devices, body(): right = lax.ppermute(down, 'gy', [(i, (i - 1) % gy) for i in range(gy)])  2.09 us
    ppermute x1, starting transfers between devices, body(): got_b = lax.ppermute(xb, 'gx', swap_pairs(gx, 1))  1.61 us
    ppermute x1, waiting for transfers between devices, body(): got_b = lax.ppermute(xb, 'gx', swap_pairs(gx, 1))  0.32 us
  transfers between devices with their start and end apart: 4, of which 3 were waited for; matrix products, arithmetic and copies ran while one was open for 0% of the time, Pallas kernels for 21%

profile of v11, /device:TPU:0, one launch (start us, length us, event | category | flops | bytes accessed | tf_op | source)
XLA Modules:
  0.0 15.4 jit_solution(11929685933669770802)
XLA Ops:
  0.6 2.4 %shard_map.85 = (f32[48,128]{1,0:T(8,128)S(1)}, f32[48,128]{1,0:T(8,128)S(1)}, f32[40,128]{1,0:T(8,128)S(1)}, f32[32,128]{1,0:T(8,128)S(1)}, f32[3,2,128,256]{3,...) custom-call(f32[3,2,128,256]{3,2,1,0:T(8,128)} %e_hbm.1, ...), custom_call_target="tpu_custom_call" | custom-call | tf_op jit(solution)/shard_map/pallas_call | solution.py:649
  3.0 3.1 %collective-permute-start = (f32[48,128]{1,0:T(8,128)S(1)}, f32[48,128]{1,0:T(8,128)S(1)}, u32[]{:S(2)}, u32[]{:S(2)}) collective-permute-start(f32[48,128]{1,0:T(8,128)S(1)} %get-tuple-element.35), channel_id=1, source_target_pairs={{0,1},{1,2},{2,3},{3,0},{4,5},{5,6},{6,7},{7,4},{8,9},{9,10},{10,1... | collective-permute-start | bytes 73736 | tf_op jit(solution)/shard_map/ppermute | solution.py:675
  6.1 2.1 %collective-permute-start.1 = (f32[48,128]{1,0:T(8,128)S(1)}, f32[48,128]{1,0:T(8,128)S(1)}, u32[]{:S(2)}, u32[]{:S(2)}) collective-permute-start(f32[48,128]{1,0:T(8,128)S(1)} %get-tuple-element.36), channel_id=1, source_target_pairs={{0,3},{1,0},{2,1},{3,2},{4,7},{5,4},{6,5},{7,6},{8,11},{9,8},{10,9... | collective-permute-start | bytes 73736 | tf_op jit(solution)/shard_map/ppermute | solution.py:676
  8.2 1.5 %shard_map.86 = (f32[40,256]{1,0:T(8,128)S(1)}, f32[32,256]{1,0:T(8,128)S(1)}, f32[128,256]{1,0:T(8,128)S(1)}, f32[3,2,128,256]{3,2,1,0:T(8,128)S(1)}, f32[3,2,1...) custom-call(f32[3,2,128,256]{3,2,1,0:T(8,128)S(1)} %get-tuple-elemen, ...), custom_call_target="tpu_custom_call" | custom-call | tf_op jit(solution)/shard_map/pallas_call | solution.py:649
  9.7 0.3 %collective-permute-done.left_ref = f32[48,128]{1,0:T(8,128)S(1)} collective-permute-done((f32[48,128]{1,0:T(8,128)S(1)}, f32[48,128]{1,0:T(8,128)S(1)}, u32[]{:S(2)}, u32[]{:S(2)}) %collective-permute-start) | collective-permute-done | bytes 24608 | tf_op jit(solution)/shard_map/ppermute | solution.py:675
  10.0 0.2 collective-permute-done.1.right_ref
  10.2 0.4 %shard_map.87 = (f32[96,128]{1,0:T(8,128)S(1)}, f32[96,128]{1,0:T(8,128)S(1)}, f32[40,384]{1,0:T(8,128)S(1)}, f32[32,384]{1,0:T(8,128)S(1)}, f32[128,128]{1,0:T(8,128)S(1)}, /*index=5*/f32[15,8,128]{2,1,0:T(8,128)S(1)}) custom-call(f32[48,128]{1,0:T(8,128)S(1)} %collective-permute-done.left_ref, f32[48,128]{1,0:T(8,128)S(1)} %collective-permute-done.1.right_ref, ...), custom_call_target="tpu_custom_call" | custom-call | tf_op jit(solution)/shard_map/pallas_call | solution.py:649
  10.6 0.1 collective-permute-start.2
  10.7 1.6 %collective-permute-start.3 = (f32[96,128]{1,0:T(8,128)S(1)}, f32[96,128]{1,0:T(8,128)S(1)}, u32[]{:S(2)}, u32[]{:S(2)}) collective-permute-start(f32[96,128]{1,0:T(8,128)S(1)} %get-tuple-element.49), channel_id=1, source_target_pairs={{0,12},{4,8},{8,4},{12,0},{1,13},{5,9},{9,5},{13,1},{2,14},{6,10},... | collective-permute-start | bytes 147464 | tf_op jit(solution)/shard_map/ppermute | solution.py:693
  12.3 1.6 %shard_map.88 = (f32[3,2,128,256]{3,2,1,0:T(8,128)}, f32[3,2,128,256]{3,2,1,0:T(8,128)}, f32[128,256]{1,0:T(8,128)}, f32[3,2,16,256]{3,2,1,0:T(8,128)S(1)}, f32[...) custom-call(f32[128,128]{1,0:T(8,128)S(1)} %get-tuple-element.52.cols_ref, ...), custom_call_target="tpu_custom_call" | custom-call | tf_op jit(solution)/shard_map/pallas_call | solution.py:649
  13.9 0.0 collective-permute-done.2.ra_ref
  13.9 0.3 %collective-permute-done.3.rb_ref = f32[96,128]{1,0:T(8,128)S(1)} collective-permute-done((f32[96,128]{1,0:T(8,128)S(1)}, f32[96,128]{1,0:T(8,128)S(1)}, u32[]{:S(2)}, u32[]{:S(2)}) %collective-permute-start.3) | collective-permute-done | bytes 49184 | tf_op jit(solution)/shard_map/ppermute | solution.py:693
  14.3 1.1 %shard_map.89 = (f32[3,2,128,256]{3,2,1,0:T(8,128)}, f32[3,2,128,256]{3,2,1,0:T(8,128)}, f32[128,256]{1,0:T(8,128)}) custom-call(f32[96,128]{1,0:T(8,128)S(1)} %collective-permute-done.2.ra_ref, f32[96,128]{1,0:T(8,128)S(1)} %collective-permute-done.3.rb_ref, ...), custom_call_target="tpu_custom_call", output_to_operand_aliasing={{0}: (10, {}), {1}: (11, {}), {2}: (12, {})} | custom-call | tf_op jit(solution)/shard_map/pallas_call | solution.py:649
Async XLA Ops:
  3.0 7.0 %collective-permute-start = (f32[48,128]{1,0:T(8,128)S(1)}, f32[48,128]{1,0:T(8,128)S(1)}, u32[]{:S(2)}, u32[]{:S(2)}) collective-permute-start(f32[48,128]{1,0:T(8,128)S(1)} %get-tuple-element.35), channel_id=1, source_target_pairs={{0,1},{1,2},{2,3},{3,0},{4,5},{5,6},{6,7},{7,4},{8,9},{9,10},{10,1... | collective-permute-start | bytes 73736 | tf_op jit(solution)/shard_map/ppermute | solution.py:675
  6.1 4.1 %collective-permute-start.1 = (f32[48,128]{1,0:T(8,128)S(1)}, f32[48,128]{1,0:T(8,128)S(1)}, u32[]{:S(2)}, u32[]{:S(2)}) collective-permute-start(f32[48,128]{1,0:T(8,128)S(1)} %get-tuple-element.36), channel_id=1, source_target_pairs={{0,3},{1,0},{2,1},{3,2},{4,7},{5,4},{6,5},{7,6},{8,11},{9,8},{10,9... | collective-permute-start | bytes 73736 | tf_op jit(solution)/shard_map/ppermute | solution.py:676
  10.6 3.3 %collective-permute-start.2 = (f32[96,128]{1,0:T(8,128)S(1)}, f32[96,128]{1,0:T(8,128)S(1)}, u32[]{:S(2)}, u32[]{:S(2)}) collective-permute-start(f32[96,128]{1,0:T(8,128)S(1)} %get-tuple-element.48), channel_id=1, source_target_pairs={{0,4},{4,0},{8,12},{12,8},{1,5},{5,1},{9,13},{13,9},{2,6},{6,2},{1... | collective-permute-start | bytes 147464 | tf_op jit(solution)/shard_map/ppermute | solution.py:692
  10.7 3.6 %collective-permute-start.3 = (f32[96,128]{1,0:T(8,128)S(1)}, f32[96,128]{1,0:T(8,128)S(1)}, u32[]{:S(2)}, u32[]{:S(2)}) collective-permute-start(f32[96,128]{1,0:T(8,128)S(1)} %get-tuple-element.49), channel_id=1, source_target_pairs={{0,12},{4,8},{8,4},{12,0},{1,13},{5,9},{9,5},{13,1},{2,14},{6,10},... | collective-permute-start | bytes 147464 | tf_op jit(solution)/shard_map/ppermute | solution.py:693

commit v12 on v11

--- a/solution.py
+++ b/solution.py
@@ -350,12 +350,12 @@
     h1 = magnetic(e1, h0)
     e2 = less(e1, turn(h1, ratio))
     pack = place(jnp.zeros((n, 128), F32), ratio, PACK_R)
+    copies[5].wait()
+    fwd = [folded(f_ref, 0)]
+    grad = product(e1, fwd[0])
     for k, (first, last) in enumerate(((e1, h0), (e2, h1))):
         for j, (c, z) in enumerate(sides):
             pack = place(pack, jnp.where(lane < 64, first[c][z], last[c][z]), PACK_PAIR + 8 * k + 2 * j, 2)
-    copies[5].wait()
-    fwd = [folded(f_ref, 0)]
-    grad = product(e1, fwd[0])
     for j, (c, z) in enumerate(sides):
         pack = jnp.where(lane == PACK_F0 + j, pltpu.roll(fwd[0][c][z], PACK_F0 + j, 1), pack)
     copies[6].wait()

time: 15.6 us -> 15.6 us (level)
  no operation moved by 1% of the time
where the time goes in v12:
time: 15.6 us; the launch traced here: 15.4 us
  Pallas kernels  7.11 us (46%)
  starting transfers between devices  6.85 us (44%)
  waiting for transfers between devices  0.77 us (5%)
  between operations  0.68 us (4%)
    pallas_call x5, Pallas kernels, call(): pl.pallas_call(kernel, out_shape=[s if hasattr(s, 'dtype') else jax.Shape...  7.11 us
    ppermute x1, starting transfers between devices, body(): left = lax.ppermute(up, 'gy', [(i, (i + 1) % gy) for i in range(gy)])  3.08 us
    ppermute x1, starting transfers between devices, body(): right = lax.ppermute(down, 'gy', [(i, (i - 1) % gy) for i in range(gy)])  2.09 us
    ppermute x1, starting transfers between devices, body(): got_b = lax.ppermute(xb, 'gx', swap_pairs(gx, 1))  1.61 us
    ppermute x1, waiting for transfers between devices, body(): got_b = lax.ppermute(xb, 'gx', swap_pairs(gx, 1))  0.32 us
  transfers between devices with their start and end apart: 4, of which 3 were waited for; matrix products, arithmetic and copies ran while one was open for 0% of the time, Pallas kernels for 21%

profile of v12, /device:TPU:0, one launch (start us, length us, event | category | flops | bytes accessed | tf_op | source)
XLA Modules:
  0.0 15.4 jit_solution(6580904808736430869)
XLA Ops:
  0.6 2.4 %shard_map.85 = (f32[48,128]{1,0:T(8,128)S(1)}, f32[48,128]{1,0:T(8,128)S(1)}, f32[40,128]{1,0:T(8,128)S(1)}, f32[32,128]{1,0:T(8,128)S(1)}, f32[3,2,128,256]{3,...) custom-call(f32[3,2,128,256]{3,2,1,0:T(8,128)} %e_hbm.1, ...), custom_call_target="tpu_custom_call" | custom-call | tf_op jit(solution)/shard_map/pallas_call | solution.py:649
  3.0 3.1 %collective-permute-start = (f32[48,128]{1,0:T(8,128)S(1)}, f32[48,128]{1,0:T(8,128)S(1)}, u32[]{:S(2)}, u32[]{:S(2)}) collective-permute-start(f32[48,128]{1,0:T(8,128)S(1)} %get-tuple-element.35), channel_id=1, source_target_pairs={{0,1},{1,2},{2,3},{3,0},{4,5},{5,6},{6,7},{7,4},{8,9},{9,10},{10,1... | collective-permute-start | bytes 73736 | tf_op jit(solution)/shard_map/ppermute | solution.py:675
  6.1 2.1 %collective-permute-start.1 = (f32[48,128]{1,0:T(8,128)S(1)}, f32[48,128]{1,0:T(8,128)S(1)}, u32[]{:S(2)}, u32[]{:S(2)}) collective-permute-start(f32[48,128]{1,0:T(8,128)S(1)} %get-tuple-element.36), channel_id=1, source_target_pairs={{0,3},{1,0},{2,1},{3,2},{4,7},{5,4},{6,5},{7,6},{8,11},{9,8},{10,9... | collective-permute-start | bytes 73736 | tf_op jit(solution)/shard_map/ppermute | solution.py:676
  8.2 1.5 %shard_map.86 = (f32[40,256]{1,0:T(8,128)S(1)}, f32[32,256]{1,0:T(8,128)S(1)}, f32[128,256]{1,0:T(8,128)S(1)}, f32[3,2,128,256]{3,2,1,0:T(8,128)S(1)}, f32[3,2,1...) custom-call(f32[3,2,128,256]{3,2,1,0:T(8,128)S(1)} %get-tuple-elemen, ...), custom_call_target="tpu_custom_call" | custom-call | tf_op jit(solution)/shard_map/pallas_call | solution.py:649
  9.7 0.3 %collective-permute-done.left_ref = f32[48,128]{1,0:T(8,128)S(1)} collective-permute-done((f32[48,128]{1,0:T(8,128)S(1)}, f32[48,128]{1,0:T(8,128)S(1)}, u32[]{:S(2)}, u32[]{:S(2)}) %collective-permute-start) | collective-permute-done | bytes 24608 | tf_op jit(solution)/shard_map/ppermute | solution.py:675
  10.0 0.2 collective-permute-done.1.right_ref
  10.2 0.4 %shard_map.87 = (f32[96,128]{1,0:T(8,128)S(1)}, f32[96,128]{1,0:T(8,128)S(1)}, f32[40,384]{1,0:T(8,128)S(1)}, f32[32,384]{1,0:T(8,128)S(1)}, f32[128,128]{1,0:T(8,128)S(1)}, /*index=5*/f32[15,8,128]{2,1,0:T(8,128)S(1)}) custom-call(f32[48,128]{1,0:T(8,128)S(1)} %collective-permute-done.left_ref, f32[48,128]{1,0:T(8,128)S(1)} %collective-permute-done.1.right_ref, ...), custom_call_target="tpu_custom_call" | custom-call | tf_op jit(solution)/shard_map/pallas_call | solution.py:649
  10.6 0.1 collective-permute-start.2
  10.7 1.6 %collective-permute-start.3 = (f32[96,128]{1,0:T(8,128)S(1)}, f32[96,128]{1,0:T(8,128)S(1)}, u32[]{:S(2)}, u32[]{:S(2)}) collective-permute-start(f32[96,128]{1,0:T(8,128)S(1)} %get-tuple-element.49), channel_id=1, source_target_pairs={{0,12},{4,8},{8,4},{12,0},{1,13},{5,9},{9,5},{13,1},{2,14},{6,10},... | collective-permute-start | bytes 147464 | tf_op jit(solution)/shard_map/ppermute | solution.py:693
  12.3 1.6 %shard_map.88 = (f32[3,2,128,256]{3,2,1,0:T(8,128)}, f32[3,2,128,256]{3,2,1,0:T(8,128)}, f32[128,256]{1,0:T(8,128)}, f32[3,2,16,256]{3,2,1,0:T(8,128)S(1)}, f32[...) custom-call(f32[128,128]{1,0:T(8,128)S(1)} %get-tuple-element.52.cols_ref, ...), custom_call_target="tpu_custom_call" | custom-call | tf_op jit(solution)/shard_map/pallas_call | solution.py:649
  13.9 0.0 collective-permute-done.2.ra_ref
  14.0 0.3 %collective-permute-done.3.rb_ref = f32[96,128]{1,0:T(8,128)S(1)} collective-permute-done((f32[96,128]{1,0:T(8,128)S(1)}, f32[96,128]{1,0:T(8,128)S(1)}, u32[]{:S(2)}, u32[]{:S(2)}) %collective-permute-start.3) | collective-permute-done | bytes 49184 | tf_op jit(solution)/shard_map/ppermute | solution.py:693
  14.3 1.1 %shard_map.89 = (f32[3,2,128,256]{3,2,1,0:T(8,128)}, f32[3,2,128,256]{3,2,1,0:T(8,128)}, f32[128,256]{1,0:T(8,128)}) custom-call(f32[96,128]{1,0:T(8,128)S(1)} %collective-permute-done.2.ra_ref, f32[96,128]{1,0:T(8,128)S(1)} %collective-permute-done.3.rb_ref, ...), custom_call_target="tpu_custom_call", output_to_operand_aliasing={{0}: (10, {}), {1}: (11, {}), {2}: (12, {})} | custom-call | tf_op jit(solution)/shard_map/pallas_call | solution.py:649
Async XLA Ops:
  3.0 7.0 %collective-permute-start = (f32[48,128]{1,0:T(8,128)S(1)}, f32[48,128]{1,0:T(8,128)S(1)}, u32[]{:S(2)}, u32[]{:S(2)}) collective-permute-start(f32[48,128]{1,0:T(8,128)S(1)} %get-tuple-element.35), channel_id=1, source_target_pairs={{0,1},{1,2},{2,3},{3,0},{4,5},{5,6},{6,7},{7,4},{8,9},{9,10},{10,1... | collective-permute-start | bytes 73736 | tf_op jit(solution)/shard_map/ppermute | solution.py:675
  6.1 4.1 %collective-permute-start.1 = (f32[48,128]{1,0:T(8,128)S(1)}, f32[48,128]{1,0:T(8,128)S(1)}, u32[]{:S(2)}, u32[]{:S(2)}) collective-permute-start(f32[48,128]{1,0:T(8,128)S(1)} %get-tuple-element.36), channel_id=1, source_target_pairs={{0,3},{1,0},{2,1},{3,2},{4,7},{5,4},{6,5},{7,6},{8,11},{9,8},{10,9... | collective-permute-start | bytes 73736 | tf_op jit(solution)/shard_map/ppermute | solution.py:676
  10.6 3.3 %collective-permute-start.2 = (f32[96,128]{1,0:T(8,128)S(1)}, f32[96,128]{1,0:T(8,128)S(1)}, u32[]{:S(2)}, u32[]{:S(2)}) collective-permute-start(f32[96,128]{1,0:T(8,128)S(1)} %get-tuple-element.48), channel_id=1, source_target_pairs={{0,4},{4,0},{8,12},{12,8},{1,5},{5,1},{9,13},{13,9},{2,6},{6,2},{1... | collective-permute-start | bytes 147464 | tf_op jit(solution)/shard_map/ppermute | solution.py:692
  10.7 3.6 %collective-permute-start.3 = (f32[96,128]{1,0:T(8,128)S(1)}, f32[96,128]{1,0:T(8,128)S(1)}, u32[]{:S(2)}, u32[]{:S(2)}) collective-permute-start(f32[96,128]{1,0:T(8,128)S(1)} %get-tuple-element.49), channel_id=1, source_target_pairs={{0,12},{4,8},{8,4},{12,0},{1,13},{5,9},{9,5},{13,1},{2,14},{6,10},... | collective-permute-start | bytes 147464 | tf_op jit(solution)/shard_map/ppermute | solution.py:693
